TPU v7x, 1024 devices: a whole 4x8x16 slice. The times are simulated.
1024 devices in a mesh: dp: 128 (over z, y_hi, x), tensor: 8 (over y_lo, core).
Axes of the slice: x: 4, y: 8 (y_hi: 2, y_lo: 4; y = y_hi * 4 + y_lo), z: 16, core: 2. Of those that a mesh axis runs over, the one named last changes fastest.
Arguments:
- panel: bfloat16 [131072, 3072], P(('dp', 'tensor')), may hold values from -6 to 6
- row_scale: bfloat16 [131072], P(('dp', 'tensor')), may hold values from 0.29882812 to 3
- expert_ids: int32 [131072, 4], P(('dp', 'tensor')), may hold values from 0 to 15, as said below
- weight: bfloat16 [3072, 5376], P('dp', 'tensor'), may hold values from -0.109375 to 0.109375
- up_branch: bfloat16 [49152, 5376], P('dp', 'tensor'), may hold values from -6 to 6
- cotangent: bfloat16 [49152, 5376], P('dp', 'tensor'), may hold values from -6 to 6
Outputs:
- hidden: bfloat16 [49152, 5376], P('dp', 'tensor')
- input_grad: bfloat16 [131072, 3072], P(('dp', 'tensor'))
Inputs may be any that keep to these rules, and one draw needn't show every extreme that they name: `expert_ids`: each row names 4 different experts. Among the 128 rows of one device at most 48 name expert 0, and in every draw some device has exactly 48.
All inputs are finite; a program needn't handle non-finite values.
Results may differ from a plain program's by a relative error of at most 0.017.
Values may be sent and summed in bfloat16 or wider, within the bound.
No kernel may reach another device: no remote copies, remote signals or barrier semaphores. Data moves between devices by JAX's collectives and lax.ppermute only.
A program may use at most 32 MiB of HBM per device.

v0:
```python
import jax
import jax.numpy as jnp
from jax import lax
from jax.sharding import PartitionSpec as P


def body(panel, row_scale, expert_ids, weight, up_branch, cotangent):
    group_rows = up_branch.shape[0]
    slot_count = group_rows // lax.axis_size("tensor")
    hit = jnp.any(expert_ids == 0, axis=1)
    place = jnp.cumsum(hit.astype(jnp.int32)) - 1
    slots = jnp.arange(slot_count, dtype=jnp.int32)
    select = ((place[None, :] == slots[:, None]) & hit[None, :]).astype(jnp.bfloat16)
    own_rows = jnp.dot(select, panel, preferred_element_type=jnp.float32).astype(jnp.bfloat16)
    own_scale = jnp.dot(select, row_scale[:, None], preferred_element_type=jnp.float32)[
        :, 0
    ].astype(jnp.bfloat16)
    rows, scales = (
        lax.all_gather(own_rows, "tensor", axis=0, tiled=True),
        lax.all_gather(own_scale, "tensor", axis=0, tiled=True),
    )
    scales32 = scales.astype(jnp.float32)
    gathered = lax.all_gather(weight, "dp", axis=0, tiled=True)
    product = jnp.dot(rows, gathered, preferred_element_type=jnp.float32)
    gate = product * scales32[:, None]
    sig = jax.nn.sigmoid(gate)
    upper = up_branch.astype(jnp.float32)
    hidden = (gate * sig * upper).astype(jnp.bfloat16)
    filled = scales32 > 0.0
    dgate = jnp.where(
        filled[:, None],
        cotangent.astype(jnp.float32) * upper * sig * (1.0 + gate * (1.0 - sig)),
        0.0,
    ).astype(jnp.bfloat16)
    slot_grad = lax.psum_scatter(
        jnp.dot(dgate, gathered.T, preferred_element_type=jnp.float32).astype(jnp.bfloat16),
        "tensor",
        scatter_dimension=0,
        tiled=True,
    )
    input_grad = jnp.einsum(
        "st,sd->td", select, slot_grad, preferred_element_type=jnp.float32
    ).astype(jnp.bfloat16)
    return (hidden, input_grad)


def solution(mesh):
    in_specs = (
        P(("dp", "tensor"), None),
        P(("dp", "tensor")),
        P(("dp", "tensor"), None),
        P("dp", "tensor"),
        P("dp", "tensor"),
        P("dp", "tensor"),
    )
    out_specs = (P("dp", "tensor"), P(("dp", "tensor"), None))
    return jax.shard_map(body, mesh=mesh, in_specs=in_specs, out_specs=out_specs, check_vma=False)
```

profile of v0, /device:TPU:1, one launch (start us, length us, event | category | flops | bytes accessed | tf_op | source)
XLA Modules:
  0.0 387.1 jit_solution(12598037818973892218)
XLA Ops:
  7.2 0.0 copy-start
  7.2 0.0 all-gather.3.cloned.1.call-start
  7.2 0.8 compare_reduce_fusion
  8.0 0.1 copy.9
  8.1 0.2 reduce-window.8
  8.3 0.1 add_reduce_fusion
  8.4 0.0 copy-done
  8.4 1.0 convolution_convert_fusion.2
  9.4 0.0 all-gather.3.cloned.1.call-update
  9.4 0.0 all-gather.5.cloned.1.call-start
  9.4 0.7 all-gather.5.cloned.1.call-update
  10.1 0.0 reduce-scatter.2.cloned.1.call-start
  10.2 1.3 dynamic-slice
  12.1 0.8 fusion
  12.9 0.2 dynamic-update-slice
  13.1 27.1 %all-reduce = bf16[384]{0:T(512)(128)(2,1)S(1)} all-reduce(bf16[384]{0:T(512)(128)(2,1)S(1)} %dynamic-update-slice), channel_id=1, replica_groups=mesh['dp'=128,'tensor'=8] {'tensor'}, use_global_device_ids=true, to_apply=%add | all-reduce | flops 384 | bytes 1536
  40.2 0.0 copy-start.2
  40.3 0.0 copy-start.3
  40.3 26.5 %all-gather.3.cloned.1.call-done = bf16[384,3072]{1,0:T(8,128)(2,1)} async-done(((bf16[48,3072]{1,0:T(8,128)(2,1)}), bf16[384,3072]{1,0:T(8,128)(2,1)}) %all-gather.3.cloned.1.call-update) | async-done | bytes 2359312 | tf_op jit(solution)/shard_map/all_gather | solution.py:19
  66.7 246.9 %all-gather.5.cloned.1.call-done = bf16[3072,672]{1,0:T(8,128)(2,1)} async-done(((bf16[24,672]{1,0:T(8,128)(2,1)}), bf16[3072,672]{1,0:T(8,128)(2,1)}) %all-gather.5.cloned.1.call-update) | async-done | bytes 4128784 | tf_op jit(solution)/shard_map/all_gather | solution.py:23
  313.6 0.0 copy-start.1
  313.6 6.6 %fusion.1 = (bf16[384,672]{0,1:T(8,128)(2,1)}, f32[384,672]{0,1:T(8,128)S(1)}) fusion(bf16[384,672]{0,1:T(8,128)(2,1)} %param.10, f32[384]{0:T(512)S(1)} %convert_element_type.47, bf16[384,3072]{1,0:T(8,128)(2,1)} %all-gather.3.cloned.1.call-done, bf16[3072,672]{1,0:T(8,128)(2,1)} %all-gather.5.cloned.1.call-done), kind=kOutput, calls=%fused_computation.8 | convolution fusion | flops 1587511296 | bytes 8553984 | tf_op jit(solution)/shard_map/dot_general | solution.py:24
  320.2 0.0 copy-done.2
  320.2 0.0 copy-done.3
  320.2 0.0 copy-done.1
  320.2 3.8 convolution_convert_fusion
  324.0 0.0 reduce-scatter.2.cloned.1.call-update
  324.0 54.3 %reduce-scatter.2.cloned.1.call-done = bf16[48,3072]{1,0:T(8,128)(2,1)} async-done(((bf16[384,3072]{1,0:T(8,128)(2,1)}), bf16[48,3072]{1,0:T(8,128)(2,1)}) %reduce-scatter.2.cloned.1.call-update) | async-done | bytes 294928 | tf_op jit(solution)/shard_map/reduce_scatter | solution.py:35
  378.3 2.3 convolution_convert_fusion.1
  (4 shorter events, 0.0 us)
Async XLA Ops:
  7.2 1.2 copy-start
  7.2 59.6 %all-gather.3.cloned.1.call-start = ((), (), s32[]{:S(2)}) async-start(), calls=%async_computation.1 | async-start | bytes 2654208 | tf_op jit(solution)/shard_map/all_gather | solution.py:19
  9.4 304.2 %all-gather.5.cloned.1.call-start = ((), (), s32[]{:S(2)}) async-start(), calls=%async_computation.2 | async-start | bytes 4755456 | tf_op jit(solution)/shard_map/all_gather | solution.py:23
  10.1 368.2 %reduce-scatter.2.cloned.1.call-start = ((), (), s32[]{:S(2)}) async-start(), calls=%async_computation.3 | async-start | bytes 2654208 | tf_op jit(solution)/shard_map/reduce_scatter | solution.py:35
  40.2 280.0 %copy-start.2 = (bf16[384,672]{0,1:T(8,128)(2,1)S(1)}, bf16[384,672]{0,1:T(8,128)(2,1)}, u32[]{:S(2)}) copy-start(bf16[384,672]{0,1:T(8,128)(2,1)} %param.10) | copy-start | bytes 1548292
  40.3 280.0 %copy-start.3 = (bf16[384,672]{0,1:T(8,128)(2,1)S(1)}, bf16[384,672]{0,1:T(8,128)(2,1)}, u32[]{:S(2)}) copy-start(bf16[384,672]{0,1:T(8,128)(2,1)} %param.11) | copy-start | bytes 1548292
  313.6 6.6 %copy-start.1 = (bf16[3072,672]{1,0:T(8,128)(2,1)S(1)}, bf16[3072,672]{1,0:T(8,128)(2,1)}, u32[]{:S(2)}) copy-start(bf16[3072,672]{1,0:T(8,128)(2,1)} %all-gather.5.cloned.1.call-done) | copy-start | bytes 12386308
Sparse Core Ops, SparseCore 0:
  11.2 55.4 all-gather.2
  72.5 241.0 all-gather.4
  324.1 54.1 reduce-scatter.1
where the time goes:
time: 388 us; the launch traced here: 387 us
  waiting for transfers between devices  328 us (85%)
  blocking collectives  27.1 us (7%)
  matrix products  14.4 us (4%)
  between operations  14.4 us (4%)
    all_gather x1, waiting for transfers between devices, body(): gathered = lax.all_gather(weight, 'dp', axis=0, tiled=True)  247 us
    reduce_scatter x1, waiting for transfers between devices, body(): lax.psum_scatter(jnp.dot(dgate, gathered.T, preferred_element_type=jnp.fl...  54.3 us
    unnamed x1, blocking collectives  27.1 us
    all_gather x1, waiting for transfers between devices, body(): lax.all_gather(own_rows, 'tensor', axis=0, tiled=True)  26.5 us
  transfers between devices with their start and end apart: 3, of which 3 were waited for; matrix products, arithmetic and copies ran while one was open for 1% of the time, Pallas kernels for 0%

commit v1 on v0

v1 whole, which is shorter than its diff:
```python
import jax
import jax.numpy as jnp
from jax import lax
from jax.sharding import Mesh, PartitionSpec as P

AXES = ("za", "zb", "yh", "x", "yl", "core")
SIZES = (4, 4, 2, 4, 4, 2)
GROUP = ("za", "zb", "yh", "x")
TENSOR = ("yl", "core")


def shifted(za, zb, by):
    count = za * zb
    return [(i, (i + by) % count) for i in range(count)]


def everyone(part, axes):
    count = lax.axis_size(axes)
    return lax.all_to_all(jnp.broadcast_to(part[None], (count,) + part.shape), axes, 0, 0)


def z_neighbours(part):
    za, zb = lax.axis_size("za"), lax.axis_size("zb")
    return [lax.ppermute(part, ("za", "zb"), shifted(za, zb, by)) for by in (1, -1, -2)]


def by_residue(own, others):
    below, above, far = others
    zb = lax.axis_index("zb")
    out = []
    for r in range(4):
        away = (r - zb) % 4
        out.append(
            jnp.where(away == 0, own, jnp.where(away == 1, above, jnp.where(away == 2, far, below)))
        )
    return jnp.stack(out)


def body(panel, row_scale, expert_ids, weight, up_branch, cotangent):
    n_yl, n_core = lax.axis_size("yl"), lax.axis_size("core")
    slot_count = up_branch.shape[0] // (n_yl * n_core)
    depth, width = weight.shape
    model = panel.shape[1]
    cut = (width // 2 + 127) // 128 * 128

    hit = jnp.any(expert_ids == 0, axis=1)
    place = jnp.cumsum(hit.astype(jnp.int32)) - 1
    slots = jnp.arange(slot_count, dtype=jnp.int32)
    select = ((place[None, :] == slots[:, None]) & hit[None, :]).astype(jnp.bfloat16)
    own_rows = jnp.dot(select, panel, preferred_element_type=jnp.float32).astype(jnp.bfloat16)
    own_scale = jnp.dot(
        select, jnp.broadcast_to(row_scale[:, None], (row_scale.shape[0], 128)),
        preferred_element_type=jnp.float32,
    ).astype(jnp.bfloat16)
    sent = jnp.concatenate([own_rows, own_scale], axis=1)
    got = lax.all_gather(sent, TENSOR, axis=0, tiled=True)
    rows = got[:, :model]
    scales32 = got[:, model:model + 1].astype(jnp.float32)

    far = everyone(weight, ("za", "yh")).reshape(4, 2, depth, width)
    one, two = far[..., :cut], far[..., cut:]
    one_z = by_residue(one, z_neighbours(one))
    two_x = everyone(two, ("x",))
    two_z = z_neighbours(two_x)
    one_x = everyone(one_z, ("x",))
    w_one = one_x.transpose(2, 1, 3, 0, 4, 5).reshape(model, cut)
    w_two = by_residue(two_x, two_z).transpose(2, 0, 3, 1, 4, 5).reshape(model, width - cut)
    gathered = jnp.concatenate([w_one, w_two], axis=1)

    product = jnp.dot(rows, gathered, preferred_element_type=jnp.float32)
    gate = product * scales32
    sig = jax.nn.sigmoid(gate)
    upper = up_branch.astype(jnp.float32)
    hidden = (gate * sig * upper).astype(jnp.bfloat16)
    filled = scales32 > 0.0
    dgate = jnp.where(
        filled,
        cotangent.astype(jnp.float32) * upper * sig * (1.0 + gate * (1.0 - sig)),
        0.0,
    ).astype(jnp.bfloat16)

    core = lax.axis_index("core")
    halves = dgate.reshape(n_yl, n_core, slot_count, width)

    def back(which):
        part = lax.dynamic_index_in_dim(halves, which, 1, keepdims=False)
        part = part.reshape(n_yl * slot_count, width)
        return jnp.dot(part, gathered.T, preferred_element_type=jnp.float32).astype(jnp.bfloat16)

    swapped = lax.ppermute(back(1 - core), "core", [(0, 1), (1, 0)])
    pair = (back(core).astype(jnp.float32) + swapped.astype(jnp.float32)).astype(jnp.bfloat16)
    parts = lax.all_to_all(pair.reshape(n_yl, slot_count, model), "yl", 0, 0)
    slot_grad = jnp.sum(parts.astype(jnp.float32), axis=0).astype(jnp.bfloat16)
    input_grad = jnp.einsum(
        "st,sd->td", select, slot_grad, preferred_element_type=jnp.float32
    ).astype(jnp.bfloat16)
    return (hidden, input_grad)


def solution(mesh):
    fine = Mesh(mesh.devices.reshape(SIZES), AXES)
    in_specs = (
        P(AXES, None),
        P(AXES),
        P(AXES, None),
        P(GROUP, TENSOR),
        P(GROUP, TENSOR),
        P(GROUP, TENSOR),
    )
    out_specs = (P(GROUP, TENSOR), P(AXES, None))
    return jax.shard_map(body, mesh=fine, in_specs=in_specs, out_specs=out_specs, check_vma=False)
```

time: 388 us -> 201 us (0.52)
  waiting for transfers between devices: 328 us -> 42 us
  blocking collectives: 27.1 us -> 74.6 us
  starting transfers between devices: 0.12 us -> 38.2 us
  local copies, waits for them, and re-layouts: 1.61 us -> 9.5 us
  other arithmetic: 1.06 us -> 6.84 us
    all_gather x2 -> x1, waiting for transfers between devices: 273 us -> 0.01 us  [body(): got = lax.all_gather(sent, TENSOR, axis=0, tiled=True)]
    all_to_all x0 -> x2, blocking collectives: none -> 74.6 us  [the longest x1 43.9 us: everyone(): lax.all_to_all(jnp.broadcast_to(part[None], (count,) + part.shape), axes,...]
    reduce_scatter x1 -> x0, waiting for transfers between devices: 54.3 us -> none  [body(): lax.psum_scatter(jnp.dot(dgate, gathered.T, preferred_element_type=jnp.fl...]
    ppermute x0 -> x7, waiting for transfers between devices: none -> 34.4 us  [the longest x6 31.9 us: z_neighbours(): lax.ppermute(part, ('za', 'zb'), shifted(za, zb, by))]
    ppermute x0 -> x7, starting transfers between devices: none -> 30.5 us  [the longest x6 24.8 us: z_neighbours(): lax.ppermute(part, ('za', 'zb'), shifted(za, zb, by))]
    unnamed x1 -> x0, blocking collectives: 27.1 us -> none
    all_to_all x0 -> x2, starting transfers between devices: none -> 7.64 us  [everyone(): lax.all_to_all(jnp.broadcast_to(part[None], (count,) + part.shape), axes,...]
    all_to_all x0 -> x2, waiting for transfers between devices: none -> 7.6 us  [everyone(): lax.all_to_all(jnp.broadcast_to(part[None], (count,) + part.shape), axes,...]
  transfers between devices with their start and end apart: 3 -> 10, of which waited for: 3 -> 4; matrix products, arithmetic and copies ran while one was open for 1% -> 4% of each run, Pallas kernels for 0% -> 0%
where the time goes in v1:
time: 201 us; the launch traced here: 200 us
  blocking collectives  74.6 us (37%)
  waiting for transfers between devices  42 us (21%)
  starting transfers between devices  38.2 us (19%)
  matrix products  15 us (7%)
  between operations  14.3 us (7%)
  local copies, waits for them, and re-layouts  9.5 us (5%)
  other arithmetic  6.84 us (3%)
    all_to_all x1, blocking collectives, everyone(): lax.all_to_all(jnp.broadcast_to(part[None], (count,) + part.shape), axes,...  43.9 us
    ppermute x6, waiting for transfers between devices, z_neighbours(): lax.ppermute(part, ('za', 'zb'), shifted(za, zb, by))  31.9 us
    all_to_all x1, blocking collectives, body(): parts = lax.all_to_all(pair.reshape(n_yl, slot_count, model), 'yl', 0, 0)  30.7 us
    ppermute x6, starting transfers between devices, z_neighbours(): lax.ppermute(part, ('za', 'zb'), shifted(za, zb, by))  24.8 us
    all_to_all x2, starting transfers between devices, everyone(): lax.all_to_all(jnp.broadcast_to(part[None], (count,) + part.shape), axes,...  7.64 us
    all_to_all x2, waiting for transfers between devices, everyone(): lax.all_to_all(jnp.broadcast_to(part[None], (count,) + part.shape), axes,...  7.6 us
    dot_general x1, matrix products, body(): product = jnp.dot(rows, gathered, preferred_element_type=jnp.float32)  7.21 us
    ppermute x1, starting transfers between devices, body(): swapped = lax.ppermute(back(1 - core), 'core', [(0, 1), (1, 0)])  5.76 us
  transfers between devices with their start and end apart: 10, of which 4 were waited for; matrix products, arithmetic and copies ran while one was open for 4% of the time, Pallas kernels for 0%

profile of v1, /device:TPU:1, one launch (start us, length us, event | category | flops | bytes accessed | tf_op | source)
XLA Modules:
  0.0 200.5 jit_solution(343499926775370031)
XLA Ops:
  7.2 0.8 compare_reduce_fusion
  8.7 0.9 convolution_convert_fusion.4
  9.5 0.8 pad_maximum_fusion.9
  10.3 43.9 %all_to_all.20 = bf16[8,24,672]{2,1,0:T(8,128)(2,1)S(1)} all-to-all(bf16[8,24,672]{2,1,0:T(8,128)(2,1)S(1)} %broadcast_in_dim.19), channel_id=1, replica_groups=mesh['za'=4,'zb'=4,'yh'=2,'x'=4,'yl'=4,'core'=2] {'za','yh'}, dimensions={0} | all-to-all | bytes 516096 | tf_op jit(solution)/shard_map/all_to_all | solution.py:19
  54.2 10.8 %collective-permute-start = (bf16[4,2,24,384]{3,2,1,0:T(8,128)(2,1)S(1)}, bf16[4,2,24,384]{3,2,1,0:T(8,128)(2,1)S(1)}, u32[]{:S(2)}, u32[]{:S(2)}) collective-permute-start(bf16[4,2,24,384]{3,2,1,0:T(8,128)(2,1)S(1)} %slice.17), channel_id=1, source_target_pairs={{0,960},{64,0},{128,64},{192,128},{256,192},{320,256},{384,320},{4... | collective-permute-start | bytes 442376 | tf_op jit(solution)/shard_map/ppermute | solution.py:24
  65.0 2.2 %collective-permute-start.1 = (bf16[4,2,24,384]{3,2,1,0:T(8,128)(2,1)S(1)}, bf16[4,2,24,384]{3,2,1,0:T(8,128)(2,1)S(1)}, u32[]{:S(2)}, u32[]{:S(2)}) collective-permute-start(bf16[4,2,24,384]{3,2,1,0:T(8,128)(2,1)S(1)} %slice.17), channel_id=1, source_target_pairs={{0,896},{64,960},{128,0},{192,64},{256,128},{320,192},{384,256},{4... | collective-permute-start | bytes 442376 | tf_op jit(solution)/shard_map/ppermute | solution.py:24
  67.2 3.4 %collective-permute-start.2 = (bf16[4,2,24,384]{3,2,1,0:T(8,128)(2,1)S(1)}, bf16[4,2,24,384]{3,2,1,0:T(8,128)(2,1)S(1)}, u32[]{:S(2)}, u32[]{:S(2)}) collective-permute-start(bf16[4,2,24,384]{3,2,1,0:T(8,128)(2,1)S(1)} %slice.17), channel_id=1, source_target_pairs={{0,64},{64,128},{128,192},{192,256},{256,320},{320,384},{384,448},... | collective-permute-start | bytes 442376 | tf_op jit(solution)/shard_map/ppermute | solution.py:24
  70.7 0.9 broadcast_in_dim.21
  71.6 4.0 %all-to-all-start.2 = ((bf16[4,4,2,24,288]{4,3,2,1,0:T(8,128)(2,1)}), bf16[4,4,2,24,288]{4,3,2,1,0:T(8,128)(2,1)S(1)}, u32[]{:S(2)}, u32[]{:S(2)}) async-start(bf16[4,4,2,24,288]{4,3,2,1,0:T(8,128)(2,1)} %broadcast_in_dim.21), calls=%async_computation.2 | async-start | bytes 1179648 | tf_op jit(solution)/shard_map/all_to_all | solution.py:19
  75.8 7.6 %all-to-all-done.2 = bf16[4,4,2,24,288]{4,3,2,1,0:T(8,128)(2,1)S(1)} async-done(((bf16[4,4,2,24,288]{4,3,2,1,0:T(8,128)(2,1)}), bf16[4,4,2,24,288]{4,3,2,1,0:T(8,128)(2,1)S(1)}, u32[]{:S(2)}, u32[]{:S(2)}) %all-to-all-start.2) | async-done | bytes 442400 | tf_op jit(solution)/shard_map/all_to_all | solution.py:19
  83.4 1.7 broadcast_in_dim.20
  85.1 3.6 %all-to-all-start.1 = ((bf16[4,4,4,2,24,384]{5,4,3,1,2,0:T(8,128)(2,1)}), bf16[4,4,4,2,24,384]{5,4,3,1,2,0:T(8,128)(2,1)S(1)}, u32[]{:S(2)}, u32[]{:S(2)}) async-start(bf16[4,4,4,2,24,384]{5,4,3,1,2,0:T(8,128)(2,1)} %broadcast_in_dim.20), calls=%async_computation.1 | async-start | bytes 4718592 | tf_op jit(solution)/shard_map/all_to_all | solution.py:19
  88.8 3.4 %collective-permute-start.3 = (bf16[4,4,2,24,288]{4,3,2,1,0:T(8,128)(2,1)}, bf16[4,4,2,24,288]{4,3,2,1,0:T(8,128)(2,1)}, u32[]{:S(2)}, u32[]{:S(2)}) collective-permute-start(bf16[4,4,2,24,288]{4,3,2,1,0:T(8,128)(2,1)} %copy-done.1), channel_id=1, source_target_pairs={{0,960},{64,0},{128,64},{192,128},{256,192},{320,256},{384,320},{4... | collective-permute-start | bytes 1327112 | tf_op jit(solution)/shard_map/ppermute | solution.py:24
  92.2 1.9 collective-permute-start.4
  94.1 3.1 %collective-permute-start.5 = (bf16[4,4,2,24,288]{4,3,2,1,0:T(8,128)(2,1)}, bf16[4,4,2,24,288]{4,3,2,1,0:T(8,128)(2,1)}, u32[]{:S(2)}, u32[]{:S(2)}) collective-permute-start(bf16[4,4,2,24,288]{4,3,2,1,0:T(8,128)(2,1)} %copy-done.1), channel_id=1, source_target_pairs={{0,64},{64,128},{128,192},{192,256},{256,320},{320,384},{384,448},... | collective-permute-start | bytes 1327112 | tf_op jit(solution)/shard_map/ppermute | solution.py:24
  97.2 5.3 %collective-permute-done.3 = bf16[4,4,2,24,288]{4,3,2,1,0:T(8,128)(2,1)} collective-permute-done((bf16[4,4,2,24,288]{4,3,2,1,0:T(8,128)(2,1)}, bf16[4,4,2,24,288]{4,3,2,1,0:T(8,128)(2,1)}, u32[]{:S(2)}, u32[]{:S(2)}) %collective-permute-start.3) | collective-permute-done | bytes 442400 | tf_op jit(solution)/shard_map/ppermute | solution.py:24
  102.5 26.6 %collective-permute-done.4 = bf16[4,4,2,24,288]{4,3,2,1,0:T(8,128)(2,1)} collective-permute-done((bf16[4,4,2,24,288]{4,3,2,1,0:T(8,128)(2,1)}, bf16[4,4,2,24,288]{4,3,2,1,0:T(8,128)(2,1)}, u32[]{:S(2)}, u32[]{:S(2)}) %collective-permute-start.4) | collective-permute-done | bytes 442400 | tf_op jit(solution)/shard_map/ppermute | solution.py:24
  129.2 2.0 select_bitcast_fusion.3
  131.2 0.6 maximum_bitcast_fusion
  131.7 1.8 copy.25
  133.5 1.7 copy.24
  135.3 1.0 convert_reduce_fusion
  136.3 1.0 fusion.11
  137.3 7.2 %fusion.10 = (bf16[384,672]{0,1:T(8,128)(2,1)}, bf16[384,672]{0,1:T(8,128)(2,1)}) fusion(bf16[384,672]{0,1:T(8,128)(2,1)} %param.10, bf16[384,672]{0,1:T(8,128)(2,1)} %param.11, pred[384]{0:T(512)(128)(4,1)S(1)} %fusion.11, f32[384]{0:T(512)S(1)} %convert_reduce_fusion, bf16[3072,288]{1,0:T(8,128)(2,1)} %bitcast.39, bf16[3072,384]{1,0:T(8,128)(2,1)} %bitcast.42, ...), kind=kOutput, calls=%fused_computation.18 | convolution fusion | flops 1598091264 | bytes 9144192 | tf_op jit(solution)/shard_map/dot_general | solution.py:70
  144.6 2.1 %copy.26 = bf16[384,672]{1,0:T(8,128)(2,1)} copy(bf16[384,672]{0,1:T(8,128)(2,1)} %get-tuple-element.6) | data formatting | bytes 1032192 | tf_op jit(solution)/shard_map/convert_element_type | solution.py:80
  146.6 1.1 constant_dynamic-slice_fusion.1
  147.8 3.5 %convolution_convert_fusion = bf16[192,3072]{1,0:T(8,128)(2,1)S(1)} fusion(bf16[192,672]{1,0:T(8,128)(2,1)S(1)} %bitcast.51, bf16[3072,288]{1,0:T(8,128)(2,1)S(1)} %bitcast.40, bf16[3072,384]{1,0:T(8,128)(2,1)} %bitcast.43), kind=kOutput, calls=%fused_computation.1 | convolution fusion | flops 801570816 | bytes 5566464 | tf_op jit(solution)/shard_map/dot_general | solution.py:88
  151.3 5.8 %collective-permute-start.6 = (bf16[192,3072]{1,0:T(8,128)(2,1)S(1)}, bf16[192,3072]{1,0:T(8,128)(2,1)S(1)}, u32[]{:S(2)}, u32[]{:S(2)}) collective-permute-start(bf16[192,3072]{1,0:T(8,128)(2,1)S(1)} %convolution_convert_fusion), channel_id=1, source_target_pairs={{0,1},{1,0},{2,3},{3,2},{4,5},{5,4},{6,7},{7,6},{8,9},{9,8},{10,11... | collective-permute-start | bytes 3538952 | tf_op jit(solution)/shard_map/ppermute | solution.py:90
  157.0 2.5 %collective-permute-done.6 = bf16[192,3072]{1,0:T(8,128)(2,1)S(1)} collective-permute-done((bf16[192,3072]{1,0:T(8,128)(2,1)S(1)}, bf16[192,3072]{1,0:T(8,128)(2,1)S(1)}, u32[]{:S(2)}, u32[]{:S(2)}) %collective-permute-start.6) | collective-permute-done | bytes 1179680 | tf_op jit(solution)/shard_map/ppermute | solution.py:90
  159.5 1.9 add_convert_fusion
  161.4 30.7 %all_to_all.21 = bf16[4,48,3072]{2,1,0:T(8,128)(2,1)S(1)} all-to-all(bf16[4,48,3072]{2,1,0:T(8,128)(2,1)S(1)} %bitcast.49), channel_id=1, replica_groups=mesh['za'=4,'zb'=4,'yh'=2,'x'=4,'yl'=4,'core'=2] {'yl'}, dimensions={0} | all-to-all | bytes 2359296 | tf_op jit(solution)/shard_map/all_to_all | solution.py:92
  192.3 1.3 convolution_convert_fusion.2
  (29 shorter events, 1.2 us)
Async XLA Ops:
  7.2 1.2 copy-start
  7.2 3.1 %copy-start.4 = (bf16[24,672]{1,0:T(8,128)(2,1)S(1)}, bf16[24,672]{1,0:T(8,128)(2,1)}, u32[]{:S(2)}) copy-start(bf16[24,672]{1,0:T(8,128)(2,1)} %param.9) | copy-start | bytes 96772
  7.2 128.1 %all-gather.2.cloned.1.call-start = ((), (), s32[]{:S(2)}) async-start(), calls=%async_computation.4 | async-start | bytes 2764800 | tf_op jit(solution)/shard_map/all_gather | solution.py:56
  54.2 21.4 %collective-permute-start = (bf16[4,2,24,384]{3,2,1,0:T(8,128)(2,1)S(1)}, bf16[4,2,24,384]{3,2,1,0:T(8,128)(2,1)S(1)}, u32[]{:S(2)}, u32[]{:S(2)}) collective-permute-start(bf16[4,2,24,384]{3,2,1,0:T(8,128)(2,1)S(1)} %slice.17), channel_id=1, source_target_pairs={{0,960},{64,0},{128,64},{192,128},{256,192},{320,256},{384,320},{4... | collective-permute-start | bytes 442376 | tf_op jit(solution)/shard_map/ppermute | solution.py:24
  65.0 10.6 %collective-permute-start.1 = (bf16[4,2,24,384]{3,2,1,0:T(8,128)(2,1)S(1)}, bf16[4,2,24,384]{3,2,1,0:T(8,128)(2,1)S(1)}, u32[]{:S(2)}, u32[]{:S(2)}) collective-permute-start(bf16[4,2,24,384]{3,2,1,0:T(8,128)(2,1)S(1)} %slice.17), channel_id=1, source_target_pairs={{0,896},{64,960},{128,0},{192,64},{256,128},{320,192},{384,256},{4... | collective-permute-start | bytes 442376 | tf_op jit(solution)/shard_map/ppermute | solution.py:24
  67.2 8.4 %collective-permute-start.2 = (bf16[4,2,24,384]{3,2,1,0:T(8,128)(2,1)S(1)}, bf16[4,2,24,384]{3,2,1,0:T(8,128)(2,1)S(1)}, u32[]{:S(2)}, u32[]{:S(2)}) collective-permute-start(bf16[4,2,24,384]{3,2,1,0:T(8,128)(2,1)S(1)} %slice.17), channel_id=1, source_target_pairs={{0,64},{64,128},{128,192},{192,256},{256,320},{320,384},{384,448},... | collective-permute-start | bytes 442376 | tf_op jit(solution)/shard_map/ppermute | solution.py:24
  71.6 11.8 %all-to-all-start.2 = ((bf16[4,4,2,24,288]{4,3,2,1,0:T(8,128)(2,1)}), bf16[4,4,2,24,288]{4,3,2,1,0:T(8,128)(2,1)S(1)}, u32[]{:S(2)}, u32[]{:S(2)}) async-start(bf16[4,4,2,24,288]{4,3,2,1,0:T(8,128)(2,1)} %broadcast_in_dim.21), calls=%async_computation.2 | async-start | bytes 1179648 | tf_op jit(solution)/shard_map/all_to_all | solution.py:19
  83.4 1.7 copy-start.1
  85.1 48.4 %all-to-all-start.1 = ((bf16[4,4,4,2,24,384]{5,4,3,1,2,0:T(8,128)(2,1)}), bf16[4,4,4,2,24,384]{5,4,3,1,2,0:T(8,128)(2,1)S(1)}, u32[]{:S(2)}, u32[]{:S(2)}) async-start(bf16[4,4,4,2,24,384]{5,4,3,1,2,0:T(8,128)(2,1)} %broadcast_in_dim.20), calls=%async_computation.1 | async-start | bytes 4718592 | tf_op jit(solution)/shard_map/all_to_all | solution.py:19
  88.8 13.7 %collective-permute-start.3 = (bf16[4,4,2,24,288]{4,3,2,1,0:T(8,128)(2,1)}, bf16[4,4,2,24,288]{4,3,2,1,0:T(8,128)(2,1)}, u32[]{:S(2)}, u32[]{:S(2)}) collective-permute-start(bf16[4,4,2,24,288]{4,3,2,1,0:T(8,128)(2,1)} %copy-done.1), channel_id=1, source_target_pairs={{0,960},{64,0},{128,64},{192,128},{256,192},{320,256},{384,320},{4... | collective-permute-start | bytes 1327112 | tf_op jit(solution)/shard_map/ppermute | solution.py:24
  92.2 37.0 %collective-permute-start.4 = (bf16[4,4,2,24,288]{4,3,2,1,0:T(8,128)(2,1)}, bf16[4,4,2,24,288]{4,3,2,1,0:T(8,128)(2,1)}, u32[]{:S(2)}, u32[]{:S(2)}) collective-permute-start(bf16[4,4,2,24,288]{4,3,2,1,0:T(8,128)(2,1)} %copy-done.1), channel_id=1, source_target_pairs={{0,896},{64,960},{128,0},{192,64},{256,128},{320,192},{384,256},{4... | collective-permute-start | bytes 1327112 | tf_op jit(solution)/shard_map/ppermute | solution.py:24
  94.1 35.0 %collective-permute-start.5 = (bf16[4,4,2,24,288]{4,3,2,1,0:T(8,128)(2,1)}, bf16[4,4,2,24,288]{4,3,2,1,0:T(8,128)(2,1)}, u32[]{:S(2)}, u32[]{:S(2)}) collective-permute-start(bf16[4,4,2,24,288]{4,3,2,1,0:T(8,128)(2,1)} %copy-done.1), channel_id=1, source_target_pairs={{0,64},{64,128},{128,192},{192,256},{256,320},{320,384},{384,448},... | collective-permute-start | bytes 1327112 | tf_op jit(solution)/shard_map/ppermute | solution.py:24
  137.3 10.4 %copy-start.2 = (bf16[4,4,2,4,24,288]{5,4,3,2,1,0:T(8,128)(2,1)S(1)}, bf16[4,4,2,4,24,288]{5,4,3,2,1,0:T(8,128)(2,1)}, u32[]{:S(2)}) copy-start(bf16[4,4,2,4,24,288]{5,4,3,2,1,0:T(8,128)(2,1)} %copy.25) | copy-start | bytes 5308420
  147.7 11.7 %copy-start.3 = (bf16[4,4,4,2,24,384]{5,4,0,3,1,2:T(8,128)(2,1)S(1)}, bf16[4,4,4,2,24,384]{5,4,0,3,1,2:T(8,128)(2,1)}, u32[]{:S(2)}) copy-start(bf16[4,4,4,2,24,384]{5,4,0,3,1,2:T(8,128)(2,1)} %copy.24) | copy-start | bytes 7077892
  151.3 8.2 %collective-permute-start.6 = (bf16[192,3072]{1,0:T(8,128)(2,1)S(1)}, bf16[192,3072]{1,0:T(8,128)(2,1)S(1)}, u32[]{:S(2)}, u32[]{:S(2)}) collective-permute-start(bf16[192,3072]{1,0:T(8,128)(2,1)S(1)} %convolution_convert_fusion), channel_id=1, source_target_pairs={{0,1},{1,0},{2,3},{3,2},{4,5},{5,4},{6,7},{7,6},{8,9},{9,8},{10,11... | collective-permute-start | bytes 3538952 | tf_op jit(solution)/shard_map/ppermute | solution.py:90
Sparse Core Ops, SparseCore 0:
  11.3 58.6 all-gather.1

commit v2 on v1

--- a/solution.py
+++ b/solution.py
@@ -19,13 +19,16 @@
     return lax.all_to_all(jnp.broadcast_to(part[None], (count,) + part.shape), axes, 0, 0)
 
 
-def z_neighbours(part):
+def along_z(part, by):
     za, zb = lax.axis_size("za"), lax.axis_size("zb")
-    return [lax.ppermute(part, ("za", "zb"), shifted(za, zb, by)) for by in (1, -1, -2)]
+    return lax.ppermute(part, ("za", "zb"), shifted(za, zb, by))
 
 
-def by_residue(own, others):
-    below, above, far = others
+def in_order(own, other, which):
+    return jnp.where(which == 0, jnp.stack([own, other]), jnp.stack([other, own]))
+
+
+def by_residue(own, below, above, far):
     zb = lax.axis_index("zb")
     out = []
     for r in range(4):
@@ -53,19 +56,38 @@
         preferred_element_type=jnp.float32,
     ).astype(jnp.bfloat16)
     sent = jnp.concatenate([own_rows, own_scale], axis=1)
-    got = lax.all_gather(sent, TENSOR, axis=0, tiled=True)
+    core = lax.axis_index("core")
+
+    far = everyone(weight, ("za", "yh")).reshape(4, 2, depth, width)
+    far, sent = lax.optimization_barrier((far, sent))
+
+    one, two = far[..., :cut], far[..., cut:]
+    one_z = by_residue(one, along_z(one, 1), along_z(one, -1), along_z(one, -2))
+    two_x = everyone(two, ("x",))
+    zb = lax.axis_index("zb")
+    two_far = jnp.concatenate([along_z(two_x[:2], -2), along_z(two_x[2:], 2)])
+    one_x = everyone(one_z, ("x",))
+
+    near = lax.ppermute(sent, "yl", [(i, i ^ 1) for i in range(4)])
+    yl = lax.axis_index("yl")
+    two_rows = in_order(sent, near, yl % 2)
+    other_rows = lax.ppermute(two_rows, "yl", [(i, i ^ 2) for i in range(4)])
+    four_rows = in_order(two_rows, other_rows, yl // 2)
+    four_rows = four_rows.reshape(n_yl, slot_count, model + 128)
+    theirs = lax.ppermute(four_rows, "core", [(0, 1), (1, 0)])
+    got = jnp.where(core == 0, jnp.stack([four_rows, theirs], 1), jnp.stack([theirs, four_rows], 1))
+    got = got.reshape(n_yl * n_core * slot_count, model + 128)
     rows = got[:, :model]
     scales32 = got[:, model:model + 1].astype(jnp.float32)
 
-    far = everyone(weight, ("za", "yh")).reshape(4, 2, depth, width)
-    one, two = far[..., :cut], far[..., cut:]
-    one_z = by_residue(one, z_neighbours(one))
-    two_x = everyone(two, ("x",))
-    two_z = z_neighbours(two_x)
-    one_x = everyone(one_z, ("x",))
-    w_one = one_x.transpose(2, 1, 3, 0, 4, 5).reshape(model, cut)
-    w_two = by_residue(two_x, two_z).transpose(2, 0, 3, 1, 4, 5).reshape(model, width - cut)
-    gathered = jnp.concatenate([w_one, w_two], axis=1)
+    whole = jnp.zeros((4, 4, 2, 4, depth, width), jnp.bfloat16)
+    zero = jnp.zeros((), jnp.int32)
+    for piece, by in ((two_x, 0), (along_z(two_x, 1), -1), (along_z(two_x, -1), 1), (two_far, 2)):
+        piece = piece.transpose(1, 2, 0, 3, 4)[:, None]
+        at = (zero, (zb + by + 4) % 4, zero, zero, zero, zero + cut)
+        whole = lax.dynamic_update_slice(whole, piece, at)
+    whole = whole.at[..., :cut].set(one_x.transpose(2, 1, 3, 0, 4, 5))
+    gathered = whole.reshape(model, width)
 
     product = jnp.dot(rows, gathered, preferred_element_type=jnp.float32)
     gate = product * scales32
@@ -79,17 +101,13 @@
         0.0,
     ).astype(jnp.bfloat16)
 
-    core = lax.axis_index("core")
-    halves = dgate.reshape(n_yl, n_core, slot_count, width)
-
-    def back(which):
-        part = lax.dynamic_index_in_dim(halves, which, 1, keepdims=False)
-        part = part.reshape(n_yl * slot_count, width)
-        return jnp.dot(part, gathered.T, preferred_element_type=jnp.float32).astype(jnp.bfloat16)
-
-    swapped = lax.ppermute(back(1 - core), "core", [(0, 1), (1, 0)])
-    pair = (back(core).astype(jnp.float32) + swapped.astype(jnp.float32)).astype(jnp.bfloat16)
-    parts = lax.all_to_all(pair.reshape(n_yl, slot_count, model), "yl", 0, 0)
+    partial = jnp.dot(dgate, gathered.T, preferred_element_type=jnp.float32).astype(jnp.bfloat16)
+    partial = partial.reshape(n_yl, n_core, slot_count, model)
+    given = lax.dynamic_index_in_dim(partial, 1 - core, 1, keepdims=False)
+    kept = lax.dynamic_index_in_dim(partial, core, 1, keepdims=False)
+    swapped = lax.ppermute(given, "core", [(0, 1), (1, 0)])
+    pair = (kept.astype(jnp.float32) + swapped.astype(jnp.float32)).astype(jnp.bfloat16)
+    parts = lax.all_to_all(pair, "yl", 0, 0)
     slot_grad = jnp.sum(parts.astype(jnp.float32), axis=0).astype(jnp.bfloat16)
     input_grad = jnp.einsum(
         "st,sd->td", select, slot_grad, preferred_element_type=jnp.float32

time: 201 us -> 182 us (0.905)
  blocking collectives: 74.6 us -> 31 us
  starting transfers between devices: 38.2 us -> 76.2 us
  between operations: 14.3 us -> 1.04 us
  waiting for transfers between devices: 42 us -> 33 us
  other arithmetic: 6.84 us -> 13 us
  local copies, waits for them, and re-layouts: 9.5 us -> 13.9 us
  matrix products: 15 us -> 12.8 us
    all_to_all x2 -> x1, blocking collectives: 74.6 us -> 31 us  [body(): parts = lax.all_to_all(pair, 'yl', 0, 0)]
    all_to_all x2 -> x3, starting transfers between devices: 7.64 us -> 32.5 us  [everyone(): lax.all_to_all(jnp.broadcast_to(part[None], (count,) + part.shape), axes,...]
    ppermute x7 -> x11, waiting for transfers between devices: 34.4 us -> 18.2 us  [the longest x1 8.66 us: body(): other_rows = lax.ppermute(two_rows, 'yl', [(i, i ^ 2) for i in range(4)])]
    ppermute x7 -> x11, starting transfers between devices: 30.5 us -> 43.7 us  [the longest x7 31.1 us: along_z(): return lax.ppermute(part, ('za', 'zb'), shifted(za, zb, by))]
    select_n x0 -> x4, other arithmetic: none -> 7.76 us  [the longest x3 4.76 us: in_order(): jnp.where(which == 0, jnp.stack([own, other]), jnp.stack([other, own]))]
    all_to_all x2 -> x3, waiting for transfers between devices: 7.6 us -> 14.8 us  [everyone(): lax.all_to_all(jnp.broadcast_to(part[None], (count,) + part.shape), axes,...]
    dynamic_update_slice x0 -> x3, local copies, waits for them, and re-layouts: none -> 2.77 us  [body(): whole = lax.dynamic_update_slice(whole, piece, at)]
    broadcast_in_dim x0 -> x1, local copies, waits for them, and re-layouts: none -> 2.69 us  [body(): whole = jnp.zeros((4, 4, 2, 4, depth, width), jnp.bfloat16)]
  transfers between devices with their start and end apart: 10 -> 14, of which waited for: 4 -> 5; matrix products, arithmetic and copies ran while one was open for 4% -> 11% of each run, Pallas kernels for 0% -> 0%
where the time goes in v2:
time: 182 us; the launch traced here: 181 us
  starting transfers between devices  76.2 us (42%)
  waiting for transfers between devices  33 us (18%)
  blocking collectives  31 us (17%)
  local copies, waits for them, and re-layouts  13.9 us (8%)
  other arithmetic  13 us (7%)
  matrix products  12.8 us (7%)
    all_to_all x3, starting transfers between devices, everyone(): lax.all_to_all(jnp.broadcast_to(part[None], (count,) + part.shape), axes,...  32.5 us
    ppermute x7, starting transfers between devices, along_z(): return lax.ppermute(part, ('za', 'zb'), shifted(za, zb, by))  31.1 us
    all_to_all x1, blocking collectives, body(): parts = lax.all_to_all(pair, 'yl', 0, 0)  31 us
    all_to_all x3, waiting for transfers between devices, everyone(): lax.all_to_all(jnp.broadcast_to(part[None], (count,) + part.shape), axes,...  14.8 us
    ppermute x1, waiting for transfers between devices, body(): other_rows = lax.ppermute(two_rows, 'yl', [(i, i ^ 2) for i in range(4)])  8.66 us
    dot_general x1, matrix products, body(): product = jnp.dot(rows, gathered, preferred_element_type=jnp.float32)  5.74 us
    ppermute x1, waiting for transfers between devices, body(): near = lax.ppermute(sent, 'yl', [(i, i ^ 1) for i in range(4)])  5.63 us
    ppermute x1, starting transfers between devices, body(): swapped = lax.ppermute(given, 'core', [(0, 1), (1, 0)])  5.39 us
  transfers between devices with their start and end apart: 14, of which 5 were waited for; matrix products, arithmetic and copies ran while one was open for 11% of the time, Pallas kernels for 0%

profile of v2, /device:TPU:1, one launch (start us, length us, event | category | flops | bytes accessed | tf_op | source)
XLA Modules:
  0.0 181.1 jit_solution(14371570031913206321)
XLA Ops:
  0.6 1.6 broadcast_in_dim.56
  2.2 24.5 %all-to-all-start = ((bf16[8,24,672]{2,1,0:T(8,128)(2,1)}), bf16[8,24,672]{2,1,0:T(8,128)(2,1)S(1)}, u32[]{:S(2)}, u32[]{:S(2)}) async-start(bf16[8,24,672]{2,1,0:T(8,128)(2,1)} %broadcast_in_dim.56), calls=%async_computation | async-start | bytes 589824 | tf_op jit(solution)/shard_map/all_to_all | solution.py:19
  29.0 14.8 %all-to-all-done = bf16[8,24,672]{2,1,0:T(8,128)(2,1)S(1)} async-done(((bf16[8,24,672]{2,1,0:T(8,128)(2,1)}), bf16[8,24,672]{2,1,0:T(8,128)(2,1)S(1)}, u32[]{:S(2)}, u32[]{:S(2)}) %all-to-all-start) | async-done | bytes 258080 | tf_op jit(solution)/shard_map/all_to_all | solution.py:19
  43.8 13.4 %collective-permute-start.7 = (bf16[4,2,24,384]{3,2,1,0:T(8,128)(2,1)S(1)}, bf16[4,2,24,384]{3,2,1,0:T(8,128)(2,1)S(1)}, u32[]{:S(2)}, u32[]{:S(2)}) collective-permute-start(bf16[4,2,24,384]{3,2,1,0:T(8,128)(2,1)S(1)} %slice.59), channel_id=1, source_target_pairs={{0,960},{64,0},{128,64},{192,128},{256,192},{320,256},{384,320},{4... | collective-permute-start | bytes 442376 | tf_op jit(solution)/shard_map/ppermute | solution.py:24
  57.2 1.9 %collective-permute-start.8 = (bf16[4,2,24,384]{3,2,1,0:T(8,128)(2,1)S(1)}, bf16[4,2,24,384]{3,2,1,0:T(8,128)(2,1)S(1)}, u32[]{:S(2)}, u32[]{:S(2)}) collective-permute-start(bf16[4,2,24,384]{3,2,1,0:T(8,128)(2,1)S(1)} %slice.59), channel_id=1, source_target_pairs={{0,896},{64,960},{128,0},{192,64},{256,128},{320,192},{384,256},{4... | collective-permute-start | bytes 442376 | tf_op jit(solution)/shard_map/ppermute | solution.py:24
  59.1 3.1 %collective-permute-start.9 = (bf16[4,2,24,384]{3,2,1,0:T(8,128)(2,1)S(1)}, bf16[4,2,24,384]{3,2,1,0:T(8,128)(2,1)}, u32[]{:S(2)}, u32[]{:S(2)}) collective-permute-start(bf16[4,2,24,384]{3,2,1,0:T(8,128)(2,1)S(1)} %slice.59), channel_id=1, source_target_pairs={{0,64},{64,128},{128,192},{192,256},{256,320},{320,384},{384,448},... | collective-permute-start | bytes 442376 | tf_op jit(solution)/shard_map/ppermute | solution.py:24
  63.3 4.0 %all-to-all-start.1 = ((bf16[4,4,2,24,288]{4,3,2,1,0:T(8,128)(2,1)}), bf16[4,4,2,24,288]{4,3,2,1,0:T(8,128)(2,1)S(1)}, u32[]{:S(2)}, u32[]{:S(2)}) async-start(bf16[4,4,2,24,288]{4,3,2,1,0:T(8,128)(2,1)} %broadcast_in_dim.59), calls=%async_computation.1 | async-start | bytes 1179648 | tf_op jit(solution)/shard_map/all_to_all | solution.py:19
  67.3 2.4 %collective-permute-start = (bf16[48,3200]{1,0:T(8,128)(2,1)S(1)}, bf16[48,3200]{1,0:T(8,128)(2,1)S(1)}, u32[]{:S(2)}, u32[]{:S(2)}) collective-permute-start(bf16[48,3200]{1,0:T(8,128)(2,1)S(1)} %pad_maximum_fusion.1), channel_id=1, source_target_pairs={{0,2},{2,0},{4,6},{6,4},{1,3},{3,1},{5,7},{7,5},{8,10},{10,8},{12,... | collective-permute-start | bytes 921608 | tf_op jit(solution)/shard_map/ppermute | solution.py:71
  71.0 5.6 %collective-permute-done = bf16[48,3200]{1,0:T(8,128)(2,1)S(1)} collective-permute-done((bf16[48,3200]{1,0:T(8,128)(2,1)S(1)}, bf16[48,3200]{1,0:T(8,128)(2,1)S(1)}, u32[]{:S(2)}, u32[]{:S(2)}) %collective-permute-start) | collective-permute-done | bytes 307232 | tf_op jit(solution)/shard_map/ppermute | solution.py:71
  77.6 2.4 %collective-permute-start.1 = (bf16[2,48,3200]{2,1,0:T(8,128)(2,1)}, bf16[2,48,3200]{2,1,0:T(8,128)(2,1)}, u32[]{:S(2)}, u32[]{:S(2)}) collective-permute-start(bf16[2,48,3200]{2,1,0:T(8,128)(2,1)} %maximum_select_fusion.3), channel_id=1, source_target_pairs={{0,4},{2,6},{4,0},{6,2},{1,5},{3,7},{5,1},{7,3},{8,12},{10,14},{12... | collective-permute-start | bytes 1843208 | tf_op jit(solution)/shard_map/ppermute | solution.py:74
  80.0 1.7 broadcast_in_dim.64
  81.8 4.0 %all-to-all-start.2 = ((bf16[4,4,4,2,24,384]{5,4,3,1,2,0:T(8,128)(2,1)}), bf16[4,4,4,2,24,384]{5,4,3,1,2,0:T(8,128)(2,1)S(1)}, u32[]{:S(2)}, u32[]{:S(2)}) async-start(bf16[4,4,4,2,24,384]{5,4,3,1,2,0:T(8,128)(2,1)} %broadcast_in_dim.64), calls=%async_computation.2 | async-start | bytes 4718592 | tf_op jit(solution)/shard_map/all_to_all | solution.py:19
  85.7 1.2 maximum_select_fusion.2
  88.1 2.2 %collective-permute-start.5 = (bf16[2,4,2,24,288]{4,3,2,1,0:T(8,128)(2,1)S(1)}, bf16[2,4,2,24,288]{4,3,2,1,0:T(8,128)(2,1)S(1)}, u32[]{:S(2)}, u32[]{:S(2)}) collective-permute-start(bf16[2,4,2,24,288]{4,3,2,1,0:T(8,128)(2,1)S(1)} %get-tuple-element.22), channel_id=1, source_target_pairs={{0,896},{64,960},{128,0},{192,64},{256,128},{320,192},{384,256},{4... | collective-permute-start | bytes 663560 | tf_op jit(solution)/shard_map/ppermute | solution.py:24
  90.3 4.0 %collective-permute-start.6 = (bf16[2,4,2,24,288]{4,3,2,1,0:T(8,128)(2,1)S(1)}, bf16[2,4,2,24,288]{4,3,2,1,0:T(8,128)(2,1)S(1)}, u32[]{:S(2)}, u32[]{:S(2)}) collective-permute-start(bf16[2,4,2,24,288]{4,3,2,1,0:T(8,128)(2,1)S(1)} %get-tuple-element.23), channel_id=1, source_target_pairs={{0,128},{64,192},{128,256},{192,320},{256,384},{320,448},{384,512}... | collective-permute-start | bytes 663560 | tf_op jit(solution)/shard_map/ppermute | solution.py:24
  94.3 3.1 %collective-permute-start.3 = (bf16[4,4,2,24,288]{4,3,2,1,0:T(8,128)(2,1)S(1)}, bf16[4,4,2,24,288]{4,3,2,1,0:T(8,128)(2,1)S(1)}, u32[]{:S(2)}, u32[]{:S(2)}) collective-permute-start(bf16[4,4,2,24,288]{4,3,2,1,0:T(8,128)(2,1)S(1)} %copy-done.2), channel_id=1, source_target_pairs={{0,64},{64,128},{128,192},{192,256},{256,320},{320,384},{384,448},... | collective-permute-start | bytes 1327112 | tf_op jit(solution)/shard_map/ppermute | solution.py:24
  97.4 3.5 %collective-permute-start.4 = (bf16[4,4,2,24,288]{4,3,2,1,0:T(8,128)(2,1)S(1)}, bf16[4,4,2,24,288]{4,3,2,1,0:T(8,128)(2,1)S(1)}, u32[]{:S(2)}, u32[]{:S(2)}) collective-permute-start(bf16[4,4,2,24,288]{4,3,2,1,0:T(8,128)(2,1)S(1)} %copy-done.2), channel_id=1, source_target_pairs={{0,960},{64,0},{128,64},{192,128},{256,192},{320,256},{384,320},{4... | collective-permute-start | bytes 1327112 | tf_op jit(solution)/shard_map/ppermute | solution.py:24
  100.8 8.7 %collective-permute-done.1 = bf16[2,48,3200]{2,1,0:T(8,128)(2,1)} collective-permute-done((bf16[2,48,3200]{2,1,0:T(8,128)(2,1)}, bf16[2,48,3200]{2,1,0:T(8,128)(2,1)}, u32[]{:S(2)}, u32[]{:S(2)}) %collective-permute-start.1) | collective-permute-done | bytes 614432 | tf_op jit(solution)/shard_map/ppermute | solution.py:74
  109.5 2.6 %maximum_select_fusion.1 = bf16[2,2,48,3200]{3,2,1,0:T(8,128)(2,1)} fusion(bf16[1,2,48,3200]{3,2,1,0:T(8,128)(2,1)} %bitcast.6, bf16[1,2,48,3200]{3,2,1,0:T(8,128)(2,1)S(1)} %maximum_select_fusion.2, pred[]{:T(512)S(6)} %eq.75), kind=kLoop, calls=%fused_computation.12 | loop fusion | flops 1843200 | bytes 2457601 | tf_op jit(solution)/shard_map/jit(_where)/select_n | solution.py:28
  112.1 2.4 %collective-permute-start.2 = (bf16[4,48,3200]{2,1,0:T(8,128)(2,1)}, bf16[4,48,3200]{2,1,0:T(8,128)(2,1)}, u32[]{:S(2)}, u32[]{:S(2)}) collective-permute-start(bf16[4,48,3200]{2,1,0:T(8,128)(2,1)} %bitcast.9), channel_id=1, source_target_pairs={{0,1},{1,0},{2,3},{3,2},{4,5},{5,4},{6,7},{7,6},{8,9},{9,8},{10,11... | collective-permute-start | bytes 3686408 | tf_op jit(solution)/shard_map/ppermute | solution.py:77
  114.5 2.7 %broadcast_in_dim.58 = bf16[4,4,2,4,24,672]{5,4,3,2,1,0:T(8,128)(2,1)} broadcast(bf16[]{:T(256)} %constant.125.clone.1), dimensions={} | broadcast | bytes 4128770 | tf_op jit(solution)/shard_map/broadcast_in_dim | solution.py:83
  118.1 1.1 collective-permute-done.3
  122.0 1.8 copy_dynamic-update-slice_fusion
  123.8 3.0 %maximum_select_fusion = bf16[4,2,48,3200]{3,2,1,0:T(8,128)(2,1)S(1)} fusion(bf16[4,1,48,3200]{3,2,1,0:T(8,128)(2,1)} %bitcast.10, bf16[4,1,48,3200]{3,2,1,0:T(8,128)(2,1)} %bitcast.8, pred[]{:T(512)S(6)} %eq.74), kind=kLoop, calls=%fused_computation.3 | loop fusion | flops 3686400 | bytes 4915201 | tf_op jit(solution)/shard_map/jit(_where)/select_n | solution.py:78
  127.1 5.7 %fusion.6 = (bf16[384,672]{0,1:T(8,128)(2,1)}, f32[384,672]{0,1:T(8,128)S(1)}) fusion(bf16[384,672]{0,1:T(8,128)(2,1)S(1)} %copy-done.4, f32[384]{0:T(512)S(1)} %convert_reduce_fusion, bf16[3072,672]{1,0:T(8,128)(2,1)} %bitcast.26, bf16[384,3200]{1,0:T(8,128)(2,1)S(1)} %bitcast.59), kind=kOutput, calls=%fused_computation.15 | convolution fusion | flops 1587511296 | bytes 8554496 | tf_op jit(solution)/shard_map/dot_general | solution.py:92
  132.8 4.7 %convolution_convert_fusion = bf16[384,3072]{1,0:T(8,128)(2,1)S(1)} fusion(bf16[3072,672]{1,0:T(8,128)(2,1)} %bitcast.26, bf16[384,672]{0,1:T(8,128)(2,1)S(1)} %copy-done.4, f32[384,672]{0,1:T(8,128)S(1)} %get-tuple-element.25, bf16[384,672]{0,1:T(8,128)(2,1)S(1)} %copy-done.5, pred[384]{0:T(512)(128)(4,1)S(1)} %fusion.15), kind=kOutput, calls=%fused_computation | convolution fusion | flops 1589981184 | bytes 8552832 | tf_op jit(solution)/shard_map/dot_general | solution.py:104
  137.5 1.1 dynamic-slice_bitcast_fusion
  138.6 5.4 %collective-permute-start.10 = (bf16[4,48,3072]{2,1,0:T(8,128)(2,1)}, bf16[4,48,3072]{2,1,0:T(8,128)(2,1)}, u32[]{:S(2)}, u32[]{:S(2)}) collective-permute-start(bf16[4,48,3072]{2,1,0:T(8,128)(2,1)} %dynamic-slice_bitcast_fusion), channel_id=1, source_target_pairs={{0,1},{1,0},{2,3},{3,2},{4,5},{5,4},{6,7},{7,6},{8,9},{9,8},{10,11... | collective-permute-start | bytes 3538952 | tf_op jit(solution)/shard_map/ppermute | solution.py:108
  144.0 2.8 %collective-permute-done.10 = bf16[4,48,3072]{2,1,0:T(8,128)(2,1)} collective-permute-done((bf16[4,48,3072]{2,1,0:T(8,128)(2,1)}, bf16[4,48,3072]{2,1,0:T(8,128)(2,1)}, u32[]{:S(2)}, u32[]{:S(2)}) %collective-permute-start.10) | collective-permute-done | bytes 1179680 | tf_op jit(solution)/shard_map/ppermute | solution.py:108
  146.8 1.7 fusion.2
  148.5 31.0 %all_to_all.20 = bf16[4,48,3072]{2,1,0:T(8,128)(2,1)S(1)} all-to-all(bf16[4,48,3072]{2,1,0:T(8,128)(2,1)S(1)} %fusion.2), channel_id=1, replica_groups=mesh['za'=4,'zb'=4,'yh'=2,'x'=4,'yl'=4,'core'=2] {'yl'}, dimensions={0} | all-to-all | bytes 2359296 | tf_op jit(solution)/shard_map/all_to_all | solution.py:110
  179.8 1.3 convolution_convert_fusion.1
  (44 shorter events, 10.6 us)
Async XLA Ops:
  0.6 28.1 %copy-start = (bf16[128,3072]{1,0:T(8,128)(2,1)S(1)}, bf16[128,3072]{1,0:T(8,128)(2,1)}, u32[]{:S(2)}) copy-start(bf16[128,3072]{1,0:T(8,128)(2,1)} %param.8) | copy-start | bytes 2359300
  2.2 41.6 %all-to-all-start = ((bf16[8,24,672]{2,1,0:T(8,128)(2,1)}), bf16[8,24,672]{2,1,0:T(8,128)(2,1)S(1)}, u32[]{:S(2)}, u32[]{:S(2)}) async-start(bf16[8,24,672]{2,1,0:T(8,128)(2,1)} %broadcast_in_dim.56), calls=%async_computation | async-start | bytes 589824 | tf_op jit(solution)/shard_map/all_to_all | solution.py:19
  43.8 25.9 %collective-permute-start.7 = (bf16[4,2,24,384]{3,2,1,0:T(8,128)(2,1)S(1)}, bf16[4,2,24,384]{3,2,1,0:T(8,128)(2,1)S(1)}, u32[]{:S(2)}, u32[]{:S(2)}) collective-permute-start(bf16[4,2,24,384]{3,2,1,0:T(8,128)(2,1)S(1)} %slice.59), channel_id=1, source_target_pairs={{0,960},{64,0},{128,64},{192,128},{256,192},{320,256},{384,320},{4... | collective-permute-start | bytes 442376 | tf_op jit(solution)/shard_map/ppermute | solution.py:24
  57.2 12.6 %collective-permute-start.8 = (bf16[4,2,24,384]{3,2,1,0:T(8,128)(2,1)S(1)}, bf16[4,2,24,384]{3,2,1,0:T(8,128)(2,1)S(1)}, u32[]{:S(2)}, u32[]{:S(2)}) collective-permute-start(bf16[4,2,24,384]{3,2,1,0:T(8,128)(2,1)S(1)} %slice.59), channel_id=1, source_target_pairs={{0,896},{64,960},{128,0},{192,64},{256,128},{320,192},{384,256},{4... | collective-permute-start | bytes 442376 | tf_op jit(solution)/shard_map/ppermute | solution.py:24
  59.1 10.6 %collective-permute-start.9 = (bf16[4,2,24,384]{3,2,1,0:T(8,128)(2,1)S(1)}, bf16[4,2,24,384]{3,2,1,0:T(8,128)(2,1)}, u32[]{:S(2)}, u32[]{:S(2)}) collective-permute-start(bf16[4,2,24,384]{3,2,1,0:T(8,128)(2,1)S(1)} %slice.59), channel_id=1, source_target_pairs={{0,64},{64,128},{128,192},{192,256},{256,320},{320,384},{384,448},... | collective-permute-start | bytes 442376 | tf_op jit(solution)/shard_map/ppermute | solution.py:24
  63.3 16.7 %all-to-all-start.1 = ((bf16[4,4,2,24,288]{4,3,2,1,0:T(8,128)(2,1)}), bf16[4,4,2,24,288]{4,3,2,1,0:T(8,128)(2,1)S(1)}, u32[]{:S(2)}, u32[]{:S(2)}) async-start(bf16[4,4,2,24,288]{4,3,2,1,0:T(8,128)(2,1)} %broadcast_in_dim.59), calls=%async_computation.1 | async-start | bytes 1179648 | tf_op jit(solution)/shard_map/all_to_all | solution.py:19
  67.3 9.3 %collective-permute-start = (bf16[48,3200]{1,0:T(8,128)(2,1)S(1)}, bf16[48,3200]{1,0:T(8,128)(2,1)S(1)}, u32[]{:S(2)}, u32[]{:S(2)}) collective-permute-start(bf16[48,3200]{1,0:T(8,128)(2,1)S(1)} %pad_maximum_fusion.1), channel_id=1, source_target_pairs={{0,2},{2,0},{4,6},{6,4},{1,3},{3,1},{5,7},{7,5},{8,10},{10,8},{12,... | collective-permute-start | bytes 921608 | tf_op jit(solution)/shard_map/ppermute | solution.py:71
  76.6 5.2 %copy-start.3 = (bf16[48,3200]{1,0:T(8,128)(2,1)}, bf16[48,3200]{1,0:T(8,128)(2,1)S(1)}, u32[]{:S(2)}) copy-start(bf16[48,3200]{1,0:T(8,128)(2,1)S(1)} %collective-permute-done) | copy-start | bytes 921604
  77.6 31.9 %collective-permute-start.1 = (bf16[2,48,3200]{2,1,0:T(8,128)(2,1)}, bf16[2,48,3200]{2,1,0:T(8,128)(2,1)}, u32[]{:S(2)}, u32[]{:S(2)}) collective-permute-start(bf16[2,48,3200]{2,1,0:T(8,128)(2,1)} %maximum_select_fusion.3), channel_id=1, source_target_pairs={{0,4},{2,6},{4,0},{6,2},{1,5},{3,7},{5,1},{7,3},{8,12},{10,14},{12... | collective-permute-start | bytes 1843208 | tf_op jit(solution)/shard_map/ppermute | solution.py:74
  80.0 1.8 copy-start.1
  81.8 40.2 %all-to-all-start.2 = ((bf16[4,4,4,2,24,384]{5,4,3,1,2,0:T(8,128)(2,1)}), bf16[4,4,4,2,24,384]{5,4,3,1,2,0:T(8,128)(2,1)S(1)}, u32[]{:S(2)}, u32[]{:S(2)}) async-start(bf16[4,4,4,2,24,384]{5,4,3,1,2,0:T(8,128)(2,1)} %broadcast_in_dim.64), calls=%async_computation.2 | async-start | bytes 4718592 | tf_op jit(solution)/shard_map/all_to_all | solution.py:19
  85.7 8.5 %copy-start.2 = (bf16[4,4,2,24,288]{4,3,2,1,0:T(8,128)(2,1)S(1)}, bf16[4,4,2,24,288]{4,3,2,1,0:T(8,128)(2,1)}, u32[]{:S(2)}) copy-start(bf16[4,4,2,24,288]{4,3,2,1,0:T(8,128)(2,1)} %copy-done.1) | copy-start | bytes 1327108
  88.1 33.0 %collective-permute-start.5 = (bf16[2,4,2,24,288]{4,3,2,1,0:T(8,128)(2,1)S(1)}, bf16[2,4,2,24,288]{4,3,2,1,0:T(8,128)(2,1)S(1)}, u32[]{:S(2)}, u32[]{:S(2)}) collective-permute-start(bf16[2,4,2,24,288]{4,3,2,1,0:T(8,128)(2,1)S(1)} %get-tuple-element.22), channel_id=1, source_target_pairs={{0,896},{64,960},{128,0},{192,64},{256,128},{320,192},{384,256},{4... | collective-permute-start | bytes 663560 | tf_op jit(solution)/shard_map/ppermute | solution.py:24
  90.3 30.8 %collective-permute-start.6 = (bf16[2,4,2,24,288]{4,3,2,1,0:T(8,128)(2,1)S(1)}, bf16[2,4,2,24,288]{4,3,2,1,0:T(8,128)(2,1)S(1)}, u32[]{:S(2)}, u32[]{:S(2)}) collective-permute-start(bf16[2,4,2,24,288]{4,3,2,1,0:T(8,128)(2,1)S(1)} %get-tuple-element.23), channel_id=1, source_target_pairs={{0,128},{64,192},{128,256},{192,320},{256,384},{320,448},{384,512}... | collective-permute-start | bytes 663560 | tf_op jit(solution)/shard_map/ppermute | solution.py:24
  94.3 25.0 %collective-permute-start.3 = (bf16[4,4,2,24,288]{4,3,2,1,0:T(8,128)(2,1)S(1)}, bf16[4,4,2,24,288]{4,3,2,1,0:T(8,128)(2,1)S(1)}, u32[]{:S(2)}, u32[]{:S(2)}) collective-permute-start(bf16[4,4,2,24,288]{4,3,2,1,0:T(8,128)(2,1)S(1)} %copy-done.2), channel_id=1, source_target_pairs={{0,64},{64,128},{128,192},{192,256},{256,320},{320,384},{384,448},... | collective-permute-start | bytes 1327112 | tf_op jit(solution)/shard_map/ppermute | solution.py:24
  97.4 22.8 %collective-permute-start.4 = (bf16[4,4,2,24,288]{4,3,2,1,0:T(8,128)(2,1)S(1)}, bf16[4,4,2,24,288]{4,3,2,1,0:T(8,128)(2,1)S(1)}, u32[]{:S(2)}, u32[]{:S(2)}) collective-permute-start(bf16[4,4,2,24,288]{4,3,2,1,0:T(8,128)(2,1)S(1)} %copy-done.2), channel_id=1, source_target_pairs={{0,960},{64,0},{128,64},{192,128},{256,192},{320,256},{384,320},{4... | collective-permute-start | bytes 1327112 | tf_op jit(solution)/shard_map/ppermute | solution.py:24
  112.1 11.7 %collective-permute-start.2 = (bf16[4,48,3200]{2,1,0:T(8,128)(2,1)}, bf16[4,48,3200]{2,1,0:T(8,128)(2,1)}, u32[]{:S(2)}, u32[]{:S(2)}) collective-permute-start(bf16[4,48,3200]{2,1,0:T(8,128)(2,1)} %bitcast.9), channel_id=1, source_target_pairs={{0,1},{1,0},{2,3},{3,2},{4,5},{5,4},{6,7},{7,6},{8,9},{9,8},{10,11... | collective-permute-start | bytes 3686408 | tf_op jit(solution)/shard_map/ppermute | solution.py:77
  123.8 3.3 %copy-start.4 = (bf16[384,672]{0,1:T(8,128)(2,1)S(1)}, bf16[384,672]{0,1:T(8,128)(2,1)}, u32[]{:S(2)}) copy-start(bf16[384,672]{0,1:T(8,128)(2,1)} %param.12) | copy-start | bytes 1548292
  127.1 5.8 %copy-start.5 = (bf16[384,672]{0,1:T(8,128)(2,1)S(1)}, bf16[384,672]{0,1:T(8,128)(2,1)}, u32[]{:S(2)}) copy-start(bf16[384,672]{0,1:T(8,128)(2,1)} %param.13) | copy-start | bytes 1548292
  138.6 8.2 %collective-permute-start.10 = (bf16[4,48,3072]{2,1,0:T(8,128)(2,1)}, bf16[4,48,3072]{2,1,0:T(8,128)(2,1)}, u32[]{:S(2)}, u32[]{:S(2)}) collective-permute-start(bf16[4,48,3072]{2,1,0:T(8,128)(2,1)} %dynamic-slice_bitcast_fusion), channel_id=1, source_target_pairs={{0,1},{1,0},{2,3},{3,2},{4,5},{5,4},{6,7},{7,6},{8,9},{9,8},{10,11... | collective-permute-start | bytes 3538952 | tf_op jit(solution)/shard_map/ppermute | solution.py:108

commit v3 on v2

--- a/solution.py
+++ b/solution.py
@@ -26,6 +26,10 @@
 
 def in_order(own, other, which):
     return jnp.where(which == 0, jnp.stack([own, other]), jnp.stack([other, own]))
+
+
+def nothing(array):
+    return (array[(0,) * array.ndim] * 0).astype(jnp.int32)
 
 
 def by_residue(own, below, above, far):
@@ -58,31 +62,74 @@
     sent = jnp.concatenate([own_rows, own_scale], axis=1)
     core = lax.axis_index("core")
 
+    yl = lax.axis_index("yl")
+    by_one, by_two = [(i, i ^ 1) for i in range(4)], [(i, i ^ 2) for i in range(4)]
+    near = lax.ppermute(sent, "yl", by_one)
+    opposite = lax.ppermute(sent, "yl", by_two)
+
     far = everyone(weight, ("za", "yh")).reshape(4, 2, depth, width)
-    far, sent = lax.optimization_barrier((far, sent))
+    one, two = far[..., :cut], far[..., cut:]
+    last = lax.ppermute(near, "yl", by_two)
+    two_x = everyone(two, ("x",))
+    beside = (along_z(one, 1), along_z(one, -1), along_z(one, -2))
+    one_x = everyone(by_residue(one, *beside), ("x",))
+    zb = lax.axis_index("zb")
+    out = []
+    for r in range(4):
+        away = (r - zb) % 4
+        out.append(
+            jnp.where(away == 0, own, jnp.where(away == 1, above, jnp.where(away == 2, far, below)))
+        )
+    return jnp.stack(out)
 
+
+def body(panel, row_scale, expert_ids, weight, up_branch, cotangent):
+    n_yl, n_core = lax.axis_size("yl"), lax.axis_size("core")
+    slot_count = up_branch.shape[0] // (n_yl * n_core)
+    depth, width = weight.shape
+    model = panel.shape[1]
+    cut = (width // 2 + 127) // 128 * 128
+
+    hit = jnp.any(expert_ids == 0, axis=1)
+    place = jnp.cumsum(hit.astype(jnp.int32)) - 1
+    slots = jnp.arange(slot_count, dtype=jnp.int32)
+    select = ((place[None, :] == slots[:, None]) & hit[None, :]).astype(jnp.bfloat16)
+    own_rows = jnp.dot(select, panel, preferred_element_type=jnp.float32).astype(jnp.bfloat16)
+    own_scale = jnp.dot(
+        select, jnp.broadcast_to(row_scale[:, None], (row_scale.shape[0], 128)),
+        preferred_element_type=jnp.float32,
+    ).astype(jnp.bfloat16)
+    sent = jnp.concatenate([own_rows, own_scale], axis=1)
+    core = lax.axis_index("core")
+
+    yl = lax.axis_index("yl")
+    by_one, by_two = [(i, i ^ 1) for i in range(4)], [(i, i ^ 2) for i in range(4)]
+    near = lax.ppermute(sent, "yl", by_one)
+    opposite = lax.ppermute(sent, "yl", by_two)
+
+    far = everyone(weight, ("za", "yh")).reshape(4, 2, depth, width)
     one, two = far[..., :cut], far[..., cut:]
-    one_z = by_residue(one, along_z(one, 1), along_z(one, -1), along_z(one, -2))
+    last = lax.ppermute(near, "yl", by_two)
     two_x = everyone(two, ("x",))
+    beside = (along_z(one, 1), along_z(one, -1), along_z(one, -2))
+    one_x = everyone(by_residue(one, *beside), ("x",))
+    four_rows = in_order(in_order(sent, near, yl % 2), in_order(opposite, last, yl % 2), yl // 2)
+    four_rows = four_rows.reshape(n_yl, slot_count, model + 128)
+    theirs = lax.ppermute(four_rows, "core", [(0, 1), (1, 0)])
     zb = lax.axis_index("zb")
     two_far = jnp.concatenate([along_z(two_x[:2], -2), along_z(two_x[2:], 2)])
-    one_x = everyone(one_z, ("x",))
 
-    near = lax.ppermute(sent, "yl", [(i, i ^ 1) for i in range(4)])
-    yl = lax.axis_index("yl")
-    two_rows = in_order(sent, near, yl % 2)
-    other_rows = lax.ppermute(two_rows, "yl", [(i, i ^ 2) for i in range(4)])
-    four_rows = in_order(two_rows, other_rows, yl // 2)
-    four_rows = four_rows.reshape(n_yl, slot_count, model + 128)
-    theirs = lax.ppermute(four_rows, "core", [(0, 1), (1, 0)])
-    got = jnp.where(core == 0, jnp.stack([four_rows, theirs], 1), jnp.stack([theirs, four_rows], 1))
+    below, above = along_z(two_x, 1), along_z(two_x, -1)
+    below, last = lax.optimization_barrier((below, last))
+    first = core + nothing(above) == 0
+    got = jnp.where(first, jnp.stack([four_rows, theirs], 1), jnp.stack([theirs, four_rows], 1))
     got = got.reshape(n_yl * n_core * slot_count, model + 128)
     rows = got[:, :model]
     scales32 = got[:, model:model + 1].astype(jnp.float32)
 
     whole = jnp.zeros((4, 4, 2, 4, depth, width), jnp.bfloat16)
     zero = jnp.zeros((), jnp.int32)
-    for piece, by in ((two_x, 0), (along_z(two_x, 1), -1), (along_z(two_x, -1), 1), (two_far, 2)):
+    for piece, by in ((two_x, 0), (below, -1), (above, 1), (two_far, 2)):
         piece = piece.transpose(1, 2, 0, 3, 4)[:, None]
         at = (zero, (zb + by + 4) % 4, zero, zero, zero, zero + cut)
         whole = lax.dynamic_update_slice(whole, piece, at)
@@ -101,14 +148,25 @@
         0.0,
     ).astype(jnp.bfloat16)
 
+    def pick(array, axis, which):
+        return lax.dynamic_index_in_dim(array, which, axis, keepdims=False)
+
+    def add(one, other):
+        return (one.astype(jnp.float32) + other.astype(jnp.float32)).astype(jnp.bfloat16)
+
     partial = jnp.dot(dgate, gathered.T, preferred_element_type=jnp.float32).astype(jnp.bfloat16)
-    partial = partial.reshape(n_yl, n_core, slot_count, model)
-    given = lax.dynamic_index_in_dim(partial, 1 - core, 1, keepdims=False)
-    kept = lax.dynamic_index_in_dim(partial, core, 1, keepdims=False)
-    swapped = lax.ppermute(given, "core", [(0, 1), (1, 0)])
-    pair = (kept.astype(jnp.float32) + swapped.astype(jnp.float32)).astype(jnp.bfloat16)
-    parts = lax.all_to_all(pair, "yl", 0, 0)
-    slot_grad = jnp.sum(parts.astype(jnp.float32), axis=0).astype(jnp.bfloat16)
+    partial = partial.reshape(2, 2, n_core, slot_count, model)
+
+    def returned(part):
+        swapped = lax.ppermute(pick(part, 2, 1 - core), "core", [(0, 1), (1, 0)])
+        pair = add(pick(part, 2, core), swapped)
+        near = lax.ppermute(pick(pair, 1, 1 - yl % 2), "yl", by_one)
+        four = add(pick(pair, 1, yl % 2), near)
+        far = lax.ppermute(pick(four, 0, 1 - yl // 2), "yl", by_two)
+        return add(pick(four, 0, yl // 2), far)
+
+    half = model // 2
+    slot_grad = jnp.concatenate([returned(partial[..., :half]), returned(partial[..., half:])], axis=1)
     input_grad = jnp.einsum(
         "st,sd->td", select, slot_grad, preferred_element_type=jnp.float32
     ).astype(jnp.bfloat16)

time: 182 us -> 183 us (level)
  blocking collectives: 31 us -> 0 us
  waiting for transfers between devices: 33 us -> 55.6 us
  starting transfers between devices: 76.2 us -> 86.4 us
  local copies, waits for them, and re-layouts: 13.9 us -> 18.9 us
  other arithmetic: 13 us -> 8.41 us
  matrix products: 12.8 us -> 10.6 us
    all_to_all x1 -> x0, blocking collectives: 31 us -> none  [body(): parts = lax.all_to_all(pair, 'yl', 0, 0)]
    ppermute x3 -> x9, waiting for transfers between devices: 17.1 us -> 38.1 us  [the longest x1 20.2 us: body(): last = lax.ppermute(near, 'yl', by_two)]
    ppermute x3 -> x9, starting transfers between devices: 10.2 us -> 29 us  [the longest x2 5.93 us: returned(): swapped = lax.ppermute(pick(part, 2, 1 - core), 'core', [(0, 1), (1, 0)])]
    ppermute x7, waiting for transfers between devices: 1.15 us -> 7.8 us  [along_z(): return lax.ppermute(part, ('za', 'zb'), shifted(za, zb, by))]
    ppermute x7, starting transfers between devices: 31.1 us -> 24.9 us  [along_z(): return lax.ppermute(part, ('za', 'zb'), shifted(za, zb, by))]
    unnamed x12 -> x23, local copies, waits for them, and re-layouts: 0.03 us -> 5.99 us
    all_to_all x3, waiting for transfers between devices: 14.8 us -> 9.72 us  [everyone(): lax.all_to_all(jnp.broadcast_to(part[None], (count,) + part.shape), axes,...]
    all_to_all x3, starting transfers between devices: 32.5 us -> 28.7 us  [everyone(): lax.all_to_all(jnp.broadcast_to(part[None], (count,) + part.shape), axes,...]
  transfers between devices with their start and end apart: 14 -> 20, of which waited for: 5 -> 7; matrix products, arithmetic and copies ran while one was open for 11% -> 10% of each run, Pallas kernels for 0% -> 0%
where the time goes in v3:
time: 183 us; the launch traced here: 182 us
  starting transfers between devices  86.4 us (47%)
  waiting for transfers between devices  55.6 us (30%)
  local copies, waits for them, and re-layouts  18.9 us (10%)
  matrix products  10.6 us (6%)
  other arithmetic  8.41 us (5%)
    all_to_all x3, starting transfers between devices, everyone(): lax.all_to_all(jnp.broadcast_to(part[None], (count,) + part.shape), axes,...  28.7 us
    ppermute x7, starting transfers between devices, along_z(): return lax.ppermute(part, ('za', 'zb'), shifted(za, zb, by))  24.9 us
    ppermute x1, waiting for transfers between devices, body(): last = lax.ppermute(near, 'yl', by_two)  20.2 us
    all_to_all x3, waiting for transfers between devices, everyone(): lax.all_to_all(jnp.broadcast_to(part[None], (count,) + part.shape), axes,...  9.72 us
    ppermute x2, waiting for transfers between devices, returned(): far = lax.ppermute(pick(four, 0, 1 - yl // 2), 'yl', by_two)  9.27 us
    ppermute x2, waiting for transfers between devices, returned(): near = lax.ppermute(pick(pair, 1, 1 - yl % 2), 'yl', by_one)  8.57 us
    ppermute x7, waiting for transfers between devices, along_z(): return lax.ppermute(part, ('za', 'zb'), shifted(za, zb, by))  7.8 us
    unnamed x23, local copies, waits for them, and re-layouts  5.99 us
  transfers between devices with their start and end apart: 20, of which 7 were waited for; matrix products, arithmetic and copies ran while one was open for 10% of the time, Pallas kernels for 0%

profile of v3, /device:TPU:1, one launch (start us, length us, event | category | flops | bytes accessed | tf_op | source)
XLA Modules:
  0.0 181.6 jit_solution(16714949965631553986)
XLA Ops:
  3.0 4.0 %collective-permute-start.1 = (bf16[48,3200]{1,0:T(8,128)(2,1)S(1)}, bf16[48,3200]{1,0:T(8,128)(2,1)S(1)}, u32[]{:S(2)}, u32[]{:S(2)}) collective-permute-start(bf16[48,3200]{1,0:T(8,128)(2,1)S(1)} %get-tuple-element.27), channel_id=1, source_target_pairs={{0,2},{2,0},{4,6},{6,4},{1,3},{3,1},{5,7},{7,5},{8,10},{10,8},{12,... | collective-permute-start | bytes 921608 | tf_op jit(solution)/shard_map/ppermute | solution.py:107
  7.0 4.2 %collective-permute-start.2 = (bf16[48,3200]{1,0:T(8,128)(2,1)S(1)}, bf16[48,3200]{1,0:T(8,128)(2,1)S(1)}, u32[]{:S(2)}, u32[]{:S(2)}) collective-permute-start(bf16[48,3200]{1,0:T(8,128)(2,1)S(1)} %get-tuple-element.27), channel_id=1, source_target_pairs={{0,4},{2,6},{4,0},{6,2},{1,5},{3,7},{5,1},{7,3},{8,12},{10,14},{12... | collective-permute-start | bytes 921608 | tf_op jit(solution)/shard_map/ppermute | solution.py:108
  12.0 21.0 %all-to-all-start = ((bf16[8,24,672]{2,1,0:T(8,128)(2,1)}), bf16[8,24,672]{2,1,0:T(8,128)(2,1)S(1)}, u32[]{:S(2)}, u32[]{:S(2)}) async-start(bf16[8,24,672]{2,1,0:T(8,128)(2,1)} %broadcast_in_dim.56), calls=%async_computation | async-start | bytes 589824 | tf_op jit(solution)/shard_map/all_to_all | solution.py:19
  33.0 3.8 %collective-permute-start.3 = (bf16[48,3200]{1,0:T(8,128)(2,1)S(1)}, bf16[48,3200]{1,0:T(8,128)(2,1)S(1)}, u32[]{:S(2)}, u32[]{:S(2)}) collective-permute-start(bf16[48,3200]{1,0:T(8,128)(2,1)S(1)} %collective-permute-done.1), channel_id=1, source_target_pairs={{0,4},{2,6},{4,0},{6,2},{1,5},{3,7},{5,1},{7,3},{8,12},{10,14},{12... | collective-permute-start | bytes 921608 | tf_op jit(solution)/shard_map/ppermute | solution.py:112
  36.9 20.2 %collective-permute-done.3 = bf16[48,3200]{1,0:T(8,128)(2,1)S(1)} collective-permute-done((bf16[48,3200]{1,0:T(8,128)(2,1)S(1)}, bf16[48,3200]{1,0:T(8,128)(2,1)S(1)}, u32[]{:S(2)}, u32[]{:S(2)}) %collective-permute-start.3) | collective-permute-done | bytes 307232 | tf_op jit(solution)/shard_map/ppermute | solution.py:112
  57.3 2.6 %collective-permute-start.10 = (bf16[4,2,24,384]{3,2,1,0:T(8,128)(2,1)S(1)}, bf16[4,2,24,384]{3,2,1,0:T(8,128)(2,1)S(1)}, u32[]{:S(2)}, u32[]{:S(2)}) collective-permute-start(bf16[4,2,24,384]{3,2,1,0:T(8,128)(2,1)S(1)} %slice.78), channel_id=1, source_target_pairs={{0,64},{64,128},{128,192},{192,256},{256,320},{320,384},{384,448},... | collective-permute-start | bytes 442376 | tf_op jit(solution)/shard_map/ppermute | solution.py:24
  59.9 6.3 %collective-permute-start.8 = (bf16[4,2,24,384]{3,2,1,0:T(8,128)(2,1)S(1)}, bf16[4,2,24,384]{3,2,1,0:T(8,128)(2,1)S(1)}, u32[]{:S(2)}, u32[]{:S(2)}) collective-permute-start(bf16[4,2,24,384]{3,2,1,0:T(8,128)(2,1)S(1)} %slice.78), channel_id=1, source_target_pairs={{0,960},{64,0},{128,64},{192,128},{256,192},{320,256},{384,320},{4... | collective-permute-start | bytes 442376 | tf_op jit(solution)/shard_map/ppermute | solution.py:24
  66.3 3.1 %collective-permute-start.9 = (bf16[4,2,24,384]{3,2,1,0:T(8,128)(2,1)S(1)}, bf16[4,2,24,384]{3,2,1,0:T(8,128)(2,1)S(1)}, u32[]{:S(2)}, u32[]{:S(2)}) collective-permute-start(bf16[4,2,24,384]{3,2,1,0:T(8,128)(2,1)S(1)} %slice.78), channel_id=1, source_target_pairs={{0,896},{64,960},{128,0},{192,64},{256,128},{320,192},{384,256},{4... | collective-permute-start | bytes 442376 | tf_op jit(solution)/shard_map/ppermute | solution.py:24
  70.7 3.8 %collective-permute-start.4 = (bf16[4,48,3200]{2,1,0:T(8,128)(2,1)}, bf16[4,48,3200]{2,1,0:T(8,128)(2,1)}, u32[]{:S(2)}, u32[]{:S(2)}) collective-permute-start(bf16[4,48,3200]{2,1,0:T(8,128)(2,1)} %bitcast.9), channel_id=1, source_target_pairs={{0,1},{1,0},{2,3},{3,2},{4,5},{5,4},{6,7},{7,6},{8,9},{9,8},{10,11... | collective-permute-start | bytes 3686408 | tf_op jit(solution)/shard_map/ppermute | solution.py:118
  75.5 4.0 %all-to-all-start.1 = ((bf16[4,4,2,24,288]{4,3,2,1,0:T(8,128)(2,1)}), bf16[4,4,2,24,288]{4,3,2,1,0:T(8,128)(2,1)S(1)}, u32[]{:S(2)}, u32[]{:S(2)}) async-start(bf16[4,4,2,24,288]{4,3,2,1,0:T(8,128)(2,1)} %broadcast_in_dim.57), calls=%async_computation.1 | async-start | bytes 1179648 | tf_op jit(solution)/shard_map/all_to_all | solution.py:19
  79.8 9.7 %all-to-all-done.1 = bf16[4,4,2,24,288]{4,3,2,1,0:T(8,128)(2,1)S(1)} async-done(((bf16[4,4,2,24,288]{4,3,2,1,0:T(8,128)(2,1)}), bf16[4,4,2,24,288]{4,3,2,1,0:T(8,128)(2,1)S(1)}, u32[]{:S(2)}, u32[]{:S(2)}) %all-to-all-start.1) | async-done | bytes 442400 | tf_op jit(solution)/shard_map/all_to_all | solution.py:19
  91.3 3.6 %all-to-all-start.2 = ((bf16[4,4,4,2,24,384]{5,4,3,1,2,0:T(8,128)(2,1)}), bf16[4,4,4,2,24,384]{5,4,3,1,2,0:T(8,128)(2,1)S(1)}, u32[]{:S(2)}, u32[]{:S(2)}) async-start(bf16[4,4,4,2,24,384]{5,4,3,1,2,0:T(8,128)(2,1)} %broadcast_in_dim.64), calls=%async_computation.2 | async-start | bytes 4718592 | tf_op jit(solution)/shard_map/all_to_all | solution.py:19
  94.9 3.1 %collective-permute-start.5 = (bf16[4,4,2,24,288]{4,3,2,1,0:T(8,128)(2,1)}, bf16[4,4,2,24,288]{4,3,2,1,0:T(8,128)(2,1)}, u32[]{:S(2)}, u32[]{:S(2)}) collective-permute-start(bf16[4,4,2,24,288]{4,3,2,1,0:T(8,128)(2,1)} %copy-done.1), channel_id=1, source_target_pairs={{0,64},{64,128},{128,192},{192,256},{256,320},{320,384},{384,448},... | collective-permute-start | bytes 1327112 | tf_op jit(solution)/shard_map/ppermute | solution.py:24
  98.0 3.4 %collective-permute-start = (bf16[4,4,2,24,288]{4,3,2,1,0:T(8,128)(2,1)}, bf16[4,4,2,24,288]{4,3,2,1,0:T(8,128)(2,1)S(1)}, u32[]{:S(2)}, u32[]{:S(2)}) collective-permute-start(bf16[4,4,2,24,288]{4,3,2,1,0:T(8,128)(2,1)} %copy-done.1), channel_id=1, source_target_pairs={{0,960},{64,0},{128,64},{192,128},{256,192},{320,256},{384,320},{4... | collective-permute-start | bytes 1327112 | tf_op jit(solution)/shard_map/ppermute | solution.py:24
  101.4 1.9 %fusion.40 = (bf16[2,4,2,24,288]{4,3,2,1,0:T(8,128)(2,1)}, bf16[2,4,2,24,288]{4,3,2,1,0:T(8,128)(2,1)}) fusion(bf16[4,4,2,24,288]{4,3,2,1,0:T(8,128)(2,1)} %copy-done.1), kind=kLoop, calls=%fused_computation.78 | loop fusion | bytes 884736 | tf_op jit(solution)/shard_map/slice | solution.py:120
  103.3 4.0 %collective-permute-start.6 = (bf16[2,4,2,24,288]{4,3,2,1,0:T(8,128)(2,1)}, bf16[2,4,2,24,288]{4,3,2,1,0:T(8,128)(2,1)S(1)}, u32[]{:S(2)}, u32[]{:S(2)}) collective-permute-start(bf16[2,4,2,24,288]{4,3,2,1,0:T(8,128)(2,1)} %get-tuple-element.24), channel_id=1, source_target_pairs={{0,896},{64,960},{128,0},{192,64},{256,128},{320,192},{384,256},{4... | collective-permute-start | bytes 663560 | tf_op jit(solution)/shard_map/ppermute | solution.py:24
  107.3 2.3 %collective-permute-start.7 = (bf16[2,4,2,24,288]{4,3,2,1,0:T(8,128)(2,1)}, bf16[2,4,2,24,288]{4,3,2,1,0:T(8,128)(2,1)}, u32[]{:S(2)}, u32[]{:S(2)}) collective-permute-start(bf16[2,4,2,24,288]{4,3,2,1,0:T(8,128)(2,1)} %get-tuple-element.25), channel_id=1, source_target_pairs={{0,128},{64,192},{128,256},{192,320},{256,384},{320,448},{384,512}... | collective-permute-start | bytes 663560 | tf_op jit(solution)/shard_map/ppermute | solution.py:24
  110.4 2.1 %copy-done.3 = bf16[4,4,2,4,24,672]{5,4,3,2,1,0:T(8,128)(2,1)} copy-done((bf16[4,4,2,4,24,672]{5,4,3,2,1,0:T(8,128)(2,1)}, bf16[4,4,2,4,24,672]{5,4,3,2,1,0:T(8,128)(2,1)S(1)}, u32[]{:S(2)}) %copy-start.3) | copy-done | bytes 4128792
  115.6 2.0 %copy_dynamic-update-slice_fusion.3 = bf16[4,4,2,4,24,672]{5,4,3,2,1,0:T(8,128)(2,1)} fusion(bf16[4,4,2,4,24,672]{5,4,3,2,1,0:T(8,128)(2,1)} %copy-done.3, s32[]{:T(128)S(6)} %select_n.249, bf16[4,4,2,24,288]{4,3,2,1,0:T(8,128)(2,1)} %collective-permute-done.5), kind=kLoop, calls=%fused_computation.34 | loop fusion | bytes 1179652 | tf_op jit(solution)/shard_map/dynamic_update_slice | solution.py:135
  117.6 2.0 %copy_dynamic-update-slice_fusion.2 = bf16[4,4,2,4,24,672]{5,4,3,2,1,0:T(8,128)(2,1)} fusion(bf16[4,4,2,4,24,672]{5,4,3,2,1,0:T(8,128)(2,1)} %copy_dynamic-update-slice_fusion.3, s32[]{:T(128)S(6)} %select_n.251, bf16[4,4,2,24,288]{4,3,2,1,0:T(8,128)(2,1)} %copy-done.7), kind=kLoop, calls=%fused_computation.33 | loop fusion | bytes 1179652 | tf_op jit(solution)/shard_map/dynamic_update_slice | solution.py:135
  119.6 6.7 %collective-permute-done.6 = bf16[2,4,2,24,288]{4,3,2,1,0:T(8,128)(2,1)S(1)} collective-permute-done((bf16[2,4,2,24,288]{4,3,2,1,0:T(8,128)(2,1)}, bf16[2,4,2,24,288]{4,3,2,1,0:T(8,128)(2,1)S(1)}, u32[]{:S(2)}, u32[]{:S(2)}) %collective-permute-start.6) | collective-permute-done | bytes 221216 | tf_op jit(solution)/shard_map/ppermute | solution.py:24
  128.1 2.9 %maximum_select_fusion = bf16[4,2,48,3200]{3,2,1,0:T(8,128)(2,1)S(1)} fusion(bf16[4,1,48,3200]{3,2,1,0:T(8,128)(2,1)} %bitcast.10, bf16[4,1,48,3200]{3,2,1,0:T(8,128)(2,1)} %bitcast.8, pred[]{:T(512)S(6)} %eq.80), kind=kLoop, calls=%fused_computation.3 | loop fusion | flops 3686400 | bytes 4915201 | tf_op jit(solution)/shard_map/jit(_where)/select_n | solution.py:125
  135.3 5.8 %fusion.7 = (bf16[384,672]{0,1:T(8,128)(2,1)}, f32[384,672]{0,1:T(8,128)S(1)}) fusion(bf16[384,672]{0,1:T(8,128)(2,1)S(1)} %copy-done.9, f32[384]{0:T(512)S(1)} %convert_reduce_fusion, bf16[3072,672]{1,0:T(8,128)(2,1)} %bitcast.86, bf16[384,3200]{1,0:T(8,128)(2,1)S(1)} %bitcast.90), kind=kOutput, calls=%fused_computation.16 | convolution fusion | flops 1587511296 | bytes 8554496 | tf_op jit(solution)/shard_map/dot_general | solution.py:139
  141.1 2.3 %convolution_convert_fusion = bf16[384,3072]{1,0:T(8,128)(2,1)S(1)} fusion(bf16[3072,672]{1,0:T(8,128)(2,1)S(1)} %bitcast.87, bf16[384,672]{0,1:T(8,128)(2,1)S(1)} %copy-done.9, f32[384,672]{0,1:T(8,128)S(1)} %get-tuple-element.29, bf16[384,672]{0,1:T(8,128)(2,1)S(1)} %copy-done.10, pred[384]{0:T(512)(128)(4,1)S(1)} %fusion.23), kind=kOutput, calls=%fused_computation | convolution fusion | flops 1589981184 | bytes 8552832 | tf_op jit(solution)/shard_map/dot_general | solution.py:157
  144.6 4.0 %collective-permute-start.11 = (bf16[2,2,48,1536]{3,2,0,1:T(8,128)(2,1)}, bf16[2,2,48,1536]{3,2,0,1:T(8,128)(2,1)S(1)}, u32[]{:S(2)}, u32[]{:S(2)}) collective-permute-start(bf16[2,2,48,1536]{3,2,0,1:T(8,128)(2,1)} %bitcast.85), channel_id=1, source_target_pairs={{0,1},{1,0},{2,3},{3,2},{4,5},{5,4},{6,7},{7,6},{8,9},{9,8},{10,11... | collective-permute-start | bytes 1769480 | tf_op jit(solution)/shard_map/ppermute | solution.py:161
  150.9 2.5 %collective-permute-start.12 = (bf16[2,48,1536]{2,1,0:T(8,128)(2,1)S(1)}, bf16[2,48,1536]{2,1,0:T(8,128)(2,1)S(1)}, u32[]{:S(2)}, u32[]{:S(2)}) collective-permute-start(bf16[2,48,1536]{2,1,0:T(8,128)(2,1)S(1)} %dynamic-slice_bitcast_fusion.2), channel_id=1, source_target_pairs={{0,2},{2,0},{4,6},{6,4},{1,3},{3,1},{5,7},{7,5},{8,10},{10,8},{12,... | collective-permute-start | bytes 884744 | tf_op jit(solution)/shard_map/ppermute | solution.py:163
  153.6 2.8 %collective-permute-start.15 = (bf16[2,48,1536]{2,1,0:T(8,128)(2,1)S(1)}, bf16[2,48,1536]{2,1,0:T(8,128)(2,1)S(1)}, u32[]{:S(2)}, u32[]{:S(2)}) collective-permute-start(bf16[2,48,1536]{2,1,0:T(8,128)(2,1)S(1)} %dynamic-slice_bitcast_fusion.1), channel_id=1, source_target_pairs={{0,2},{2,0},{4,6},{6,4},{1,3},{3,1},{5,7},{7,5},{8,10},{10,8},{12,... | collective-permute-start | bytes 884744 | tf_op jit(solution)/shard_map/ppermute | solution.py:163
  156.4 4.5 %collective-permute-done.12 = bf16[2,48,1536]{2,1,0:T(8,128)(2,1)S(1)} collective-permute-done((bf16[2,48,1536]{2,1,0:T(8,128)(2,1)S(1)}, bf16[2,48,1536]{2,1,0:T(8,128)(2,1)S(1)}, u32[]{:S(2)}, u32[]{:S(2)}) %collective-permute-start.12) | collective-permute-done | bytes 294944 | tf_op jit(solution)/shard_map/ppermute | solution.py:163
  160.9 3.7 %collective-permute-start.13 = (bf16[48,1536]{1,0:T(8,128)(2,1)S(1)}, bf16[48,1536]{1,0:T(8,128)(2,1)S(1)}, u32[]{:S(2)}, u32[]{:S(2)}) collective-permute-start(bf16[48,1536]{1,0:T(8,128)(2,1)S(1)} %dynamic-slice_bitcast_fusion.4), channel_id=1, source_target_pairs={{0,4},{2,6},{4,0},{6,2},{1,5},{3,7},{5,1},{7,3},{8,12},{10,14},{12... | collective-permute-start | bytes 442376 | tf_op jit(solution)/shard_map/ppermute | solution.py:165
  164.6 4.1 %collective-permute-done.15 = bf16[2,48,1536]{2,1,0:T(8,128)(2,1)S(1)} collective-permute-done((bf16[2,48,1536]{2,1,0:T(8,128)(2,1)S(1)}, bf16[2,48,1536]{2,1,0:T(8,128)(2,1)S(1)}, u32[]{:S(2)}, u32[]{:S(2)}) %collective-permute-start.15) | collective-permute-done | bytes 294944 | tf_op jit(solution)/shard_map/ppermute | solution.py:163
  168.8 2.1 %collective-permute-start.16 = (bf16[48,1536]{1,0:T(8,128)(2,1)S(1)}, bf16[48,1536]{1,0:T(8,128)(2,1)S(1)}, u32[]{:S(2)}, u32[]{:S(2)}) collective-permute-start(bf16[48,1536]{1,0:T(8,128)(2,1)S(1)} %dynamic-slice_bitcast_fusion.3), channel_id=1, source_target_pairs={{0,4},{2,6},{4,0},{6,2},{1,5},{3,7},{5,1},{7,3},{8,12},{10,14},{12... | collective-permute-start | bytes 442376 | tf_op jit(solution)/shard_map/ppermute | solution.py:165
  171.0 9.3 %collective-permute-done.16 = bf16[48,1536]{1,0:T(8,128)(2,1)S(1)} collective-permute-done((bf16[48,1536]{1,0:T(8,128)(2,1)S(1)}, bf16[48,1536]{1,0:T(8,128)(2,1)S(1)}, u32[]{:S(2)}, u32[]{:S(2)}) %collective-permute-start.16) | collective-permute-done | bytes 147488 | tf_op jit(solution)/shard_map/ppermute | solution.py:165
  (77 shorter events, 21.9 us)
Async XLA Ops:
  0.6 1.2 copy-start
  0.6 10.6 %copy-start.8 = (bf16[24,672]{1,0:T(8,128)(2,1)S(1)}, bf16[24,672]{1,0:T(8,128)(2,1)}, u32[]{:S(2)}) copy-start(bf16[24,672]{1,0:T(8,128)(2,1)} %param.11) | copy-start | bytes 96772
  3.0 30.0 %collective-permute-start.1 = (bf16[48,3200]{1,0:T(8,128)(2,1)S(1)}, bf16[48,3200]{1,0:T(8,128)(2,1)S(1)}, u32[]{:S(2)}, u32[]{:S(2)}) collective-permute-start(bf16[48,3200]{1,0:T(8,128)(2,1)S(1)} %get-tuple-element.27), channel_id=1, source_target_pairs={{0,2},{2,0},{4,6},{6,4},{1,3},{3,1},{5,7},{7,5},{8,10},{10,8},{12,... | collective-permute-start | bytes 921608 | tf_op jit(solution)/shard_map/ppermute | solution.py:107
  7.0 29.9 %collective-permute-start.2 = (bf16[48,3200]{1,0:T(8,128)(2,1)S(1)}, bf16[48,3200]{1,0:T(8,128)(2,1)S(1)}, u32[]{:S(2)}, u32[]{:S(2)}) collective-permute-start(bf16[48,3200]{1,0:T(8,128)(2,1)S(1)} %get-tuple-element.27), channel_id=1, source_target_pairs={{0,4},{2,6},{4,0},{6,2},{1,5},{3,7},{5,1},{7,3},{8,12},{10,14},{12... | collective-permute-start | bytes 921608 | tf_op jit(solution)/shard_map/ppermute | solution.py:108
  12.0 45.3 %all-to-all-start = ((bf16[8,24,672]{2,1,0:T(8,128)(2,1)}), bf16[8,24,672]{2,1,0:T(8,128)(2,1)S(1)}, u32[]{:S(2)}, u32[]{:S(2)}) async-start(bf16[8,24,672]{2,1,0:T(8,128)(2,1)} %broadcast_in_dim.56), calls=%async_computation | async-start | bytes 589824 | tf_op jit(solution)/shard_map/all_to_all | solution.py:19
  33.0 24.1 %collective-permute-start.3 = (bf16[48,3200]{1,0:T(8,128)(2,1)S(1)}, bf16[48,3200]{1,0:T(8,128)(2,1)S(1)}, u32[]{:S(2)}, u32[]{:S(2)}) collective-permute-start(bf16[48,3200]{1,0:T(8,128)(2,1)S(1)} %collective-permute-done.1), channel_id=1, source_target_pairs={{0,4},{2,6},{4,0},{6,2},{1,5},{3,7},{5,1},{7,3},{8,12},{10,14},{12... | collective-permute-start | bytes 921608 | tf_op jit(solution)/shard_map/ppermute | solution.py:112
  57.3 22.2 %collective-permute-start.10 = (bf16[4,2,24,384]{3,2,1,0:T(8,128)(2,1)S(1)}, bf16[4,2,24,384]{3,2,1,0:T(8,128)(2,1)S(1)}, u32[]{:S(2)}, u32[]{:S(2)}) collective-permute-start(bf16[4,2,24,384]{3,2,1,0:T(8,128)(2,1)S(1)} %slice.78), channel_id=1, source_target_pairs={{0,64},{64,128},{128,192},{192,256},{256,320},{320,384},{384,448},... | collective-permute-start | bytes 442376 | tf_op jit(solution)/shard_map/ppermute | solution.py:24
  59.9 19.5 %collective-permute-start.8 = (bf16[4,2,24,384]{3,2,1,0:T(8,128)(2,1)S(1)}, bf16[4,2,24,384]{3,2,1,0:T(8,128)(2,1)S(1)}, u32[]{:S(2)}, u32[]{:S(2)}) collective-permute-start(bf16[4,2,24,384]{3,2,1,0:T(8,128)(2,1)S(1)} %slice.78), channel_id=1, source_target_pairs={{0,960},{64,0},{128,64},{192,128},{256,192},{320,256},{384,320},{4... | collective-permute-start | bytes 442376 | tf_op jit(solution)/shard_map/ppermute | solution.py:24
  66.3 13.2 %collective-permute-start.9 = (bf16[4,2,24,384]{3,2,1,0:T(8,128)(2,1)S(1)}, bf16[4,2,24,384]{3,2,1,0:T(8,128)(2,1)S(1)}, u32[]{:S(2)}, u32[]{:S(2)}) collective-permute-start(bf16[4,2,24,384]{3,2,1,0:T(8,128)(2,1)S(1)} %slice.78), channel_id=1, source_target_pairs={{0,896},{64,960},{128,0},{192,64},{256,128},{320,192},{384,256},{4... | collective-permute-start | bytes 442376 | tf_op jit(solution)/shard_map/ppermute | solution.py:24
  70.7 57.4 %collective-permute-start.4 = (bf16[4,48,3200]{2,1,0:T(8,128)(2,1)}, bf16[4,48,3200]{2,1,0:T(8,128)(2,1)}, u32[]{:S(2)}, u32[]{:S(2)}) collective-permute-start(bf16[4,48,3200]{2,1,0:T(8,128)(2,1)} %bitcast.9), channel_id=1, source_target_pairs={{0,1},{1,0},{2,3},{3,2},{4,5},{5,4},{6,7},{7,6},{8,9},{9,8},{10,11... | collective-permute-start | bytes 3686408 | tf_op jit(solution)/shard_map/ppermute | solution.py:118
  75.5 14.0 %all-to-all-start.1 = ((bf16[4,4,2,24,288]{4,3,2,1,0:T(8,128)(2,1)}), bf16[4,4,2,24,288]{4,3,2,1,0:T(8,128)(2,1)S(1)}, u32[]{:S(2)}, u32[]{:S(2)}) async-start(bf16[4,4,2,24,288]{4,3,2,1,0:T(8,128)(2,1)} %broadcast_in_dim.57), calls=%async_computation.1 | async-start | bytes 1179648 | tf_op jit(solution)/shard_map/all_to_all | solution.py:19
  89.5 1.8 copy-start.1
  91.3 41.4 %all-to-all-start.2 = ((bf16[4,4,4,2,24,384]{5,4,3,1,2,0:T(8,128)(2,1)}), bf16[4,4,4,2,24,384]{5,4,3,1,2,0:T(8,128)(2,1)S(1)}, u32[]{:S(2)}, u32[]{:S(2)}) async-start(bf16[4,4,4,2,24,384]{5,4,3,1,2,0:T(8,128)(2,1)} %broadcast_in_dim.64), calls=%async_computation.2 | async-start | bytes 4718592 | tf_op jit(solution)/shard_map/all_to_all | solution.py:19
  94.9 17.6 %collective-permute-start.5 = (bf16[4,4,2,24,288]{4,3,2,1,0:T(8,128)(2,1)}, bf16[4,4,2,24,288]{4,3,2,1,0:T(8,128)(2,1)}, u32[]{:S(2)}, u32[]{:S(2)}) collective-permute-start(bf16[4,4,2,24,288]{4,3,2,1,0:T(8,128)(2,1)} %copy-done.1), channel_id=1, source_target_pairs={{0,64},{64,128},{128,192},{192,256},{256,320},{320,384},{384,448},... | collective-permute-start | bytes 1327112 | tf_op jit(solution)/shard_map/ppermute | solution.py:24
  98.0 15.6 %collective-permute-start = (bf16[4,4,2,24,288]{4,3,2,1,0:T(8,128)(2,1)}, bf16[4,4,2,24,288]{4,3,2,1,0:T(8,128)(2,1)S(1)}, u32[]{:S(2)}, u32[]{:S(2)}) collective-permute-start(bf16[4,4,2,24,288]{4,3,2,1,0:T(8,128)(2,1)} %copy-done.1), channel_id=1, source_target_pairs={{0,960},{64,0},{128,64},{192,128},{256,192},{320,256},{384,320},{4... | collective-permute-start | bytes 1327112 | tf_op jit(solution)/shard_map/ppermute | solution.py:24
  103.3 22.9 %collective-permute-start.6 = (bf16[2,4,2,24,288]{4,3,2,1,0:T(8,128)(2,1)}, bf16[2,4,2,24,288]{4,3,2,1,0:T(8,128)(2,1)S(1)}, u32[]{:S(2)}, u32[]{:S(2)}) collective-permute-start(bf16[2,4,2,24,288]{4,3,2,1,0:T(8,128)(2,1)} %get-tuple-element.24), channel_id=1, source_target_pairs={{0,896},{64,960},{128,0},{192,64},{256,128},{320,192},{384,256},{4... | collective-permute-start | bytes 663560 | tf_op jit(solution)/shard_map/ppermute | solution.py:24
  107.3 2.9 %copy-start.2 = (bf16[4,4,2,24,288]{4,3,2,1,0:T(8,128)(2,1)S(1)}, bf16[4,4,2,24,288]{4,3,2,1,0:T(8,128)(2,1)}, u32[]{:S(2)}) copy-start(bf16[4,4,2,24,288]{4,3,2,1,0:T(8,128)(2,1)} %copy-done.1) | copy-start | bytes 1327108
  107.3 18.9 %collective-permute-start.7 = (bf16[2,4,2,24,288]{4,3,2,1,0:T(8,128)(2,1)}, bf16[2,4,2,24,288]{4,3,2,1,0:T(8,128)(2,1)}, u32[]{:S(2)}, u32[]{:S(2)}) collective-permute-start(bf16[2,4,2,24,288]{4,3,2,1,0:T(8,128)(2,1)} %get-tuple-element.25), channel_id=1, source_target_pairs={{0,128},{64,192},{128,256},{192,320},{256,384},{320,448},{384,512}... | collective-permute-start | bytes 663560 | tf_op jit(solution)/shard_map/ppermute | solution.py:24
  110.4 2.1 %copy-start.3 = (bf16[4,4,2,4,24,672]{5,4,3,2,1,0:T(8,128)(2,1)}, bf16[4,4,2,4,24,672]{5,4,3,2,1,0:T(8,128)(2,1)S(1)}, u32[]{:S(2)}) copy-start(bf16[4,4,2,4,24,672]{5,4,3,2,1,0:T(8,128)(2,1)S(1)} %copy_dynamic-update-slice_fusion.4) | copy-start | bytes 12386308
  113.6 0.8 copy-start.7
  131.0 1.5 copy-start.5
  132.6 2.5 %copy-start.6 = (bf16[4,2,48,3200]{3,2,1,0:T(8,128)(2,1)S(1)}, bf16[4,2,48,3200]{3,2,1,0:T(8,128)(2,1)}, u32[]{:S(2)}) copy-start(bf16[4,2,48,3200]{3,2,1,0:T(8,128)(2,1)} %copy-done.5) | copy-start | bytes 7372804
  132.7 2.6 %copy-start.9 = (bf16[384,672]{0,1:T(8,128)(2,1)S(1)}, bf16[384,672]{0,1:T(8,128)(2,1)}, u32[]{:S(2)}) copy-start(bf16[384,672]{0,1:T(8,128)(2,1)} %param.12) | copy-start | bytes 1548292
  135.3 5.8 %copy-start.4 = (bf16[4,4,2,4,24,672]{5,4,3,2,1,0:T(8,128)(2,1)S(1)}, bf16[4,4,2,4,24,672]{5,4,3,2,1,0:T(8,128)(2,1)}, u32[]{:S(2)}) copy-start(bf16[4,4,2,4,24,672]{5,4,3,2,1,0:T(8,128)(2,1)} %copy_dynamic-update-slice_fusion) | copy-start | bytes 12386308
  135.3 5.8 %copy-start.10 = (bf16[384,672]{0,1:T(8,128)(2,1)S(1)}, bf16[384,672]{0,1:T(8,128)(2,1)}, u32[]{:S(2)}) copy-start(bf16[384,672]{0,1:T(8,128)(2,1)} %param.13) | copy-start | bytes 1548292
  144.6 6.0 %collective-permute-start.11 = (bf16[2,2,48,1536]{3,2,0,1:T(8,128)(2,1)}, bf16[2,2,48,1536]{3,2,0,1:T(8,128)(2,1)S(1)}, u32[]{:S(2)}, u32[]{:S(2)}) collective-permute-start(bf16[2,2,48,1536]{3,2,0,1:T(8,128)(2,1)} %bitcast.85), channel_id=1, source_target_pairs={{0,1},{1,0},{2,3},{3,2},{4,5},{5,4},{6,7},{7,6},{8,9},{9,8},{10,11... | collective-permute-start | bytes 1769480 | tf_op jit(solution)/shard_map/ppermute | solution.py:161
  148.7 4.7 %collective-permute-start.14 = (bf16[2,2,48,1536]{3,2,1,0:T(8,128)(2,1)S(1)}, bf16[2,2,48,1536]{3,2,1,0:T(8,128)(2,1)S(1)}, u32[]{:S(2)}, u32[]{:S(2)}) collective-permute-start(bf16[2,2,48,1536]{3,2,1,0:T(8,128)(2,1)S(1)} %dynamic-slice_bitcast_fusion), channel_id=1, source_target_pairs={{0,1},{1,0},{2,3},{3,2},{4,5},{5,4},{6,7},{7,6},{8,9},{9,8},{10,11... | collective-permute-start | bytes 1769480 | tf_op jit(solution)/shard_map/ppermute | solution.py:161
  150.9 10.0 %collective-permute-start.12 = (bf16[2,48,1536]{2,1,0:T(8,128)(2,1)S(1)}, bf16[2,48,1536]{2,1,0:T(8,128)(2,1)S(1)}, u32[]{:S(2)}, u32[]{:S(2)}) collective-permute-start(bf16[2,48,1536]{2,1,0:T(8,128)(2,1)S(1)} %dynamic-slice_bitcast_fusion.2), channel_id=1, source_target_pairs={{0,2},{2,0},{4,6},{6,4},{1,3},{3,1},{5,7},{7,5},{8,10},{10,8},{12,... | collective-permute-start | bytes 884744 | tf_op jit(solution)/shard_map/ppermute | solution.py:163
  153.6 15.1 %collective-permute-start.15 = (bf16[2,48,1536]{2,1,0:T(8,128)(2,1)S(1)}, bf16[2,48,1536]{2,1,0:T(8,128)(2,1)S(1)}, u32[]{:S(2)}, u32[]{:S(2)}) collective-permute-start(bf16[2,48,1536]{2,1,0:T(8,128)(2,1)S(1)} %dynamic-slice_bitcast_fusion.1), channel_id=1, source_target_pairs={{0,2},{2,0},{4,6},{6,4},{1,3},{3,1},{5,7},{7,5},{8,10},{10,8},{12,... | collective-permute-start | bytes 884744 | tf_op jit(solution)/shard_map/ppermute | solution.py:163
  160.9 10.0 %collective-permute-start.13 = (bf16[48,1536]{1,0:T(8,128)(2,1)S(1)}, bf16[48,1536]{1,0:T(8,128)(2,1)S(1)}, u32[]{:S(2)}, u32[]{:S(2)}) collective-permute-start(bf16[48,1536]{1,0:T(8,128)(2,1)S(1)} %dynamic-slice_bitcast_fusion.4), channel_id=1, source_target_pairs={{0,4},{2,6},{4,0},{6,2},{1,5},{3,7},{5,1},{7,3},{8,12},{10,14},{12... | collective-permute-start | bytes 442376 | tf_op jit(solution)/shard_map/ppermute | solution.py:165
  168.8 11.4 %collective-permute-start.16 = (bf16[48,1536]{1,0:T(8,128)(2,1)S(1)}, bf16[48,1536]{1,0:T(8,128)(2,1)S(1)}, u32[]{:S(2)}, u32[]{:S(2)}) collective-permute-start(bf16[48,1536]{1,0:T(8,128)(2,1)S(1)} %dynamic-slice_bitcast_fusion.3), channel_id=1, source_target_pairs={{0,4},{2,6},{4,0},{6,2},{1,5},{3,7},{5,1},{7,3},{8,12},{10,14},{12... | collective-permute-start | bytes 442376 | tf_op jit(solution)/shard_map/ppermute | solution.py:165

commit v4 on v2

--- a/solution.py
+++ b/solution.py
@@ -26,6 +26,10 @@
 
 def in_order(own, other, which):
     return jnp.where(which == 0, jnp.stack([own, other]), jnp.stack([other, own]))
+
+
+def nothing(array):
+    return (array[(0,) * array.ndim] * 0).astype(jnp.int32)
 
 
 def by_residue(own, below, above, far):
@@ -58,21 +62,23 @@
     sent = jnp.concatenate([own_rows, own_scale], axis=1)
     core = lax.axis_index("core")
 
+    yl = lax.axis_index("yl")
+    by_one, by_two = [(i, i ^ 1) for i in range(4)], [(i, i ^ 2) for i in range(4)]
+    near = lax.ppermute(sent, "yl", by_one)
+
     far = everyone(weight, ("za", "yh")).reshape(4, 2, depth, width)
-    far, sent = lax.optimization_barrier((far, sent))
-
+    far, near = lax.optimization_barrier((far, near))
     one, two = far[..., :cut], far[..., cut:]
-    one_z = by_residue(one, along_z(one, 1), along_z(one, -1), along_z(one, -2))
+    beside = (along_z(one, 1), along_z(one, -1), along_z(one, -2))
+    two_rows = in_order(sent, near, (yl + nothing(beside[2])) % 2)
+    opposite = lax.ppermute(two_rows, "yl", by_two)
+    one_x = everyone(by_residue(one, *beside), ("x",))
     two_x = everyone(two, ("x",))
     zb = lax.axis_index("zb")
+    below, above = along_z(two_x, 1), along_z(two_x, -1)
     two_far = jnp.concatenate([along_z(two_x[:2], -2), along_z(two_x[2:], 2)])
-    one_x = everyone(one_z, ("x",))
 
-    near = lax.ppermute(sent, "yl", [(i, i ^ 1) for i in range(4)])
-    yl = lax.axis_index("yl")
-    two_rows = in_order(sent, near, yl % 2)
-    other_rows = lax.ppermute(two_rows, "yl", [(i, i ^ 2) for i in range(4)])
-    four_rows = in_order(two_rows, other_rows, yl // 2)
+    four_rows = in_order(two_rows, opposite, yl // 2)
     four_rows = four_rows.reshape(n_yl, slot_count, model + 128)
     theirs = lax.ppermute(four_rows, "core", [(0, 1), (1, 0)])
     got = jnp.where(core == 0, jnp.stack([four_rows, theirs], 1), jnp.stack([theirs, four_rows], 1))
@@ -82,11 +88,17 @@
 
     whole = jnp.zeros((4, 4, 2, 4, depth, width), jnp.bfloat16)
     zero = jnp.zeros((), jnp.int32)
-    for piece, by in ((two_x, 0), (along_z(two_x, 1), -1), (along_z(two_x, -1), 1), (two_far, 2)):
+
+    def placed(whole, piece, by, after):
         piece = piece.transpose(1, 2, 0, 3, 4)[:, None]
-        at = (zero, (zb + by + 4) % 4, zero, zero, zero, zero + cut)
-        whole = lax.dynamic_update_slice(whole, piece, at)
+        at = (zero, (zb + by + after) % 4, zero, zero, zero, zero + cut)
+        return lax.dynamic_update_slice(whole, piece, at)
+
+    whole = placed(whole, two_x, 0, 4)
+    whole = placed(whole, below, -1, 4)
+    whole = placed(whole, above, 1, 4)
     whole = whole.at[..., :cut].set(one_x.transpose(2, 1, 3, 0, 4, 5))
+    whole = placed(whole, two_far, 2, 4)
     gathered = whole.reshape(model, width)
 
     product = jnp.dot(rows, gathered, preferred_element_type=jnp.float32)
@@ -101,14 +113,25 @@
         0.0,
     ).astype(jnp.bfloat16)
 
+    def pick(array, axis, which):
+        return lax.dynamic_index_in_dim(array, which, axis, keepdims=False)
+
+    def add(one, other):
+        return (one.astype(jnp.float32) + other.astype(jnp.float32)).astype(jnp.bfloat16)
+
     partial = jnp.dot(dgate, gathered.T, preferred_element_type=jnp.float32).astype(jnp.bfloat16)
-    partial = partial.reshape(n_yl, n_core, slot_count, model)
-    given = lax.dynamic_index_in_dim(partial, 1 - core, 1, keepdims=False)
-    kept = lax.dynamic_index_in_dim(partial, core, 1, keepdims=False)
-    swapped = lax.ppermute(given, "core", [(0, 1), (1, 0)])
-    pair = (kept.astype(jnp.float32) + swapped.astype(jnp.float32)).astype(jnp.bfloat16)
-    parts = lax.all_to_all(pair, "yl", 0, 0)
-    slot_grad = jnp.sum(parts.astype(jnp.float32), axis=0).astype(jnp.bfloat16)
+    partial = partial.reshape(2, 2, n_core, slot_count, model)
+
+    def returned(part):
+        swapped = lax.ppermute(pick(part, 2, 1 - core), "core", [(0, 1), (1, 0)])
+        pair = add(pick(part, 2, core), swapped)
+        near = lax.ppermute(pick(pair, 1, 1 - yl % 2), "yl", by_one)
+        four = add(pick(pair, 1, yl % 2), near)
+        far = lax.ppermute(pick(four, 0, 1 - yl // 2), "yl", by_two)
+        return add(pick(four, 0, yl // 2), far)
+
+    half = model // 2
+    slot_grad = jnp.concatenate([returned(partial[..., :half]), returned(partial[..., half:])], axis=1)
     input_grad = jnp.einsum(
         "st,sd->td", select, slot_grad, preferred_element_type=jnp.float32
     ).astype(jnp.bfloat16)

time: 182 us -> 174 us (0.956)
  blocking collectives: 31 us -> 0 us
  waiting for transfers between devices: 33 us -> 44.3 us
  starting transfers between devices: 76.2 us -> 85.6 us
    all_to_all x1 -> x0, blocking collectives: 31 us -> none  [body(): parts = lax.all_to_all(pair, 'yl', 0, 0)]
    ppermute x3 -> x8, waiting for transfers between devices: 17.1 us -> 36.2 us  [the longest x1 13.5 us: body(): near = lax.ppermute(sent, 'yl', by_one)]
    all_to_all x3, waiting for transfers between devices: 14.8 us -> 2.74 us  [everyone(): lax.all_to_all(jnp.broadcast_to(part[None], (count,) + part.shape), axes,...]
    ppermute x3 -> x8, starting transfers between devices: 10.2 us -> 20.7 us  [the longest x2 6.33 us: returned(): swapped = lax.ppermute(pick(part, 2, 1 - core), 'core', [(0, 1), (1, 0)])]
    ppermute x7, waiting for transfers between devices: 1.15 us -> 5.44 us  [along_z(): return lax.ppermute(part, ('za', 'zb'), shifted(za, zb, by))]
  transfers between devices with their start and end apart: 14 -> 19, of which waited for: 5 -> 7; matrix products, arithmetic and copies ran while one was open for 11% -> 13% of each run, Pallas kernels for 0% -> 0%
where the time goes in v4:
time: 174 us; the launch traced here: 173 us
  starting transfers between devices  85.6 us (49%)
  waiting for transfers between devices  44.3 us (25%)
  local copies, waits for them, and re-layouts  15.4 us (9%)
  matrix products  12.8 us (7%)
  other arithmetic  12.7 us (7%)
  between operations  1.9 us (1%)
    all_to_all x3, starting transfers between devices, everyone(): lax.all_to_all(jnp.broadcast_to(part[None], (count,) + part.shape), axes,...  32.2 us
    ppermute x7, starting transfers between devices, along_z(): return lax.ppermute(part, ('za', 'zb'), shifted(za, zb, by))  30 us
    ppermute x1, waiting for transfers between devices, body(): near = lax.ppermute(sent, 'yl', by_one)  13.5 us
    ppermute x2, waiting for transfers between devices, returned(): near = lax.ppermute(pick(pair, 1, 1 - yl % 2), 'yl', by_one)  9.82 us
    ppermute x2, waiting for transfers between devices, returned(): far = lax.ppermute(pick(four, 0, 1 - yl // 2), 'yl', by_two)  7.59 us
    ppermute x2, starting transfers between devices, returned(): swapped = lax.ppermute(pick(part, 2, 1 - core), 'core', [(0, 1), (1, 0)])  6.33 us
    dot_general x1, matrix products, body(): product = jnp.dot(rows, gathered, preferred_element_type=jnp.float32)  5.74 us
    ppermute x7, waiting for transfers between devices, along_z(): return lax.ppermute(part, ('za', 'zb'), shifted(za, zb, by))  5.44 us
  transfers between devices with their start and end apart: 19, of which 7 were waited for; matrix products, arithmetic and copies ran while one was open for 13% of the time, Pallas kernels for 0%

profile of v4, /device:TPU:1, one launch (start us, length us, event | category | flops | bytes accessed | tf_op | source)
XLA Modules:
  0.0 172.8 jit_solution(12845904271406125562)
XLA Ops:
  2.2 24.5 %all-to-all-start = ((bf16[8,24,672]{2,1,0:T(8,128)(2,1)}), bf16[8,24,672]{2,1,0:T(8,128)(2,1)S(1)}, u32[]{:S(2)}, u32[]{:S(2)}) async-start(bf16[8,24,672]{2,1,0:T(8,128)(2,1)} %broadcast_in_dim.56), calls=%async_computation | async-start | bytes 589824 | tf_op jit(solution)/shard_map/all_to_all | solution.py:19
  29.1 2.3 %collective-permute-start = (bf16[48,3200]{1,0:T(8,128)(2,1)S(1)}, bf16[48,3200]{1,0:T(8,128)(2,1)S(1)}, u32[]{:S(2)}, u32[]{:S(2)}) collective-permute-start(bf16[48,3200]{1,0:T(8,128)(2,1)S(1)} %get-tuple-element.30), channel_id=1, source_target_pairs={{0,2},{2,0},{4,6},{6,4},{1,3},{3,1},{5,7},{7,5},{8,10},{10,8},{12,... | collective-permute-start | bytes 921608 | tf_op jit(solution)/shard_map/ppermute | solution.py:67
  31.4 13.5 %collective-permute-done = bf16[48,3200]{1,0:T(8,128)(2,1)S(1)} collective-permute-done((bf16[48,3200]{1,0:T(8,128)(2,1)S(1)}, bf16[48,3200]{1,0:T(8,128)(2,1)S(1)}, u32[]{:S(2)}, u32[]{:S(2)}) %collective-permute-start) | collective-permute-done | bytes 307232 | tf_op jit(solution)/shard_map/ppermute | solution.py:67
  44.9 10.1 %collective-permute-start.1 = (bf16[4,2,24,384]{3,2,1,0:T(8,128)(2,1)S(1)}, bf16[4,2,24,384]{3,2,1,0:T(8,128)(2,1)S(1)}, u32[]{:S(2)}, u32[]{:S(2)}) collective-permute-start(bf16[4,2,24,384]{3,2,1,0:T(8,128)(2,1)S(1)} %slice.64), channel_id=1, source_target_pairs={{0,896},{64,960},{128,0},{192,64},{256,128},{320,192},{384,256},{4... | collective-permute-start | bytes 442376 | tf_op jit(solution)/shard_map/ppermute | solution.py:24
  54.9 4.2 %collective-permute-start.6 = (bf16[4,2,24,384]{3,2,1,0:T(8,128)(2,1)S(1)}, bf16[4,2,24,384]{3,2,1,0:T(8,128)(2,1)}, u32[]{:S(2)}, u32[]{:S(2)}) collective-permute-start(bf16[4,2,24,384]{3,2,1,0:T(8,128)(2,1)S(1)} %slice.64), channel_id=1, source_target_pairs={{0,960},{64,0},{128,64},{192,128},{256,192},{320,256},{384,320},{4... | collective-permute-start | bytes 442376 | tf_op jit(solution)/shard_map/ppermute | solution.py:24
  59.1 3.1 %collective-permute-start.7 = (bf16[4,2,24,384]{3,2,1,0:T(8,128)(2,1)S(1)}, bf16[4,2,24,384]{3,2,1,0:T(8,128)(2,1)}, u32[]{:S(2)}, u32[]{:S(2)}) collective-permute-start(bf16[4,2,24,384]{3,2,1,0:T(8,128)(2,1)S(1)} %slice.64), channel_id=1, source_target_pairs={{0,64},{64,128},{128,192},{192,256},{256,320},{320,384},{384,448},... | collective-permute-start | bytes 442376 | tf_op jit(solution)/shard_map/ppermute | solution.py:24
  63.3 4.0 %all-to-all-start.1 = ((bf16[4,4,2,24,288]{4,3,2,1,0:T(8,128)(2,1)}), bf16[4,4,2,24,288]{4,3,2,1,0:T(8,128)(2,1)S(1)}, u32[]{:S(2)}, u32[]{:S(2)}) async-start(bf16[4,4,2,24,288]{4,3,2,1,0:T(8,128)(2,1)} %broadcast_in_dim.59), calls=%async_computation.1 | async-start | bytes 1179648 | tf_op jit(solution)/shard_map/all_to_all | solution.py:19
  70.8 2.4 %collective-permute-start.2 = (bf16[2,48,3200]{2,1,0:T(8,128)(2,1)}, bf16[2,48,3200]{2,1,0:T(8,128)(2,1)}, u32[]{:S(2)}, u32[]{:S(2)}) collective-permute-start(bf16[2,48,3200]{2,1,0:T(8,128)(2,1)} %maximum_select_fusion.3), channel_id=1, source_target_pairs={{0,4},{2,6},{4,0},{6,2},{1,5},{3,7},{5,1},{7,3},{8,12},{10,14},{12... | collective-permute-start | bytes 1843208 | tf_op jit(solution)/shard_map/ppermute | solution.py:74
  73.2 2.7 %all-to-all-done.1 = bf16[4,4,2,24,288]{4,3,2,1,0:T(8,128)(2,1)S(1)} async-done(((bf16[4,4,2,24,288]{4,3,2,1,0:T(8,128)(2,1)}), bf16[4,4,2,24,288]{4,3,2,1,0:T(8,128)(2,1)S(1)}, u32[]{:S(2)}, u32[]{:S(2)}) %all-to-all-start.1) | async-done | bytes 442400 | tf_op jit(solution)/shard_map/all_to_all | solution.py:19
  77.7 3.6 %all-to-all-start.2 = ((bf16[4,4,4,2,24,384]{5,4,3,1,2,0:T(8,128)(2,1)}), bf16[4,4,4,2,24,384]{5,4,3,1,2,0:T(8,128)(2,1)S(1)}, u32[]{:S(2)}, u32[]{:S(2)}) async-start(bf16[4,4,4,2,24,384]{5,4,3,1,2,0:T(8,128)(2,1)} %broadcast_in_dim.63), calls=%async_computation.2 | async-start | bytes 4718592 | tf_op jit(solution)/shard_map/all_to_all | solution.py:19
  82.5 1.9 %fusion.41 = (bf16[2,4,2,24,288]{4,3,2,1,0:T(8,128)(2,1)}, bf16[2,4,2,24,288]{4,3,2,1,0:T(8,128)(2,1)}) fusion(bf16[4,4,2,24,288]{4,3,2,1,0:T(8,128)(2,1)} %copy-done.1), kind=kLoop, calls=%fused_computation.79 | loop fusion | bytes 884736 | tf_op jit(solution)/shard_map/slice | solution.py:79
  84.5 2.2 %collective-permute-start.8 = (bf16[2,4,2,24,288]{4,3,2,1,0:T(8,128)(2,1)}, bf16[2,4,2,24,288]{4,3,2,1,0:T(8,128)(2,1)S(1)}, u32[]{:S(2)}, u32[]{:S(2)}) collective-permute-start(bf16[2,4,2,24,288]{4,3,2,1,0:T(8,128)(2,1)} %get-tuple-element.26), channel_id=1, source_target_pairs={{0,896},{64,960},{128,0},{192,64},{256,128},{320,192},{384,256},{4... | collective-permute-start | bytes 663560 | tf_op jit(solution)/shard_map/ppermute | solution.py:24
  86.7 4.0 %collective-permute-start.9 = (bf16[2,4,2,24,288]{4,3,2,1,0:T(8,128)(2,1)}, bf16[2,4,2,24,288]{4,3,2,1,0:T(8,128)(2,1)}, u32[]{:S(2)}, u32[]{:S(2)}) collective-permute-start(bf16[2,4,2,24,288]{4,3,2,1,0:T(8,128)(2,1)} %get-tuple-element.27), channel_id=1, source_target_pairs={{0,128},{64,192},{128,256},{192,320},{256,384},{320,448},{384,512}... | collective-permute-start | bytes 663560 | tf_op jit(solution)/shard_map/ppermute | solution.py:24
  90.7 3.1 %collective-permute-start.4 = (bf16[4,4,2,24,288]{4,3,2,1,0:T(8,128)(2,1)S(1)}, bf16[4,4,2,24,288]{4,3,2,1,0:T(8,128)(2,1)S(1)}, u32[]{:S(2)}, u32[]{:S(2)}) collective-permute-start(bf16[4,4,2,24,288]{4,3,2,1,0:T(8,128)(2,1)S(1)} %copy-done.2), channel_id=1, source_target_pairs={{0,64},{64,128},{128,192},{192,256},{256,320},{320,384},{384,448},... | collective-permute-start | bytes 1327112 | tf_op jit(solution)/shard_map/ppermute | solution.py:24
  93.7 3.5 %collective-permute-start.5 = (bf16[4,4,2,24,288]{4,3,2,1,0:T(8,128)(2,1)S(1)}, bf16[4,4,2,24,288]{4,3,2,1,0:T(8,128)(2,1)S(1)}, u32[]{:S(2)}, u32[]{:S(2)}) collective-permute-start(bf16[4,4,2,24,288]{4,3,2,1,0:T(8,128)(2,1)S(1)} %copy-done.2), channel_id=1, source_target_pairs={{0,960},{64,0},{128,64},{192,128},{256,192},{320,256},{384,320},{4... | collective-permute-start | bytes 1327112 | tf_op jit(solution)/shard_map/ppermute | solution.py:24
  97.2 5.3 %collective-permute-done.2 = bf16[2,48,3200]{2,1,0:T(8,128)(2,1)} collective-permute-done((bf16[2,48,3200]{2,1,0:T(8,128)(2,1)}, bf16[2,48,3200]{2,1,0:T(8,128)(2,1)}, u32[]{:S(2)}, u32[]{:S(2)}) %collective-permute-start.2) | collective-permute-done | bytes 614432 | tf_op jit(solution)/shard_map/ppermute | solution.py:74
  102.5 2.6 %maximum_select_fusion.1 = bf16[2,2,48,3200]{3,2,1,0:T(8,128)(2,1)} fusion(bf16[1,2,48,3200]{3,2,1,0:T(8,128)(2,1)} %bitcast.7, bf16[1,2,48,3200]{3,2,1,0:T(8,128)(2,1)S(1)} %maximum_select_fusion.2, pred[]{:T(512)S(6)} %eq.79), kind=kLoop, calls=%fused_computation.10 | loop fusion | flops 1843200 | bytes 2457601 | tf_op jit(solution)/shard_map/jit(_where)/select_n | solution.py:28
  105.1 2.7 %collective-permute-start.3 = (bf16[4,48,3200]{2,1,0:T(8,128)(2,1)}, bf16[4,48,3200]{2,1,0:T(8,128)(2,1)}, u32[]{:S(2)}, u32[]{:S(2)}) collective-permute-start(bf16[4,48,3200]{2,1,0:T(8,128)(2,1)} %bitcast.10), channel_id=1, source_target_pairs={{0,1},{1,0},{2,3},{3,2},{4,5},{5,4},{6,7},{7,6},{8,9},{9,8},{10,11... | collective-permute-start | bytes 3686408 | tf_op jit(solution)/shard_map/ppermute | solution.py:83
  107.8 2.7 %broadcast_in_dim.58 = bf16[4,4,2,4,24,672]{5,4,3,2,1,0:T(8,128)(2,1)} broadcast(bf16[]{:T(256)} %constant.171.clone.1), dimensions={} | broadcast | bytes 4128770 | tf_op jit(solution)/shard_map/broadcast_in_dim | solution.py:89
  111.4 5.4 %collective-permute-done.4 = bf16[4,4,2,24,288]{4,3,2,1,0:T(8,128)(2,1)S(1)} collective-permute-done((bf16[4,4,2,24,288]{4,3,2,1,0:T(8,128)(2,1)S(1)}, bf16[4,4,2,24,288]{4,3,2,1,0:T(8,128)(2,1)S(1)}, u32[]{:S(2)}, u32[]{:S(2)}) %collective-permute-start.4) | collective-permute-done | bytes 442400 | tf_op jit(solution)/shard_map/ppermute | solution.py:24
  122.4 3.0 %maximum_select_fusion = bf16[4,2,48,3200]{3,2,1,0:T(8,128)(2,1)S(1)} fusion(bf16[4,1,48,3200]{3,2,1,0:T(8,128)(2,1)} %bitcast.11, bf16[4,1,48,3200]{3,2,1,0:T(8,128)(2,1)} %bitcast.9, pred[]{:T(512)S(6)} %eq.78), kind=kLoop, calls=%fused_computation.3 | loop fusion | flops 3686400 | bytes 4915201 | tf_op jit(solution)/shard_map/jit(_where)/select_n | solution.py:84
  125.6 5.7 %fusion.7 = (bf16[384,672]{0,1:T(8,128)(2,1)}, f32[384,672]{0,1:T(8,128)S(1)}) fusion(bf16[384,672]{0,1:T(8,128)(2,1)S(1)} %copy-done.4, f32[384]{0:T(512)S(1)} %convert_reduce_fusion, bf16[3072,672]{1,0:T(8,128)(2,1)} %bitcast.27, bf16[384,3200]{1,0:T(8,128)(2,1)S(1)} %bitcast.90), kind=kOutput, calls=%fused_computation.16 | convolution fusion | flops 1587511296 | bytes 8554496 | tf_op jit(solution)/shard_map/dot_general | solution.py:104
  131.4 4.7 %convolution_convert_fusion = bf16[384,3072]{1,0:T(8,128)(2,1)S(1)} fusion(bf16[3072,672]{1,0:T(8,128)(2,1)} %bitcast.27, bf16[384,672]{0,1:T(8,128)(2,1)S(1)} %copy-done.4, f32[384,672]{0,1:T(8,128)S(1)} %get-tuple-element.32, bf16[384,672]{0,1:T(8,128)(2,1)S(1)} %copy-done.5, pred[384]{0:T(512)(128)(4,1)S(1)} %fusion.23), kind=kOutput, calls=%fused_computation | convolution fusion | flops 1589981184 | bytes 8552832 | tf_op jit(solution)/shard_map/dot_general | solution.py:122
  137.2 4.4 %collective-permute-start.10 = (bf16[2,2,48,1536]{3,2,0,1:T(8,128)(2,1)}, bf16[2,2,48,1536]{3,2,0,1:T(8,128)(2,1)S(1)}, u32[]{:S(2)}, u32[]{:S(2)}) collective-permute-start(bf16[2,2,48,1536]{3,2,0,1:T(8,128)(2,1)} %bitcast.87), channel_id=1, source_target_pairs={{0,1},{1,0},{2,3},{3,2},{4,5},{5,4},{6,7},{7,6},{8,9},{9,8},{10,11... | collective-permute-start | bytes 1769480 | tf_op jit(solution)/shard_map/ppermute | solution.py:126
  141.7 1.9 %collective-permute-start.13 = (bf16[2,2,48,1536]{3,2,1,0:T(8,128)(2,1)S(1)}, bf16[2,2,48,1536]{3,2,1,0:T(8,128)(2,1)S(1)}, u32[]{:S(2)}, u32[]{:S(2)}) collective-permute-start(bf16[2,2,48,1536]{3,2,1,0:T(8,128)(2,1)S(1)} %dynamic-slice_bitcast_fusion), channel_id=1, source_target_pairs={{0,1},{1,0},{2,3},{3,2},{4,5},{5,4},{6,7},{7,6},{8,9},{9,8},{10,11... | collective-permute-start | bytes 1769480 | tf_op jit(solution)/shard_map/ppermute | solution.py:126
  143.9 2.1 %collective-permute-start.11 = (bf16[2,48,1536]{2,1,0:T(8,128)(2,1)S(1)}, bf16[2,48,1536]{2,1,0:T(8,128)(2,1)S(1)}, u32[]{:S(2)}, u32[]{:S(2)}) collective-permute-start(bf16[2,48,1536]{2,1,0:T(8,128)(2,1)S(1)} %dynamic-slice_bitcast_fusion.2), channel_id=1, source_target_pairs={{0,2},{2,0},{4,6},{6,4},{1,3},{3,1},{5,7},{7,5},{8,10},{10,8},{12,... | collective-permute-start | bytes 884744 | tf_op jit(solution)/shard_map/ppermute | solution.py:128
  146.1 3.2 %collective-permute-start.14 = (bf16[2,48,1536]{2,1,0:T(8,128)(2,1)S(1)}, bf16[2,48,1536]{2,1,0:T(8,128)(2,1)S(1)}, u32[]{:S(2)}, u32[]{:S(2)}) collective-permute-start(bf16[2,48,1536]{2,1,0:T(8,128)(2,1)S(1)} %dynamic-slice_bitcast_fusion.1), channel_id=1, source_target_pairs={{0,2},{2,0},{4,6},{6,4},{1,3},{3,1},{5,7},{7,5},{8,10},{10,8},{12,... | collective-permute-start | bytes 884744 | tf_op jit(solution)/shard_map/ppermute | solution.py:128
  149.4 4.5 %collective-permute-done.11 = bf16[2,48,1536]{2,1,0:T(8,128)(2,1)S(1)} collective-permute-done((bf16[2,48,1536]{2,1,0:T(8,128)(2,1)S(1)}, bf16[2,48,1536]{2,1,0:T(8,128)(2,1)S(1)}, u32[]{:S(2)}, u32[]{:S(2)}) %collective-permute-start.11) | collective-permute-done | bytes 294944 | tf_op jit(solution)/shard_map/ppermute | solution.py:128
  153.9 2.4 %collective-permute-start.12 = (bf16[48,1536]{1,0:T(8,128)(2,1)S(1)}, bf16[48,1536]{1,0:T(8,128)(2,1)S(1)}, u32[]{:S(2)}, u32[]{:S(2)}) collective-permute-start(bf16[48,1536]{1,0:T(8,128)(2,1)S(1)} %dynamic-slice_bitcast_fusion.4), channel_id=1, source_target_pairs={{0,4},{2,6},{4,0},{6,2},{1,5},{3,7},{5,1},{7,3},{8,12},{10,14},{12... | collective-permute-start | bytes 442376 | tf_op jit(solution)/shard_map/ppermute | solution.py:130
  156.4 5.4 %collective-permute-done.14 = bf16[2,48,1536]{2,1,0:T(8,128)(2,1)S(1)} collective-permute-done((bf16[2,48,1536]{2,1,0:T(8,128)(2,1)S(1)}, bf16[2,48,1536]{2,1,0:T(8,128)(2,1)S(1)}, u32[]{:S(2)}, u32[]{:S(2)}) %collective-permute-start.14) | collective-permute-done | bytes 294944 | tf_op jit(solution)/shard_map/ppermute | solution.py:128
  161.8 1.9 %collective-permute-start.15 = (bf16[48,1536]{1,0:T(8,128)(2,1)S(1)}, bf16[48,1536]{1,0:T(8,128)(2,1)S(1)}, u32[]{:S(2)}, u32[]{:S(2)}) collective-permute-start(bf16[48,1536]{1,0:T(8,128)(2,1)S(1)} %dynamic-slice_bitcast_fusion.3), channel_id=1, source_target_pairs={{0,4},{2,6},{4,0},{6,2},{1,5},{3,7},{5,1},{7,3},{8,12},{10,14},{12... | collective-permute-start | bytes 442376 | tf_op jit(solution)/shard_map/ppermute | solution.py:130
  163.8 7.6 %collective-permute-done.15 = bf16[48,1536]{1,0:T(8,128)(2,1)S(1)} collective-permute-done((bf16[48,1536]{1,0:T(8,128)(2,1)S(1)}, bf16[48,1536]{1,0:T(8,128)(2,1)S(1)}, u32[]{:S(2)}, u32[]{:S(2)}) %collective-permute-start.15) | collective-permute-done | bytes 147488 | tf_op jit(solution)/shard_map/ppermute | solution.py:130
  (65 shorter events, 20.3 us)
Async XLA Ops:
  0.6 27.2 %copy-start = (bf16[128,3072]{1,0:T(8,128)(2,1)S(1)}, bf16[128,3072]{1,0:T(8,128)(2,1)}, u32[]{:S(2)}) copy-start(bf16[128,3072]{1,0:T(8,128)(2,1)} %param.8) | copy-start | bytes 2359300
  2.2 42.6 %all-to-all-start = ((bf16[8,24,672]{2,1,0:T(8,128)(2,1)}), bf16[8,24,672]{2,1,0:T(8,128)(2,1)S(1)}, u32[]{:S(2)}, u32[]{:S(2)}) async-start(bf16[8,24,672]{2,1,0:T(8,128)(2,1)} %broadcast_in_dim.56), calls=%async_computation | async-start | bytes 589824 | tf_op jit(solution)/shard_map/all_to_all | solution.py:19
  29.1 15.8 %collective-permute-start = (bf16[48,3200]{1,0:T(8,128)(2,1)S(1)}, bf16[48,3200]{1,0:T(8,128)(2,1)S(1)}, u32[]{:S(2)}, u32[]{:S(2)}) collective-permute-start(bf16[48,3200]{1,0:T(8,128)(2,1)S(1)} %get-tuple-element.30), channel_id=1, source_target_pairs={{0,2},{2,0},{4,6},{6,4},{1,3},{3,1},{5,7},{7,5},{8,10},{10,8},{12,... | collective-permute-start | bytes 921608 | tf_op jit(solution)/shard_map/ppermute | solution.py:67
  44.8 32.8 %copy-start.3 = (bf16[48,3200]{1,0:T(8,128)(2,1)}, bf16[48,3200]{1,0:T(8,128)(2,1)S(1)}, u32[]{:S(2)}) copy-start(bf16[48,3200]{1,0:T(8,128)(2,1)S(1)} %collective-permute-done) | copy-start | bytes 921604
  44.9 22.4 %collective-permute-start.1 = (bf16[4,2,24,384]{3,2,1,0:T(8,128)(2,1)S(1)}, bf16[4,2,24,384]{3,2,1,0:T(8,128)(2,1)S(1)}, u32[]{:S(2)}, u32[]{:S(2)}) collective-permute-start(bf16[4,2,24,384]{3,2,1,0:T(8,128)(2,1)S(1)} %slice.64), channel_id=1, source_target_pairs={{0,896},{64,960},{128,0},{192,64},{256,128},{320,192},{384,256},{4... | collective-permute-start | bytes 442376 | tf_op jit(solution)/shard_map/ppermute | solution.py:24
  54.9 13.6 %collective-permute-start.6 = (bf16[4,2,24,384]{3,2,1,0:T(8,128)(2,1)S(1)}, bf16[4,2,24,384]{3,2,1,0:T(8,128)(2,1)}, u32[]{:S(2)}, u32[]{:S(2)}) collective-permute-start(bf16[4,2,24,384]{3,2,1,0:T(8,128)(2,1)S(1)} %slice.64), channel_id=1, source_target_pairs={{0,960},{64,0},{128,64},{192,128},{256,192},{320,256},{384,320},{4... | collective-permute-start | bytes 442376 | tf_op jit(solution)/shard_map/ppermute | solution.py:24
  59.1 9.4 %collective-permute-start.7 = (bf16[4,2,24,384]{3,2,1,0:T(8,128)(2,1)S(1)}, bf16[4,2,24,384]{3,2,1,0:T(8,128)(2,1)}, u32[]{:S(2)}, u32[]{:S(2)}) collective-permute-start(bf16[4,2,24,384]{3,2,1,0:T(8,128)(2,1)S(1)} %slice.64), channel_id=1, source_target_pairs={{0,64},{64,128},{128,192},{192,256},{256,320},{320,384},{384,448},... | collective-permute-start | bytes 442376 | tf_op jit(solution)/shard_map/ppermute | solution.py:24
  63.3 12.6 %all-to-all-start.1 = ((bf16[4,4,2,24,288]{4,3,2,1,0:T(8,128)(2,1)}), bf16[4,4,2,24,288]{4,3,2,1,0:T(8,128)(2,1)S(1)}, u32[]{:S(2)}, u32[]{:S(2)}) async-start(bf16[4,4,2,24,288]{4,3,2,1,0:T(8,128)(2,1)} %broadcast_in_dim.59), calls=%async_computation.1 | async-start | bytes 1179648 | tf_op jit(solution)/shard_map/all_to_all | solution.py:19
  70.8 31.7 %collective-permute-start.2 = (bf16[2,48,3200]{2,1,0:T(8,128)(2,1)}, bf16[2,48,3200]{2,1,0:T(8,128)(2,1)}, u32[]{:S(2)}, u32[]{:S(2)}) collective-permute-start(bf16[2,48,3200]{2,1,0:T(8,128)(2,1)} %maximum_select_fusion.3), channel_id=1, source_target_pairs={{0,4},{2,6},{4,0},{6,2},{1,5},{3,7},{5,1},{7,3},{8,12},{10,14},{12... | collective-permute-start | bytes 1843208 | tf_op jit(solution)/shard_map/ppermute | solution.py:74
  75.9 1.8 %copy-start.1 = (bf16[4,4,2,24,288]{4,3,2,1,0:T(8,128)(2,1)}, bf16[4,4,2,24,288]{4,3,2,1,0:T(8,128)(2,1)S(1)}, u32[]{:S(2)}) copy-start(bf16[4,4,2,24,288]{4,3,2,1,0:T(8,128)(2,1)S(1)} %all-to-all-done.1) | copy-start | bytes 1327108
  77.7 41.0 %all-to-all-start.2 = ((bf16[4,4,4,2,24,384]{5,4,3,1,2,0:T(8,128)(2,1)}), bf16[4,4,4,2,24,384]{5,4,3,1,2,0:T(8,128)(2,1)S(1)}, u32[]{:S(2)}, u32[]{:S(2)}) async-start(bf16[4,4,4,2,24,384]{5,4,3,1,2,0:T(8,128)(2,1)} %broadcast_in_dim.63), calls=%async_computation.2 | async-start | bytes 4718592 | tf_op jit(solution)/shard_map/all_to_all | solution.py:19
  81.3 9.4 %copy-start.2 = (bf16[4,4,2,24,288]{4,3,2,1,0:T(8,128)(2,1)S(1)}, bf16[4,4,2,24,288]{4,3,2,1,0:T(8,128)(2,1)}, u32[]{:S(2)}) copy-start(bf16[4,4,2,24,288]{4,3,2,1,0:T(8,128)(2,1)} %copy-done.1) | copy-start | bytes 1327108
  84.5 36.0 %collective-permute-start.8 = (bf16[2,4,2,24,288]{4,3,2,1,0:T(8,128)(2,1)}, bf16[2,4,2,24,288]{4,3,2,1,0:T(8,128)(2,1)S(1)}, u32[]{:S(2)}, u32[]{:S(2)}) collective-permute-start(bf16[2,4,2,24,288]{4,3,2,1,0:T(8,128)(2,1)} %get-tuple-element.26), channel_id=1, source_target_pairs={{0,896},{64,960},{128,0},{192,64},{256,128},{320,192},{384,256},{4... | collective-permute-start | bytes 663560 | tf_op jit(solution)/shard_map/ppermute | solution.py:24
  86.7 33.8 %collective-permute-start.9 = (bf16[2,4,2,24,288]{4,3,2,1,0:T(8,128)(2,1)}, bf16[2,4,2,24,288]{4,3,2,1,0:T(8,128)(2,1)}, u32[]{:S(2)}, u32[]{:S(2)}) collective-permute-start(bf16[2,4,2,24,288]{4,3,2,1,0:T(8,128)(2,1)} %get-tuple-element.27), channel_id=1, source_target_pairs={{0,128},{64,192},{128,256},{192,320},{256,384},{320,448},{384,512}... | collective-permute-start | bytes 663560 | tf_op jit(solution)/shard_map/ppermute | solution.py:24
  90.7 26.1 %collective-permute-start.4 = (bf16[4,4,2,24,288]{4,3,2,1,0:T(8,128)(2,1)S(1)}, bf16[4,4,2,24,288]{4,3,2,1,0:T(8,128)(2,1)S(1)}, u32[]{:S(2)}, u32[]{:S(2)}) collective-permute-start(bf16[4,4,2,24,288]{4,3,2,1,0:T(8,128)(2,1)S(1)} %copy-done.2), channel_id=1, source_target_pairs={{0,64},{64,128},{128,192},{192,256},{256,320},{320,384},{384,448},... | collective-permute-start | bytes 1327112 | tf_op jit(solution)/shard_map/ppermute | solution.py:24
  93.7 24.0 %collective-permute-start.5 = (bf16[4,4,2,24,288]{4,3,2,1,0:T(8,128)(2,1)S(1)}, bf16[4,4,2,24,288]{4,3,2,1,0:T(8,128)(2,1)S(1)}, u32[]{:S(2)}, u32[]{:S(2)}) collective-permute-start(bf16[4,4,2,24,288]{4,3,2,1,0:T(8,128)(2,1)S(1)} %copy-done.2), channel_id=1, source_target_pairs={{0,960},{64,0},{128,64},{192,128},{256,192},{320,256},{384,320},{4... | collective-permute-start | bytes 1327112 | tf_op jit(solution)/shard_map/ppermute | solution.py:24
  105.1 17.3 %collective-permute-start.3 = (bf16[4,48,3200]{2,1,0:T(8,128)(2,1)}, bf16[4,48,3200]{2,1,0:T(8,128)(2,1)}, u32[]{:S(2)}, u32[]{:S(2)}) collective-permute-start(bf16[4,48,3200]{2,1,0:T(8,128)(2,1)} %bitcast.10), channel_id=1, source_target_pairs={{0,1},{1,0},{2,3},{3,2},{4,5},{5,4},{6,7},{7,6},{8,9},{9,8},{10,11... | collective-permute-start | bytes 3686408 | tf_op jit(solution)/shard_map/ppermute | solution.py:83
  122.4 3.3 %copy-start.4 = (bf16[384,672]{0,1:T(8,128)(2,1)S(1)}, bf16[384,672]{0,1:T(8,128)(2,1)}, u32[]{:S(2)}) copy-start(bf16[384,672]{0,1:T(8,128)(2,1)} %param.12) | copy-start | bytes 1548292
  125.6 5.8 %copy-start.5 = (bf16[384,672]{0,1:T(8,128)(2,1)S(1)}, bf16[384,672]{0,1:T(8,128)(2,1)}, u32[]{:S(2)}) copy-start(bf16[384,672]{0,1:T(8,128)(2,1)} %param.13) | copy-start | bytes 1548292
  137.2 6.4 %collective-permute-start.10 = (bf16[2,2,48,1536]{3,2,0,1:T(8,128)(2,1)}, bf16[2,2,48,1536]{3,2,0,1:T(8,128)(2,1)S(1)}, u32[]{:S(2)}, u32[]{:S(2)}) collective-permute-start(bf16[2,2,48,1536]{3,2,0,1:T(8,128)(2,1)} %bitcast.87), channel_id=1, source_target_pairs={{0,1},{1,0},{2,3},{3,2},{4,5},{5,4},{6,7},{7,6},{8,9},{9,8},{10,11... | collective-permute-start | bytes 1769480 | tf_op jit(solution)/shard_map/ppermute | solution.py:126
  141.7 4.2 %collective-permute-start.13 = (bf16[2,2,48,1536]{3,2,1,0:T(8,128)(2,1)S(1)}, bf16[2,2,48,1536]{3,2,1,0:T(8,128)(2,1)S(1)}, u32[]{:S(2)}, u32[]{:S(2)}) collective-permute-start(bf16[2,2,48,1536]{3,2,1,0:T(8,128)(2,1)S(1)} %dynamic-slice_bitcast_fusion), channel_id=1, source_target_pairs={{0,1},{1,0},{2,3},{3,2},{4,5},{5,4},{6,7},{7,6},{8,9},{9,8},{10,11... | collective-permute-start | bytes 1769480 | tf_op jit(solution)/shard_map/ppermute | solution.py:126
  143.9 10.0 %collective-permute-start.11 = (bf16[2,48,1536]{2,1,0:T(8,128)(2,1)S(1)}, bf16[2,48,1536]{2,1,0:T(8,128)(2,1)S(1)}, u32[]{:S(2)}, u32[]{:S(2)}) collective-permute-start(bf16[2,48,1536]{2,1,0:T(8,128)(2,1)S(1)} %dynamic-slice_bitcast_fusion.2), channel_id=1, source_target_pairs={{0,2},{2,0},{4,6},{6,4},{1,3},{3,1},{5,7},{7,5},{8,10},{10,8},{12,... | collective-permute-start | bytes 884744 | tf_op jit(solution)/shard_map/ppermute | solution.py:128
  146.1 15.6 %collective-permute-start.14 = (bf16[2,48,1536]{2,1,0:T(8,128)(2,1)S(1)}, bf16[2,48,1536]{2,1,0:T(8,128)(2,1)S(1)}, u32[]{:S(2)}, u32[]{:S(2)}) collective-permute-start(bf16[2,48,1536]{2,1,0:T(8,128)(2,1)S(1)} %dynamic-slice_bitcast_fusion.1), channel_id=1, source_target_pairs={{0,2},{2,0},{4,6},{6,4},{1,3},{3,1},{5,7},{7,5},{8,10},{10,8},{12,... | collective-permute-start | bytes 884744 | tf_op jit(solution)/shard_map/ppermute | solution.py:128
  153.9 9.8 %collective-permute-start.12 = (bf16[48,1536]{1,0:T(8,128)(2,1)S(1)}, bf16[48,1536]{1,0:T(8,128)(2,1)S(1)}, u32[]{:S(2)}, u32[]{:S(2)}) collective-permute-start(bf16[48,1536]{1,0:T(8,128)(2,1)S(1)} %dynamic-slice_bitcast_fusion.4), channel_id=1, source_target_pairs={{0,4},{2,6},{4,0},{6,2},{1,5},{3,7},{5,1},{7,3},{8,12},{10,14},{12... | collective-permute-start | bytes 442376 | tf_op jit(solution)/shard_map/ppermute | solution.py:130
  161.8 9.6 %collective-permute-start.15 = (bf16[48,1536]{1,0:T(8,128)(2,1)S(1)}, bf16[48,1536]{1,0:T(8,128)(2,1)S(1)}, u32[]{:S(2)}, u32[]{:S(2)}) collective-permute-start(bf16[48,1536]{1,0:T(8,128)(2,1)S(1)} %dynamic-slice_bitcast_fusion.3), channel_id=1, source_target_pairs={{0,4},{2,6},{4,0},{6,2},{1,5},{3,7},{5,1},{7,3},{8,12},{10,14},{12... | collective-permute-start | bytes 442376 | tf_op jit(solution)/shard_map/ppermute | solution.py:130

commit v5 on v4

--- a/solution.py
+++ b/solution.py
@@ -22,6 +22,16 @@
 def along_z(part, by):
     za, zb = lax.axis_size("za"), lax.axis_size("zb")
     return lax.ppermute(part, ("za", "zb"), shifted(za, zb, by))
+
+
+def two_along_z(part):
+    za, zb, core = lax.axis_size("za"), lax.axis_size("zb"), lax.axis_size("core")
+    count = za * zb
+    pairs = []
+    for z in range(count):
+        for c in range(core):
+            pairs.append((z * core + c, (z + (2 if c else -2)) % count * core + c))
+    return lax.ppermute(part, ("za", "zb", "core"), pairs)
 
 
 def in_order(own, other, which):
@@ -69,19 +79,20 @@
     far = everyone(weight, ("za", "yh")).reshape(4, 2, depth, width)
     far, near = lax.optimization_barrier((far, near))
     one, two = far[..., :cut], far[..., cut:]
-    beside = (along_z(one, 1), along_z(one, -1), along_z(one, -2))
+    beside = (along_z(one, 1), along_z(one, -1), two_along_z(one))
     two_rows = in_order(sent, near, (yl + nothing(beside[2])) % 2)
     opposite = lax.ppermute(two_rows, "yl", by_two)
     one_x = everyone(by_residue(one, *beside), ("x",))
     two_x = everyone(two, ("x",))
     zb = lax.axis_index("zb")
     below, above = along_z(two_x, 1), along_z(two_x, -1)
-    two_far = jnp.concatenate([along_z(two_x[:2], -2), along_z(two_x[2:], 2)])
+    two_far = two_along_z(two_x)
 
     four_rows = in_order(two_rows, opposite, yl // 2)
     four_rows = four_rows.reshape(n_yl, slot_count, model + 128)
     theirs = lax.ppermute(four_rows, "core", [(0, 1), (1, 0)])
-    got = jnp.where(core == 0, jnp.stack([four_rows, theirs], 1), jnp.stack([theirs, four_rows], 1))
+    got = jnp.stack([four_rows, four_rows], 1)
+    got = lax.dynamic_update_slice(got, theirs[:, None], (0, 1 - core, 0, 0))
     got = got.reshape(n_yl * n_core * slot_count, model + 128)
     rows = got[:, :model]
     scales32 = got[:, model:model + 1].astype(jnp.float32)

time: 174 us -> 163 us (0.937)
  starting transfers between devices: 85.6 us -> 79.5 us
  waiting for transfers between devices: 44.3 us -> 40.7 us
  other arithmetic: 12.7 us -> 9.97 us
    ppermute x7 -> x4, starting transfers between devices: 30 us -> 15.4 us  [along_z(): return lax.ppermute(part, ('za', 'zb'), shifted(za, zb, by))]
    ppermute x0 -> x2, starting transfers between devices: none -> 10.5 us  [two_along_z(): return lax.ppermute(part, ('za', 'zb', 'core'), pairs)]
    ppermute x7 -> x4, waiting for transfers between devices: 5.44 us -> 0.01 us  [along_z(): return lax.ppermute(part, ('za', 'zb'), shifted(za, zb, by))]
    another operation x1 -> x2, other arithmetic: 0.17 us -> 3.65 us  [the longest x1 3.48 us: body(): got = jnp.stack([four_rows, four_rows], 1)]
    select_n x1 -> x0, other arithmetic: 2.98 us -> none  [body(): jnp.where(core == 0, jnp.stack([four_rows, theirs], 1), jnp.stack([theirs...]
    ppermute x1, waiting for transfers between devices: 5.26 us -> 8.04 us  [body(): opposite = lax.ppermute(two_rows, 'yl', by_two)]
    dynamic_update_slice x3 -> x4, local copies, waits for them, and re-layouts: 2.74 us -> 4.78 us  [placed(): return lax.dynamic_update_slice(whole, piece, at)]
    ppermute x2, starting transfers between devices: 6.33 us -> 4.33 us  [returned(): swapped = lax.ppermute(pick(part, 2, 1 - core), 'core', [(0, 1), (1, 0)])]
  transfers between devices with their start and end apart: 19 -> 18, of which waited for: 7 -> 6; matrix products, arithmetic and copies ran while one was open for 13% -> 15% of each run, Pallas kernels for 0% -> 0%
where the time goes in v5:
time: 163 us; the launch traced here: 162 us
  starting transfers between devices  79.5 us (49%)
  waiting for transfers between devices  40.7 us (25%)
  local copies, waits for them, and re-layouts  17 us (10%)
  matrix products  12.8 us (8%)
  other arithmetic  9.97 us (6%)
  between operations  1.89 us (1%)
    all_to_all x3, starting transfers between devices, everyone(): lax.all_to_all(jnp.broadcast_to(part[None], (count,) + part.shape), axes,...  32.2 us
    ppermute x4, starting transfers between devices, along_z(): return lax.ppermute(part, ('za', 'zb'), shifted(za, zb, by))  15.4 us
    ppermute x1, waiting for transfers between devices, body(): near = lax.ppermute(sent, 'yl', by_one)  13.5 us
    ppermute x2, starting transfers between devices, two_along_z(): return lax.ppermute(part, ('za', 'zb', 'core'), pairs)  10.5 us
    ppermute x2, waiting for transfers between devices, returned(): near = lax.ppermute(pick(pair, 1, 1 - yl % 2), 'yl', by_one)  9.79 us
    ppermute x1, waiting for transfers between devices, body(): opposite = lax.ppermute(two_rows, 'yl', by_two)  8.04 us
    ppermute x2, waiting for transfers between devices, returned(): far = lax.ppermute(pick(four, 0, 1 - yl // 2), 'yl', by_two)  7.85 us
    dot_general x1, matrix products, body(): product = jnp.dot(rows, gathered, preferred_element_type=jnp.float32)  5.74 us
  transfers between devices with their start and end apart: 18, of which 6 were waited for; matrix products, arithmetic and copies ran while one was open for 15% of the time, Pallas kernels for 0%

profile of v5, /device:TPU:1, one launch (start us, length us, event | category | flops | bytes accessed | tf_op | source)
XLA Modules:
  0.0 161.9 jit_solution(15057258224631622190)
XLA Ops:
  0.6 1.6 broadcast_in_dim.59
  2.2 24.5 %all-to-all-start = ((bf16[8,24,672]{2,1,0:T(8,128)(2,1)}), bf16[8,24,672]{2,1,0:T(8,128)(2,1)S(1)}, u32[]{:S(2)}, u32[]{:S(2)}) async-start(bf16[8,24,672]{2,1,0:T(8,128)(2,1)} %broadcast_in_dim.59), calls=%async_computation | async-start | bytes 589824 | tf_op jit(solution)/shard_map/all_to_all | solution.py:19
  29.1 2.3 %collective-permute-start = (bf16[48,3200]{1,0:T(8,128)(2,1)S(1)}, bf16[48,3200]{1,0:T(8,128)(2,1)S(1)}, u32[]{:S(2)}, u32[]{:S(2)}) collective-permute-start(bf16[48,3200]{1,0:T(8,128)(2,1)S(1)} %get-tuple-element.28), channel_id=1, source_target_pairs={{0,2},{2,0},{4,6},{6,4},{1,3},{3,1},{5,7},{7,5},{8,10},{10,8},{12,... | collective-permute-start | bytes 921608 | tf_op jit(solution)/shard_map/ppermute | solution.py:77
  31.4 13.5 %collective-permute-done = bf16[48,3200]{1,0:T(8,128)(2,1)S(1)} collective-permute-done((bf16[48,3200]{1,0:T(8,128)(2,1)S(1)}, bf16[48,3200]{1,0:T(8,128)(2,1)S(1)}, u32[]{:S(2)}, u32[]{:S(2)}) %collective-permute-start) | collective-permute-done | bytes 307232 | tf_op jit(solution)/shard_map/ppermute | solution.py:77
  44.9 8.6 %collective-permute-start.1 = (bf16[4,2,24,384]{3,2,1,0:T(8,128)(2,1)S(1)}, bf16[4,2,24,384]{3,2,1,0:T(8,128)(2,1)S(1)}, u32[]{:S(2)}, u32[]{:S(2)}) collective-permute-start(bf16[4,2,24,384]{3,2,1,0:T(8,128)(2,1)S(1)} %slice.58), channel_id=1, source_target_pairs={{0,896},{1,129},{64,960},{65,193},{128,0},{129,257},{192,64},{193,... | collective-permute-start | bytes 442376 | tf_op jit(solution)/shard_map/ppermute | solution.py:34
  53.4 5.7 %collective-permute-start.6 = (bf16[4,2,24,384]{3,2,1,0:T(8,128)(2,1)S(1)}, bf16[4,2,24,384]{3,2,1,0:T(8,128)(2,1)S(1)}, u32[]{:S(2)}, u32[]{:S(2)}) collective-permute-start(bf16[4,2,24,384]{3,2,1,0:T(8,128)(2,1)S(1)} %slice.58), channel_id=1, source_target_pairs={{0,960},{64,0},{128,64},{192,128},{256,192},{320,256},{384,320},{4... | collective-permute-start | bytes 442376 | tf_op jit(solution)/shard_map/ppermute | solution.py:24
  59.1 1.9 %collective-permute-start.7 = (bf16[4,2,24,384]{3,2,1,0:T(8,128)(2,1)S(1)}, bf16[4,2,24,384]{3,2,1,0:T(8,128)(2,1)S(1)}, u32[]{:S(2)}, u32[]{:S(2)}) collective-permute-start(bf16[4,2,24,384]{3,2,1,0:T(8,128)(2,1)S(1)} %slice.58), channel_id=1, source_target_pairs={{0,64},{64,128},{128,192},{192,256},{256,320},{320,384},{384,448},... | collective-permute-start | bytes 442376 | tf_op jit(solution)/shard_map/ppermute | solution.py:24
  62.1 4.0 %all-to-all-start.1 = ((bf16[4,4,2,24,288]{4,3,2,1,0:T(8,128)(2,1)}), bf16[4,4,2,24,288]{4,3,2,1,0:T(8,128)(2,1)S(1)}, u32[]{:S(2)}, u32[]{:S(2)}) async-start(bf16[4,4,2,24,288]{4,3,2,1,0:T(8,128)(2,1)} %broadcast_in_dim.63), calls=%async_computation.1 | async-start | bytes 1179648 | tf_op jit(solution)/shard_map/all_to_all | solution.py:19
  68.6 2.4 %collective-permute-start.2 = (bf16[2,48,3200]{2,1,0:T(8,128)(2,1)}, bf16[2,48,3200]{2,1,0:T(8,128)(2,1)}, u32[]{:S(2)}, u32[]{:S(2)}) collective-permute-start(bf16[2,48,3200]{2,1,0:T(8,128)(2,1)} %maximum_select_fusion.2), channel_id=1, source_target_pairs={{0,4},{2,6},{4,0},{6,2},{1,5},{3,7},{5,1},{7,3},{8,12},{10,14},{12... | collective-permute-start | bytes 1843208 | tf_op jit(solution)/shard_map/ppermute | solution.py:84
  73.5 1.8 %broadcast_in_dim.67 = bf16[4,4,4,2,24,384]{5,4,3,1,2,0:T(8,128)(2,1)} broadcast(bf16[4,4,2,24,384]{4,3,2,0,1:T(8,128)(2,1)S(1)} %copy.34), dimensions={1,2,3,4,5} | broadcast | bytes 2949120 | tf_op jit(solution)/shard_map/broadcast_in_dim | solution.py:19
  75.3 3.6 %all-to-all-start.2 = ((bf16[4,4,4,2,24,384]{5,4,3,1,2,0:T(8,128)(2,1)}), bf16[4,4,4,2,24,384]{5,4,3,1,2,0:T(8,128)(2,1)S(1)}, u32[]{:S(2)}, u32[]{:S(2)}) async-start(bf16[4,4,4,2,24,384]{5,4,3,1,2,0:T(8,128)(2,1)} %broadcast_in_dim.67), calls=%async_computation.2 | async-start | bytes 4718592 | tf_op jit(solution)/shard_map/all_to_all | solution.py:19
  79.0 2.1 %collective-permute-start.4 = (bf16[4,4,2,24,288]{4,3,2,1,0:T(8,128)(2,1)}, bf16[4,4,2,24,288]{4,3,2,1,0:T(8,128)(2,1)S(1)}, u32[]{:S(2)}, u32[]{:S(2)}) collective-permute-start(bf16[4,4,2,24,288]{4,3,2,1,0:T(8,128)(2,1)} %copy-done.3), channel_id=1, source_target_pairs={{0,64},{64,128},{128,192},{192,256},{256,320},{320,384},{384,448},... | collective-permute-start | bytes 1327112 | tf_op jit(solution)/shard_map/ppermute | solution.py:24
  81.0 5.7 %collective-permute-start.5 = (bf16[4,4,2,24,288]{4,3,2,1,0:T(8,128)(2,1)}, bf16[4,4,2,24,288]{4,3,2,1,0:T(8,128)(2,1)S(1)}, u32[]{:S(2)}, u32[]{:S(2)}) collective-permute-start(bf16[4,4,2,24,288]{4,3,2,1,0:T(8,128)(2,1)} %copy-done.3), channel_id=1, source_target_pairs={{0,960},{64,0},{128,64},{192,128},{256,192},{320,256},{384,320},{4... | collective-permute-start | bytes 1327112 | tf_op jit(solution)/shard_map/ppermute | solution.py:24
  86.8 1.9 %collective-permute-start.8 = (bf16[4,4,2,24,288]{4,3,2,1,0:T(8,128)(2,1)}, bf16[4,4,2,24,288]{4,3,2,1,0:T(8,128)(2,1)}, u32[]{:S(2)}, u32[]{:S(2)}) collective-permute-start(bf16[4,4,2,24,288]{4,3,2,1,0:T(8,128)(2,1)} %copy-done.3), channel_id=1, source_target_pairs={{0,896},{1,129},{64,960},{65,193},{128,0},{129,257},{192,64},{193,... | collective-permute-start | bytes 1327112 | tf_op jit(solution)/shard_map/ppermute | solution.py:34
  88.7 2.7 %broadcast_in_dim.62 = bf16[4,4,2,4,24,672]{5,4,3,2,1,0:T(8,128)(2,1)} broadcast(bf16[]{:T(256)} %constant.172.clone.1), dimensions={} | broadcast | bytes 4128770 | tf_op jit(solution)/shard_map/broadcast_in_dim | solution.py:100
  92.3 8.0 %collective-permute-done.2 = bf16[2,48,3200]{2,1,0:T(8,128)(2,1)} collective-permute-done((bf16[2,48,3200]{2,1,0:T(8,128)(2,1)}, bf16[2,48,3200]{2,1,0:T(8,128)(2,1)}, u32[]{:S(2)}, u32[]{:S(2)}) %collective-permute-start.2) | collective-permute-done | bytes 614432 | tf_op jit(solution)/shard_map/ppermute | solution.py:84
  100.3 2.5 %maximum_select_fusion = bf16[2,2,48,3200]{3,2,1,0:T(8,128)(2,1)} fusion(bf16[1,2,48,3200]{3,2,1,0:T(8,128)(2,1)} %bitcast.7, bf16[1,2,48,3200]{3,2,1,0:T(8,128)(2,1)S(1)} %copy-done.2, pred[]{:T(512)S(6)} %eq.75), kind=kLoop, calls=%fused_computation.10 | loop fusion | flops 1843200 | bytes 2457601 | tf_op jit(solution)/shard_map/jit(_where)/select_n | solution.py:38
  102.9 2.7 %collective-permute-start.3 = (bf16[4,48,3200]{2,1,0:T(8,128)(2,1)}, bf16[4,48,3200]{2,1,0:T(8,128)(2,1)}, u32[]{:S(2)}, u32[]{:S(2)}) collective-permute-start(bf16[4,48,3200]{2,1,0:T(8,128)(2,1)} %bitcast.11), channel_id=1, source_target_pairs={{0,1},{1,0},{2,3},{3,2},{4,5},{5,4},{6,7},{7,6},{8,9},{9,8},{10,11... | collective-permute-start | bytes 3686408 | tf_op jit(solution)/shard_map/ppermute | solution.py:93
  105.6 3.5 %pad_maximum_fusion = bf16[4,2,48,3200]{3,2,1,0:T(8,128)(2,1)} fusion(bf16[4,1,48,3200]{3,2,1,0:T(8,128)(2,1)} %bitcast.9), kind=kLoop, calls=%fused_computation.3 | loop fusion | flops 1228800 | bytes 3686400 | tf_op jit(solution)/shard_map/stack | solution.py:94
  110.9 1.8 %copy_dynamic-update-slice_fusion = bf16[4,4,2,4,24,672]{5,4,3,2,1,0:T(8,128)(2,1)} fusion(bf16[4,4,2,4,24,672]{5,4,3,2,1,0:T(8,128)(2,1)} %copy_dynamic-update-slice_fusion.2, bf16[4,4,4,2,24,384]{5,4,3,1,2,0:T(8,128)(2,1)S(1)} %all-to-all-done.2), kind=kLoop, calls=%fused_computation.6 | loop fusion | bytes 4718592 | tf_op jit(solution)/shard_map/scatter | solution.py:111
  112.7 2.0 %copy_dynamic-update-slice_fusion.1 = bf16[4,4,2,4,24,672]{5,4,3,2,1,0:T(8,128)(2,1)} fusion(bf16[4,4,2,4,24,672]{5,4,3,2,1,0:T(8,128)(2,1)} %copy_dynamic-update-slice_fusion, s32[]{:T(128)S(6)} %select_n.262, bf16[4,4,2,24,288]{4,3,2,1,0:T(8,128)(2,1)} %collective-permute-done.8), kind=kLoop, calls=%fused_computation.32 | loop fusion | bytes 1179652 | tf_op jit(solution)/shard_map/dynamic_update_slice | solution.py:106
  116.5 5.7 %fusion.7 = (bf16[384,672]{0,1:T(8,128)(2,1)}, f32[384,672]{0,1:T(8,128)S(1)}) fusion(bf16[384,672]{0,1:T(8,128)(2,1)S(1)} %copy-done.5, f32[384]{0:T(512)S(1)} %convert_reduce_fusion, bf16[3072,672]{1,0:T(8,128)(2,1)} %bitcast.27, bf16[384,3200]{1,0:T(8,128)(2,1)S(1)} %bitcast.91), kind=kOutput, calls=%fused_computation.17 | convolution fusion | flops 1587511296 | bytes 8554496 | tf_op jit(solution)/shard_map/dot_general | solution.py:115
  122.2 4.7 %convolution_convert_fusion = bf16[384,3072]{1,0:T(8,128)(2,1)S(1)} fusion(bf16[3072,672]{1,0:T(8,128)(2,1)} %bitcast.27, bf16[384,672]{0,1:T(8,128)(2,1)S(1)} %copy-done.5, f32[384,672]{0,1:T(8,128)S(1)} %get-tuple-element.30, bf16[384,672]{0,1:T(8,128)(2,1)S(1)} %copy-done.6, pred[384]{0:T(512)(128)(4,1)S(1)} %fusion.23), kind=kOutput, calls=%fused_computation | convolution fusion | flops 1589981184 | bytes 8552832 | tf_op jit(solution)/shard_map/dot_general | solution.py:133
  128.1 2.4 %collective-permute-start.9 = (bf16[2,2,48,1536]{3,2,0,1:T(8,128)(2,1)}, bf16[2,2,48,1536]{3,2,0,1:T(8,128)(2,1)S(1)}, u32[]{:S(2)}, u32[]{:S(2)}) collective-permute-start(bf16[2,2,48,1536]{3,2,0,1:T(8,128)(2,1)} %bitcast.88), channel_id=1, source_target_pairs={{0,1},{1,0},{2,3},{3,2},{4,5},{5,4},{6,7},{7,6},{8,9},{9,8},{10,11... | collective-permute-start | bytes 1769480 | tf_op jit(solution)/shard_map/ppermute | solution.py:137
  130.6 1.9 %collective-permute-start.12 = (bf16[2,2,48,1536]{3,2,1,0:T(8,128)(2,1)S(1)}, bf16[2,2,48,1536]{3,2,1,0:T(8,128)(2,1)S(1)}, u32[]{:S(2)}, u32[]{:S(2)}) collective-permute-start(bf16[2,2,48,1536]{3,2,1,0:T(8,128)(2,1)S(1)} %dynamic-slice_bitcast_fusion), channel_id=1, source_target_pairs={{0,1},{1,0},{2,3},{3,2},{4,5},{5,4},{6,7},{7,6},{8,9},{9,8},{10,11... | collective-permute-start | bytes 1769480 | tf_op jit(solution)/shard_map/ppermute | solution.py:137
  132.7 2.2 %collective-permute-start.10 = (bf16[2,48,1536]{2,1,0:T(8,128)(2,1)S(1)}, bf16[2,48,1536]{2,1,0:T(8,128)(2,1)S(1)}, u32[]{:S(2)}, u32[]{:S(2)}) collective-permute-start(bf16[2,48,1536]{2,1,0:T(8,128)(2,1)S(1)} %dynamic-slice_bitcast_fusion.2), channel_id=1, source_target_pairs={{0,2},{2,0},{4,6},{6,4},{1,3},{3,1},{5,7},{7,5},{8,10},{10,8},{12,... | collective-permute-start | bytes 884744 | tf_op jit(solution)/shard_map/ppermute | solution.py:139
  135.1 3.1 %collective-permute-start.13 = (bf16[2,48,1536]{2,1,0:T(8,128)(2,1)S(1)}, bf16[2,48,1536]{2,1,0:T(8,128)(2,1)S(1)}, u32[]{:S(2)}, u32[]{:S(2)}) collective-permute-start(bf16[2,48,1536]{2,1,0:T(8,128)(2,1)S(1)} %dynamic-slice_bitcast_fusion.1), channel_id=1, source_target_pairs={{0,2},{2,0},{4,6},{6,4},{1,3},{3,1},{5,7},{7,5},{8,10},{10,8},{12,... | collective-permute-start | bytes 884744 | tf_op jit(solution)/shard_map/ppermute | solution.py:139
  138.2 4.5 %collective-permute-done.10 = bf16[2,48,1536]{2,1,0:T(8,128)(2,1)S(1)} collective-permute-done((bf16[2,48,1536]{2,1,0:T(8,128)(2,1)S(1)}, bf16[2,48,1536]{2,1,0:T(8,128)(2,1)S(1)}, u32[]{:S(2)}, u32[]{:S(2)}) %collective-permute-start.10) | collective-permute-done | bytes 294944 | tf_op jit(solution)/shard_map/ppermute | solution.py:139
  142.8 2.5 %collective-permute-start.11 = (bf16[48,1536]{1,0:T(8,128)(2,1)S(1)}, bf16[48,1536]{1,0:T(8,128)(2,1)S(1)}, u32[]{:S(2)}, u32[]{:S(2)}) collective-permute-start(bf16[48,1536]{1,0:T(8,128)(2,1)S(1)} %dynamic-slice_bitcast_fusion.4), channel_id=1, source_target_pairs={{0,4},{2,6},{4,0},{6,2},{1,5},{3,7},{5,1},{7,3},{8,12},{10,14},{12... | collective-permute-start | bytes 442376 | tf_op jit(solution)/shard_map/ppermute | solution.py:141
  145.3 5.3 %collective-permute-done.13 = bf16[2,48,1536]{2,1,0:T(8,128)(2,1)S(1)} collective-permute-done((bf16[2,48,1536]{2,1,0:T(8,128)(2,1)S(1)}, bf16[2,48,1536]{2,1,0:T(8,128)(2,1)S(1)}, u32[]{:S(2)}, u32[]{:S(2)}) %collective-permute-start.13) | collective-permute-done | bytes 294944 | tf_op jit(solution)/shard_map/ppermute | solution.py:139
  150.7 1.9 %collective-permute-start.14 = (bf16[48,1536]{1,0:T(8,128)(2,1)S(1)}, bf16[48,1536]{1,0:T(8,128)(2,1)S(1)}, u32[]{:S(2)}, u32[]{:S(2)}) collective-permute-start(bf16[48,1536]{1,0:T(8,128)(2,1)S(1)} %dynamic-slice_bitcast_fusion.3), channel_id=1, source_target_pairs={{0,4},{2,6},{4,0},{6,2},{1,5},{3,7},{5,1},{7,3},{8,12},{10,14},{12... | collective-permute-start | bytes 442376 | tf_op jit(solution)/shard_map/ppermute | solution.py:141
  152.7 7.8 %collective-permute-done.14 = bf16[48,1536]{1,0:T(8,128)(2,1)S(1)} collective-permute-done((bf16[48,1536]{1,0:T(8,128)(2,1)S(1)}, bf16[48,1536]{1,0:T(8,128)(2,1)S(1)}, u32[]{:S(2)}, u32[]{:S(2)}) %collective-permute-start.14) | collective-permute-done | bytes 147488 | tf_op jit(solution)/shard_map/ppermute | solution.py:141
  (65 shorter events, 15.1 us)
Async XLA Ops:
  0.6 27.2 %copy-start = (bf16[128,3072]{1,0:T(8,128)(2,1)S(1)}, bf16[128,3072]{1,0:T(8,128)(2,1)}, u32[]{:S(2)}) copy-start(bf16[128,3072]{1,0:T(8,128)(2,1)} %param.8) | copy-start | bytes 2359300
  2.2 42.6 %all-to-all-start = ((bf16[8,24,672]{2,1,0:T(8,128)(2,1)}), bf16[8,24,672]{2,1,0:T(8,128)(2,1)S(1)}, u32[]{:S(2)}, u32[]{:S(2)}) async-start(bf16[8,24,672]{2,1,0:T(8,128)(2,1)} %broadcast_in_dim.59), calls=%async_computation | async-start | bytes 589824 | tf_op jit(solution)/shard_map/all_to_all | solution.py:19
  29.1 15.8 %collective-permute-start = (bf16[48,3200]{1,0:T(8,128)(2,1)S(1)}, bf16[48,3200]{1,0:T(8,128)(2,1)S(1)}, u32[]{:S(2)}, u32[]{:S(2)}) collective-permute-start(bf16[48,3200]{1,0:T(8,128)(2,1)S(1)} %get-tuple-element.28), channel_id=1, source_target_pairs={{0,2},{2,0},{4,6},{6,4},{1,3},{3,1},{5,7},{7,5},{8,10},{10,8},{12,... | collective-permute-start | bytes 921608 | tf_op jit(solution)/shard_map/ppermute | solution.py:77
  44.9 21.3 %collective-permute-start.1 = (bf16[4,2,24,384]{3,2,1,0:T(8,128)(2,1)S(1)}, bf16[4,2,24,384]{3,2,1,0:T(8,128)(2,1)S(1)}, u32[]{:S(2)}, u32[]{:S(2)}) collective-permute-start(bf16[4,2,24,384]{3,2,1,0:T(8,128)(2,1)S(1)} %slice.58), channel_id=1, source_target_pairs={{0,896},{1,129},{64,960},{65,193},{128,0},{129,257},{192,64},{193,... | collective-permute-start | bytes 442376 | tf_op jit(solution)/shard_map/ppermute | solution.py:34
  53.4 13.9 %collective-permute-start.6 = (bf16[4,2,24,384]{3,2,1,0:T(8,128)(2,1)S(1)}, bf16[4,2,24,384]{3,2,1,0:T(8,128)(2,1)S(1)}, u32[]{:S(2)}, u32[]{:S(2)}) collective-permute-start(bf16[4,2,24,384]{3,2,1,0:T(8,128)(2,1)S(1)} %slice.58), channel_id=1, source_target_pairs={{0,960},{64,0},{128,64},{192,128},{256,192},{320,256},{384,320},{4... | collective-permute-start | bytes 442376 | tf_op jit(solution)/shard_map/ppermute | solution.py:24
  59.1 8.2 %collective-permute-start.7 = (bf16[4,2,24,384]{3,2,1,0:T(8,128)(2,1)S(1)}, bf16[4,2,24,384]{3,2,1,0:T(8,128)(2,1)S(1)}, u32[]{:S(2)}, u32[]{:S(2)}) collective-permute-start(bf16[4,2,24,384]{3,2,1,0:T(8,128)(2,1)S(1)} %slice.58), channel_id=1, source_target_pairs={{0,64},{64,128},{128,192},{192,256},{256,320},{320,384},{384,448},... | collective-permute-start | bytes 442376 | tf_op jit(solution)/shard_map/ppermute | solution.py:24
  62.1 11.4 %all-to-all-start.1 = ((bf16[4,4,2,24,288]{4,3,2,1,0:T(8,128)(2,1)}), bf16[4,4,2,24,288]{4,3,2,1,0:T(8,128)(2,1)S(1)}, u32[]{:S(2)}, u32[]{:S(2)}) async-start(bf16[4,4,2,24,288]{4,3,2,1,0:T(8,128)(2,1)} %broadcast_in_dim.63), calls=%async_computation.1 | async-start | bytes 1179648 | tf_op jit(solution)/shard_map/all_to_all | solution.py:19
  68.6 31.7 %collective-permute-start.2 = (bf16[2,48,3200]{2,1,0:T(8,128)(2,1)}, bf16[2,48,3200]{2,1,0:T(8,128)(2,1)}, u32[]{:S(2)}, u32[]{:S(2)}) collective-permute-start(bf16[2,48,3200]{2,1,0:T(8,128)(2,1)} %maximum_select_fusion.2), channel_id=1, source_target_pairs={{0,4},{2,6},{4,0},{6,2},{1,5},{3,7},{5,1},{7,3},{8,12},{10,14},{12... | collective-permute-start | bytes 1843208 | tf_op jit(solution)/shard_map/ppermute | solution.py:84
  73.5 1.8 %copy-start.3 = (bf16[4,4,2,24,288]{4,3,2,1,0:T(8,128)(2,1)}, bf16[4,4,2,24,288]{4,3,2,1,0:T(8,128)(2,1)S(1)}, u32[]{:S(2)}) copy-start(bf16[4,4,2,24,288]{4,3,2,1,0:T(8,128)(2,1)S(1)} %all-to-all-done.1) | copy-start | bytes 1327108
  75.3 35.6 %all-to-all-start.2 = ((bf16[4,4,4,2,24,384]{5,4,3,1,2,0:T(8,128)(2,1)}), bf16[4,4,4,2,24,384]{5,4,3,1,2,0:T(8,128)(2,1)S(1)}, u32[]{:S(2)}, u32[]{:S(2)}) async-start(bf16[4,4,4,2,24,384]{5,4,3,1,2,0:T(8,128)(2,1)} %broadcast_in_dim.67), calls=%async_computation.2 | async-start | bytes 4718592 | tf_op jit(solution)/shard_map/all_to_all | solution.py:19
  79.0 12.4 %copy-start.4 = (bf16[4,4,2,24,288]{4,3,2,1,0:T(8,128)(2,1)S(1)}, bf16[4,4,2,24,288]{4,3,2,1,0:T(8,128)(2,1)}, u32[]{:S(2)}) copy-start(bf16[4,4,2,24,288]{4,3,2,1,0:T(8,128)(2,1)} %copy-done.3) | copy-start | bytes 1327108
  79.0 21.3 %copy-start.2 = (bf16[1,2,48,3200]{3,2,1,0:T(8,128)(2,1)S(1)}, bf16[1,2,48,3200]{3,2,1,0:T(8,128)(2,1)}, u32[]{:S(2)}) copy-start(bf16[1,2,48,3200]{3,2,1,0:T(8,128)(2,1)} %maximum_select_fusion.1) | copy-start | bytes 1843204
  79.0 30.1 %collective-permute-start.4 = (bf16[4,4,2,24,288]{4,3,2,1,0:T(8,128)(2,1)}, bf16[4,4,2,24,288]{4,3,2,1,0:T(8,128)(2,1)S(1)}, u32[]{:S(2)}, u32[]{:S(2)}) collective-permute-start(bf16[4,4,2,24,288]{4,3,2,1,0:T(8,128)(2,1)} %copy-done.3), channel_id=1, source_target_pairs={{0,64},{64,128},{128,192},{192,256},{256,320},{320,384},{384,448},... | collective-permute-start | bytes 1327112 | tf_op jit(solution)/shard_map/ppermute | solution.py:24
  81.0 28.9 %collective-permute-start.5 = (bf16[4,4,2,24,288]{4,3,2,1,0:T(8,128)(2,1)}, bf16[4,4,2,24,288]{4,3,2,1,0:T(8,128)(2,1)S(1)}, u32[]{:S(2)}, u32[]{:S(2)}) collective-permute-start(bf16[4,4,2,24,288]{4,3,2,1,0:T(8,128)(2,1)} %copy-done.3), channel_id=1, source_target_pairs={{0,960},{64,0},{128,64},{192,128},{256,192},{320,256},{384,320},{4... | collective-permute-start | bytes 1327112 | tf_op jit(solution)/shard_map/ppermute | solution.py:24
  86.8 25.9 %collective-permute-start.8 = (bf16[4,4,2,24,288]{4,3,2,1,0:T(8,128)(2,1)}, bf16[4,4,2,24,288]{4,3,2,1,0:T(8,128)(2,1)}, u32[]{:S(2)}, u32[]{:S(2)}) collective-permute-start(bf16[4,4,2,24,288]{4,3,2,1,0:T(8,128)(2,1)} %copy-done.3), channel_id=1, source_target_pairs={{0,896},{1,129},{64,960},{65,193},{128,0},{129,257},{192,64},{193,... | collective-permute-start | bytes 1327112 | tf_op jit(solution)/shard_map/ppermute | solution.py:34
  102.9 11.9 %collective-permute-start.3 = (bf16[4,48,3200]{2,1,0:T(8,128)(2,1)}, bf16[4,48,3200]{2,1,0:T(8,128)(2,1)}, u32[]{:S(2)}, u32[]{:S(2)}) collective-permute-start(bf16[4,48,3200]{2,1,0:T(8,128)(2,1)} %bitcast.11), channel_id=1, source_target_pairs={{0,1},{1,0},{2,3},{3,2},{4,5},{5,4},{6,7},{7,6},{8,9},{9,8},{10,11... | collective-permute-start | bytes 3686408 | tf_op jit(solution)/shard_map/ppermute | solution.py:93
  110.9 3.8 %copy-start.1 = (bf16[4,2,48,3200]{3,2,1,0:T(8,128)(2,1)S(1)}, bf16[4,2,48,3200]{3,2,1,0:T(8,128)(2,1)}, u32[]{:S(2)}) copy-start(bf16[4,2,48,3200]{3,2,1,0:T(8,128)(2,1)} %pad_maximum_fusion) | copy-start | bytes 7372804
  112.7 3.8 %copy-start.5 = (bf16[384,672]{0,1:T(8,128)(2,1)S(1)}, bf16[384,672]{0,1:T(8,128)(2,1)}, u32[]{:S(2)}) copy-start(bf16[384,672]{0,1:T(8,128)(2,1)} %param.12) | copy-start | bytes 1548292
  116.5 5.8 %copy-start.6 = (bf16[384,672]{0,1:T(8,128)(2,1)S(1)}, bf16[384,672]{0,1:T(8,128)(2,1)}, u32[]{:S(2)}) copy-start(bf16[384,672]{0,1:T(8,128)(2,1)} %param.13) | copy-start | bytes 1548292
  128.1 4.4 %collective-permute-start.9 = (bf16[2,2,48,1536]{3,2,0,1:T(8,128)(2,1)}, bf16[2,2,48,1536]{3,2,0,1:T(8,128)(2,1)S(1)}, u32[]{:S(2)}, u32[]{:S(2)}) collective-permute-start(bf16[2,2,48,1536]{3,2,0,1:T(8,128)(2,1)} %bitcast.88), channel_id=1, source_target_pairs={{0,1},{1,0},{2,3},{3,2},{4,5},{5,4},{6,7},{7,6},{8,9},{9,8},{10,11... | collective-permute-start | bytes 1769480 | tf_op jit(solution)/shard_map/ppermute | solution.py:137
  130.6 4.3 %collective-permute-start.12 = (bf16[2,2,48,1536]{3,2,1,0:T(8,128)(2,1)S(1)}, bf16[2,2,48,1536]{3,2,1,0:T(8,128)(2,1)S(1)}, u32[]{:S(2)}, u32[]{:S(2)}) collective-permute-start(bf16[2,2,48,1536]{3,2,1,0:T(8,128)(2,1)S(1)} %dynamic-slice_bitcast_fusion), channel_id=1, source_target_pairs={{0,1},{1,0},{2,3},{3,2},{4,5},{5,4},{6,7},{7,6},{8,9},{9,8},{10,11... | collective-permute-start | bytes 1769480 | tf_op jit(solution)/shard_map/ppermute | solution.py:137
  132.7 10.0 %collective-permute-start.10 = (bf16[2,48,1536]{2,1,0:T(8,128)(2,1)S(1)}, bf16[2,48,1536]{2,1,0:T(8,128)(2,1)S(1)}, u32[]{:S(2)}, u32[]{:S(2)}) collective-permute-start(bf16[2,48,1536]{2,1,0:T(8,128)(2,1)S(1)} %dynamic-slice_bitcast_fusion.2), channel_id=1, source_target_pairs={{0,2},{2,0},{4,6},{6,4},{1,3},{3,1},{5,7},{7,5},{8,10},{10,8},{12,... | collective-permute-start | bytes 884744 | tf_op jit(solution)/shard_map/ppermute | solution.py:139
  135.1 15.5 %collective-permute-start.13 = (bf16[2,48,1536]{2,1,0:T(8,128)(2,1)S(1)}, bf16[2,48,1536]{2,1,0:T(8,128)(2,1)S(1)}, u32[]{:S(2)}, u32[]{:S(2)}) collective-permute-start(bf16[2,48,1536]{2,1,0:T(8,128)(2,1)S(1)} %dynamic-slice_bitcast_fusion.1), channel_id=1, source_target_pairs={{0,2},{2,0},{4,6},{6,4},{1,3},{3,1},{5,7},{7,5},{8,10},{10,8},{12,... | collective-permute-start | bytes 884744 | tf_op jit(solution)/shard_map/ppermute | solution.py:139
  142.8 9.8 %collective-permute-start.11 = (bf16[48,1536]{1,0:T(8,128)(2,1)S(1)}, bf16[48,1536]{1,0:T(8,128)(2,1)S(1)}, u32[]{:S(2)}, u32[]{:S(2)}) collective-permute-start(bf16[48,1536]{1,0:T(8,128)(2,1)S(1)} %dynamic-slice_bitcast_fusion.4), channel_id=1, source_target_pairs={{0,4},{2,6},{4,0},{6,2},{1,5},{3,7},{5,1},{7,3},{8,12},{10,14},{12... | collective-permute-start | bytes 442376 | tf_op jit(solution)/shard_map/ppermute | solution.py:141
  150.7 9.8 %collective-permute-start.14 = (bf16[48,1536]{1,0:T(8,128)(2,1)S(1)}, bf16[48,1536]{1,0:T(8,128)(2,1)S(1)}, u32[]{:S(2)}, u32[]{:S(2)}) collective-permute-start(bf16[48,1536]{1,0:T(8,128)(2,1)S(1)} %dynamic-slice_bitcast_fusion.3), channel_id=1, source_target_pairs={{0,4},{2,6},{4,0},{6,2},{1,5},{3,7},{5,1},{7,3},{8,12},{10,14},{12... | collective-permute-start | bytes 442376 | tf_op jit(solution)/shard_map/ppermute | solution.py:141

commit v6 on v5

--- a/solution.py
+++ b/solution.py
@@ -74,22 +74,24 @@
 
     yl = lax.axis_index("yl")
     by_one, by_two = [(i, i ^ 1) for i in range(4)], [(i, i ^ 2) for i in range(4)]
-    near = lax.ppermute(sent, "yl", by_one)
+    opposite = lax.ppermute(sent, "yl", by_two)
 
     far = everyone(weight, ("za", "yh")).reshape(4, 2, depth, width)
-    far, near = lax.optimization_barrier((far, near))
+    far, opposite = lax.optimization_barrier((far, opposite))
     one, two = far[..., :cut], far[..., cut:]
     beside = (along_z(one, 1), along_z(one, -1), two_along_z(one))
-    two_rows = in_order(sent, near, (yl + nothing(beside[2])) % 2)
-    opposite = lax.ppermute(two_rows, "yl", by_two)
+    two_rows = in_order(sent, opposite, (yl + nothing(beside[2])) // 2)
+    beyond = lax.ppermute(two_rows, "yl", by_one)
     one_x = everyone(by_residue(one, *beside), ("x",))
     two_x = everyone(two, ("x",))
     zb = lax.axis_index("zb")
     below, above = along_z(two_x, 1), along_z(two_x, -1)
     two_far = two_along_z(two_x)
 
-    four_rows = in_order(two_rows, opposite, yl // 2)
-    four_rows = four_rows.reshape(n_yl, slot_count, model + 128)
+    def between(even, odd):
+        return jnp.concatenate([even[:1], odd[:1], even[1:], odd[1:]])
+
+    four_rows = jnp.where(yl % 2 == 0, between(two_rows, beyond), between(beyond, two_rows))
     theirs = lax.ppermute(four_rows, "core", [(0, 1), (1, 0)])
     got = jnp.stack([four_rows, four_rows], 1)
     got = lax.dynamic_update_slice(got, theirs[:, None], (0, 1 - core, 0, 0))

time: 163 us -> 170 us (1.043)
  local copies, waits for them, and re-layouts: 17 us -> 21.8 us
  other arithmetic: 9.97 us -> 6.11 us
  starting transfers between devices: 79.5 us -> 82.7 us
  waiting for transfers between devices: 40.7 us -> 43.7 us
    ppermute x2, starting transfers between devices: 4.33 us -> 9.59 us  [returned(): swapped = lax.ppermute(pick(part, 2, 1 - core), 'core', [(0, 1), (1, 0)])]
    select_n x3 -> x1, other arithmetic: 4.44 us -> 0.95 us  [in_order(): jnp.where(which == 0, jnp.stack([own, other]), jnp.stack([other, own]))]
    ppermute x2, waiting for transfers between devices: 0.01 us -> 3.38 us  [two_along_z(): return lax.ppermute(part, ('za', 'zb', 'core'), pairs)]
    slice x0 -> x3, local copies, waits for them, and re-layouts: none -> 3.17 us  [the longest x2 3.17 us: between(): return jnp.concatenate([even[:1], odd[:1], even[1:], odd[1:]])]
    ppermute x4, starting transfers between devices: 15.4 us -> 12.9 us  [along_z(): return lax.ppermute(part, ('za', 'zb'), shifted(za, zb, by))]
    another operation x1, other arithmetic: 3.48 us -> 1.67 us  [body(): got = jnp.stack([four_rows, four_rows], 1)]
  transfers between devices with their start and end apart: 18 -> 18, of which waited for: 6 -> 7; matrix products, arithmetic and copies ran while one was open for 15% -> 13% of each run, Pallas kernels for 0% -> 0%
where the time goes in v6:
time: 170 us; the launch traced here: 169 us
  starting transfers between devices  82.7 us (49%)
  waiting for transfers between devices  43.7 us (26%)
  local copies, waits for them, and re-layouts  21.8 us (13%)
  matrix products  12.8 us (8%)
  other arithmetic  6.11 us (4%)
  between operations  1.93 us (1%)
    all_to_all x3, starting transfers between devices, everyone(): lax.all_to_all(jnp.broadcast_to(part[None], (count,) + part.shape), axes,...  32.2 us
    ppermute x1, waiting for transfers between devices, body(): opposite = lax.ppermute(sent, 'yl', by_two)  21.5 us
    ppermute x4, starting transfers between devices, along_z(): return lax.ppermute(part, ('za', 'zb'), shifted(za, zb, by))  12.9 us
    ppermute x2, starting transfers between devices, two_along_z(): return lax.ppermute(part, ('za', 'zb', 'core'), pairs)  10.2 us
    ppermute x2, waiting for transfers between devices, returned(): near = lax.ppermute(pick(pair, 1, 1 - yl % 2), 'yl', by_one)  9.89 us
    ppermute x2, starting transfers between devices, returned(): swapped = lax.ppermute(pick(part, 2, 1 - core), 'core', [(0, 1), (1, 0)])  9.59 us
    ppermute x2, waiting for transfers between devices, returned(): far = lax.ppermute(pick(four, 0, 1 - yl // 2), 'yl', by_two)  8.06 us
    dot_general x1, matrix products, body(): product = jnp.dot(rows, gathered, preferred_element_type=jnp.float32)  6.42 us
  transfers between devices with their start and end apart: 18, of which 7 were waited for; matrix products, arithmetic and copies ran while one was open for 13% of the time, Pallas kernels for 0%

profile of v6, /device:TPU:1, one launch (start us, length us, event | category | flops | bytes accessed | tf_op | source)
XLA Modules:
  0.0 169.0 jit_solution(14664113553074866852)
XLA Ops:
  0.7 1.6 broadcast_in_dim.59
  2.2 24.5 %all-to-all-start = ((bf16[8,24,672]{2,1,0:T(8,128)(2,1)}), bf16[8,24,672]{2,1,0:T(8,128)(2,1)S(1)}, u32[]{:S(2)}, u32[]{:S(2)}) async-start(bf16[8,24,672]{2,1,0:T(8,128)(2,1)} %broadcast_in_dim.59), calls=%async_computation | async-start | bytes 589824 | tf_op jit(solution)/shard_map/all_to_all | solution.py:19
  28.4 2.4 %collective-permute-start = (bf16[48,3200]{1,0:T(8,128)(2,1)S(1)}, bf16[48,3200]{1,0:T(8,128)(2,1)S(1)}, u32[]{:S(2)}, u32[]{:S(2)}) collective-permute-start(bf16[48,3200]{1,0:T(8,128)(2,1)S(1)} %get-tuple-element.35), channel_id=1, source_target_pairs={{0,4},{2,6},{4,0},{6,2},{1,5},{3,7},{5,1},{7,3},{8,12},{10,14},{12... | collective-permute-start | bytes 921608 | tf_op jit(solution)/shard_map/ppermute | solution.py:77
  30.8 21.5 %collective-permute-done = bf16[48,3200]{1,0:T(8,128)(2,1)S(1)} collective-permute-done((bf16[48,3200]{1,0:T(8,128)(2,1)S(1)}, bf16[48,3200]{1,0:T(8,128)(2,1)S(1)}, u32[]{:S(2)}, u32[]{:S(2)}) %collective-permute-start) | collective-permute-done | bytes 307232 | tf_op jit(solution)/shard_map/ppermute | solution.py:77
  52.3 4.0 %collective-permute-start.1 = (bf16[4,2,24,384]{3,2,1,0:T(8,128)(2,1)S(1)}, bf16[4,2,24,384]{3,2,1,0:T(8,128)(2,1)S(1)}, u32[]{:S(2)}, u32[]{:S(2)}) collective-permute-start(bf16[4,2,24,384]{3,2,1,0:T(8,128)(2,1)S(1)} %slice.74), channel_id=1, source_target_pairs={{0,896},{1,129},{64,960},{65,193},{128,0},{129,257},{192,64},{193,... | collective-permute-start | bytes 442376 | tf_op jit(solution)/shard_map/ppermute | solution.py:34
  56.5 4.1 %collective-permute-start.6 = (bf16[4,2,24,384]{3,2,1,0:T(8,128)(2,1)S(1)}, bf16[4,2,24,384]{3,2,1,0:T(8,128)(2,1)S(1)}, u32[]{:S(2)}, u32[]{:S(2)}) collective-permute-start(bf16[4,2,24,384]{3,2,1,0:T(8,128)(2,1)S(1)} %slice.74), channel_id=1, source_target_pairs={{0,960},{64,0},{128,64},{192,128},{256,192},{320,256},{384,320},{4... | collective-permute-start | bytes 442376 | tf_op jit(solution)/shard_map/ppermute | solution.py:24
  60.6 1.9 %collective-permute-start.7 = (bf16[4,2,24,384]{3,2,1,0:T(8,128)(2,1)S(1)}, bf16[4,2,24,384]{3,2,1,0:T(8,128)(2,1)S(1)}, u32[]{:S(2)}, u32[]{:S(2)}) collective-permute-start(bf16[4,2,24,384]{3,2,1,0:T(8,128)(2,1)S(1)} %slice.74), channel_id=1, source_target_pairs={{0,64},{64,128},{128,192},{192,256},{256,320},{320,384},{384,448},... | collective-permute-start | bytes 442376 | tf_op jit(solution)/shard_map/ppermute | solution.py:24
  63.4 4.0 %all-to-all-start.1 = ((bf16[4,4,2,24,288]{4,3,2,1,0:T(8,128)(2,1)}), bf16[4,4,2,24,288]{4,3,2,1,0:T(8,128)(2,1)S(1)}, u32[]{:S(2)}, u32[]{:S(2)}) async-start(bf16[4,4,2,24,288]{4,3,2,1,0:T(8,128)(2,1)} %broadcast_in_dim.63), calls=%async_computation.1 | async-start | bytes 1179648 | tf_op jit(solution)/shard_map/all_to_all | solution.py:19
  69.6 1.9 %collective-permute-start.2 = (bf16[2,48,3200]{2,1,0:T(8,128)(2,1)}, bf16[2,48,3200]{2,1,0:T(8,128)(2,1)}, u32[]{:S(2)}, u32[]{:S(2)}) collective-permute-start(bf16[2,48,3200]{2,1,0:T(8,128)(2,1)} %maximum_select_fusion.2), channel_id=1, source_target_pairs={{0,2},{2,0},{4,6},{6,4},{1,3},{3,1},{5,7},{7,5},{8,10},{10,8},{12,... | collective-permute-start | bytes 1843208 | tf_op jit(solution)/shard_map/ppermute | solution.py:84
  71.5 2.0 %fusion.39 = (bf16[1,48,3200]{2,1,0:T(8,128)(2,1)}, bf16[1,1,48,3200]{3,2,1,0:T(8,128)(2,1)S(1)}, bf16[1,1,48,3200]{3,2,1,0:T(8,128)(2,1)}, bf16[1,48,3200]{2,1,0:T(8,128)(2,1)}) fusion(bf16[2,48,3200]{2,1,0:T(8,128)(2,1)} %maximum_select_fusion.2), kind=kLoop, calls=%fused_computation.81 | loop fusion | bytes 1843200 | tf_op jit(solution)/shard_map/slice | solution.py:92
  74.7 1.8 %broadcast_in_dim.67 = bf16[4,4,4,2,24,384]{5,4,3,1,2,0:T(8,128)(2,1)} broadcast(bf16[4,4,2,24,384]{4,3,2,0,1:T(8,128)(2,1)S(1)} %copy.34), dimensions={1,2,3,4,5} | broadcast | bytes 2949120 | tf_op jit(solution)/shard_map/broadcast_in_dim | solution.py:19
  76.5 3.6 %all-to-all-start.2 = ((bf16[4,4,4,2,24,384]{5,4,3,1,2,0:T(8,128)(2,1)}), bf16[4,4,4,2,24,384]{5,4,3,1,2,0:T(8,128)(2,1)S(1)}, u32[]{:S(2)}, u32[]{:S(2)}) async-start(bf16[4,4,4,2,24,384]{5,4,3,1,2,0:T(8,128)(2,1)} %broadcast_in_dim.67), calls=%async_computation.2 | async-start | bytes 4718592 | tf_op jit(solution)/shard_map/all_to_all | solution.py:19
  80.1 2.8 %collective-permute-start.4 = (bf16[4,4,2,24,288]{4,3,2,1,0:T(8,128)(2,1)}, bf16[4,4,2,24,288]{4,3,2,1,0:T(8,128)(2,1)S(1)}, u32[]{:S(2)}, u32[]{:S(2)}) collective-permute-start(bf16[4,4,2,24,288]{4,3,2,1,0:T(8,128)(2,1)} %copy-done.3), channel_id=1, source_target_pairs={{0,64},{64,128},{128,192},{192,256},{256,320},{320,384},{384,448},... | collective-permute-start | bytes 1327112 | tf_op jit(solution)/shard_map/ppermute | solution.py:24
  82.9 4.1 %collective-permute-start.5 = (bf16[4,4,2,24,288]{4,3,2,1,0:T(8,128)(2,1)}, bf16[4,4,2,24,288]{4,3,2,1,0:T(8,128)(2,1)S(1)}, u32[]{:S(2)}, u32[]{:S(2)}) collective-permute-start(bf16[4,4,2,24,288]{4,3,2,1,0:T(8,128)(2,1)} %copy-done.3), channel_id=1, source_target_pairs={{0,960},{64,0},{128,64},{192,128},{256,192},{320,256},{384,320},{4... | collective-permute-start | bytes 1327112 | tf_op jit(solution)/shard_map/ppermute | solution.py:24
  87.0 6.2 %collective-permute-start.8 = (bf16[4,4,2,24,288]{4,3,2,1,0:T(8,128)(2,1)}, bf16[4,4,2,24,288]{4,3,2,1,0:T(8,128)(2,1)}, u32[]{:S(2)}, u32[]{:S(2)}) collective-permute-start(bf16[4,4,2,24,288]{4,3,2,1,0:T(8,128)(2,1)} %copy-done.3), channel_id=1, source_target_pairs={{0,896},{1,129},{64,960},{65,193},{128,0},{129,257},{192,64},{193,... | collective-permute-start | bytes 1327112 | tf_op jit(solution)/shard_map/ppermute | solution.py:34
  93.2 2.7 %broadcast_in_dim.62 = bf16[4,4,2,4,24,672]{5,4,3,2,1,0:T(8,128)(2,1)} broadcast(bf16[]{:T(256)} %constant.175.clone.1), dimensions={} | broadcast | bytes 4128770 | tf_op jit(solution)/shard_map/broadcast_in_dim | solution.py:102
  99.3 4.4 %collective-permute-start.3 = (bf16[4,48,3200]{2,1,0:T(8,128)(2,1)}, bf16[4,48,3200]{2,1,0:T(8,128)(2,1)}, u32[]{:S(2)}, u32[]{:S(2)}) collective-permute-start(bf16[4,48,3200]{2,1,0:T(8,128)(2,1)} %maximum_select_fusion.1), channel_id=1, source_target_pairs={{0,1},{1,0},{2,3},{3,2},{4,5},{5,4},{6,7},{7,6},{8,9},{9,8},{10,11... | collective-permute-start | bytes 3686408 | tf_op jit(solution)/shard_map/ppermute | solution.py:95
  104.1 1.7 pad_maximum_fusion
  107.6 1.8 %copy_dynamic-update-slice_fusion = bf16[4,4,2,4,24,672]{5,4,3,2,1,0:T(8,128)(2,1)} fusion(bf16[4,4,2,4,24,672]{5,4,3,2,1,0:T(8,128)(2,1)} %copy_dynamic-update-slice_fusion.2, bf16[4,4,4,2,24,384]{5,4,3,1,2,0:T(8,128)(2,1)S(1)} %all-to-all-done.2), kind=kLoop, calls=%fused_computation.6 | loop fusion | bytes 4718592 | tf_op jit(solution)/shard_map/scatter | solution.py:113
  109.4 3.4 %collective-permute-done.8 = bf16[4,4,2,24,288]{4,3,2,1,0:T(8,128)(2,1)} collective-permute-done((bf16[4,4,2,24,288]{4,3,2,1,0:T(8,128)(2,1)}, bf16[4,4,2,24,288]{4,3,2,1,0:T(8,128)(2,1)}, u32[]{:S(2)}, u32[]{:S(2)}) %collective-permute-start.8) | collective-permute-done | bytes 442400 | tf_op jit(solution)/shard_map/ppermute | solution.py:34
  112.8 2.0 %copy_dynamic-update-slice_fusion.1 = bf16[4,4,2,4,24,672]{5,4,3,2,1,0:T(8,128)(2,1)} fusion(bf16[4,4,2,4,24,672]{5,4,3,2,1,0:T(8,128)(2,1)} %copy_dynamic-update-slice_fusion, s32[]{:T(128)S(6)} %select_n.246, bf16[4,4,2,24,288]{4,3,2,1,0:T(8,128)(2,1)} %collective-permute-done.8), kind=kLoop, calls=%fused_computation.32 | loop fusion | bytes 1179652 | tf_op jit(solution)/shard_map/dynamic_update_slice | solution.py:108
  118.0 6.4 %fusion.7 = (bf16[384,672]{0,1:T(8,128)(2,1)}, f32[384,672]{0,1:T(8,128)S(1)}) fusion(bf16[384,672]{0,1:T(8,128)(2,1)S(1)} %copy-done.8, f32[384]{0:T(512)S(1)} %convert_reduce_fusion, bf16[3072,672]{1,0:T(8,128)(2,1)} %bitcast.25, bf16[384,3200]{1,0:T(8,128)(2,1)} %bitcast.91), kind=kOutput, calls=%fused_computation.18 | convolution fusion | flops 1587511296 | bytes 9143808 | tf_op jit(solution)/shard_map/dot_general | solution.py:117
  124.4 4.7 %convolution_convert_fusion = bf16[384,3072]{1,0:T(8,128)(2,1)S(1)} fusion(bf16[3072,672]{1,0:T(8,128)(2,1)} %bitcast.25, bf16[384,672]{0,1:T(8,128)(2,1)S(1)} %copy-done.8, f32[384,672]{0,1:T(8,128)S(1)} %get-tuple-element.37, bf16[384,672]{0,1:T(8,128)(2,1)S(1)} %copy-done.9, pred[384]{0:T(512)(128)(4,1)S(1)} %compare_reduce_fusion), kind=kOutput, calls=%fused_computation | convolution fusion | flops 1589981184 | bytes 8552832 | tf_op jit(solution)/shard_map/dot_general | solution.py:135
  130.3 7.7 %collective-permute-start.9 = (bf16[2,2,48,1536]{3,2,0,1:T(8,128)(2,1)}, bf16[2,2,48,1536]{3,2,0,1:T(8,128)(2,1)S(1)}, u32[]{:S(2)}, u32[]{:S(2)}) collective-permute-start(bf16[2,2,48,1536]{3,2,0,1:T(8,128)(2,1)} %bitcast.89), channel_id=1, source_target_pairs={{0,1},{1,0},{2,3},{3,2},{4,5},{5,4},{6,7},{7,6},{8,9},{9,8},{10,11... | collective-permute-start | bytes 1769480 | tf_op jit(solution)/shard_map/ppermute | solution.py:139
  138.0 1.9 %collective-permute-start.12 = (bf16[2,2,48,1536]{3,2,1,0:T(8,128)(2,1)S(1)}, bf16[2,2,48,1536]{3,2,1,0:T(8,128)(2,1)S(1)}, u32[]{:S(2)}, u32[]{:S(2)}) collective-permute-start(bf16[2,2,48,1536]{3,2,1,0:T(8,128)(2,1)S(1)} %dynamic-slice_bitcast_fusion), channel_id=1, source_target_pairs={{0,1},{1,0},{2,3},{3,2},{4,5},{5,4},{6,7},{7,6},{8,9},{9,8},{10,11... | collective-permute-start | bytes 1769480 | tf_op jit(solution)/shard_map/ppermute | solution.py:139
  140.1 1.9 %collective-permute-start.10 = (bf16[2,48,1536]{2,1,0:T(8,128)(2,1)S(1)}, bf16[2,48,1536]{2,1,0:T(8,128)(2,1)S(1)}, u32[]{:S(2)}, u32[]{:S(2)}) collective-permute-start(bf16[2,48,1536]{2,1,0:T(8,128)(2,1)S(1)} %dynamic-slice_bitcast_fusion.2), channel_id=1, source_target_pairs={{0,2},{2,0},{4,6},{6,4},{1,3},{3,1},{5,7},{7,5},{8,10},{10,8},{12,... | collective-permute-start | bytes 884744 | tf_op jit(solution)/shard_map/ppermute | solution.py:141
  142.3 3.4 %collective-permute-start.13 = (bf16[2,48,1536]{2,1,0:T(8,128)(2,1)S(1)}, bf16[2,48,1536]{2,1,0:T(8,128)(2,1)S(1)}, u32[]{:S(2)}, u32[]{:S(2)}) collective-permute-start(bf16[2,48,1536]{2,1,0:T(8,128)(2,1)S(1)} %dynamic-slice_bitcast_fusion.1), channel_id=1, source_target_pairs={{0,2},{2,0},{4,6},{6,4},{1,3},{3,1},{5,7},{7,5},{8,10},{10,8},{12,... | collective-permute-start | bytes 884744 | tf_op jit(solution)/shard_map/ppermute | solution.py:141
  145.6 4.5 %collective-permute-done.10 = bf16[2,48,1536]{2,1,0:T(8,128)(2,1)S(1)} collective-permute-done((bf16[2,48,1536]{2,1,0:T(8,128)(2,1)S(1)}, bf16[2,48,1536]{2,1,0:T(8,128)(2,1)S(1)}, u32[]{:S(2)}, u32[]{:S(2)}) %collective-permute-start.10) | collective-permute-done | bytes 294944 | tf_op jit(solution)/shard_map/ppermute | solution.py:141
  150.2 1.9 %collective-permute-start.11 = (bf16[48,1536]{1,0:T(8,128)(2,1)S(1)}, bf16[48,1536]{1,0:T(8,128)(2,1)S(1)}, u32[]{:S(2)}, u32[]{:S(2)}) collective-permute-start(bf16[48,1536]{1,0:T(8,128)(2,1)S(1)} %dynamic-slice_bitcast_fusion.4), channel_id=1, source_target_pairs={{0,4},{2,6},{4,0},{6,2},{1,5},{3,7},{5,1},{7,3},{8,12},{10,14},{12... | collective-permute-start | bytes 442376 | tf_op jit(solution)/shard_map/ppermute | solution.py:143
  152.1 5.4 %collective-permute-done.13 = bf16[2,48,1536]{2,1,0:T(8,128)(2,1)S(1)} collective-permute-done((bf16[2,48,1536]{2,1,0:T(8,128)(2,1)S(1)}, bf16[2,48,1536]{2,1,0:T(8,128)(2,1)S(1)}, u32[]{:S(2)}, u32[]{:S(2)}) %collective-permute-start.13) | collective-permute-done | bytes 294944 | tf_op jit(solution)/shard_map/ppermute | solution.py:141
  157.7 1.9 %collective-permute-start.14 = (bf16[48,1536]{1,0:T(8,128)(2,1)S(1)}, bf16[48,1536]{1,0:T(8,128)(2,1)S(1)}, u32[]{:S(2)}, u32[]{:S(2)}) collective-permute-start(bf16[48,1536]{1,0:T(8,128)(2,1)S(1)} %dynamic-slice_bitcast_fusion.3), channel_id=1, source_target_pairs={{0,4},{2,6},{4,0},{6,2},{1,5},{3,7},{5,1},{7,3},{8,12},{10,14},{12... | collective-permute-start | bytes 442376 | tf_op jit(solution)/shard_map/ppermute | solution.py:143
  160.9 6.8 %collective-permute-done.14 = bf16[48,1536]{1,0:T(8,128)(2,1)S(1)} collective-permute-done((bf16[48,1536]{1,0:T(8,128)(2,1)S(1)}, bf16[48,1536]{1,0:T(8,128)(2,1)S(1)}, u32[]{:S(2)}, u32[]{:S(2)}) %collective-permute-start.14) | collective-permute-done | bytes 147488 | tf_op jit(solution)/shard_map/ppermute | solution.py:143
  (77 shorter events, 18.2 us)
Async XLA Ops:
  0.6 27.2 %copy-start = (bf16[128,3072]{1,0:T(8,128)(2,1)S(1)}, bf16[128,3072]{1,0:T(8,128)(2,1)}, u32[]{:S(2)}) copy-start(bf16[128,3072]{1,0:T(8,128)(2,1)} %param.8) | copy-start | bytes 2359300
  0.6 27.5 %copy-start.10 = (bf16[128]{0:T(256)(128)(2,1)S(1)}, bf16[128]{0:T(256)(128)(2,1)}, u32[]{:S(2)}) copy-start(bf16[128]{0:T(256)(128)(2,1)} %param.9) | copy-start | bytes 772
  2.2 50.1 %all-to-all-start = ((bf16[8,24,672]{2,1,0:T(8,128)(2,1)}), bf16[8,24,672]{2,1,0:T(8,128)(2,1)S(1)}, u32[]{:S(2)}, u32[]{:S(2)}) async-start(bf16[8,24,672]{2,1,0:T(8,128)(2,1)} %broadcast_in_dim.59), calls=%async_computation | async-start | bytes 589824 | tf_op jit(solution)/shard_map/all_to_all | solution.py:19
  28.4 23.9 %collective-permute-start = (bf16[48,3200]{1,0:T(8,128)(2,1)S(1)}, bf16[48,3200]{1,0:T(8,128)(2,1)S(1)}, u32[]{:S(2)}, u32[]{:S(2)}) collective-permute-start(bf16[48,3200]{1,0:T(8,128)(2,1)S(1)} %get-tuple-element.35), channel_id=1, source_target_pairs={{0,4},{2,6},{4,0},{6,2},{1,5},{3,7},{5,1},{7,3},{8,12},{10,14},{12... | collective-permute-start | bytes 921608 | tf_op jit(solution)/shard_map/ppermute | solution.py:77
  52.3 15.1 %collective-permute-start.1 = (bf16[4,2,24,384]{3,2,1,0:T(8,128)(2,1)S(1)}, bf16[4,2,24,384]{3,2,1,0:T(8,128)(2,1)S(1)}, u32[]{:S(2)}, u32[]{:S(2)}) collective-permute-start(bf16[4,2,24,384]{3,2,1,0:T(8,128)(2,1)S(1)} %slice.74), channel_id=1, source_target_pairs={{0,896},{1,129},{64,960},{65,193},{128,0},{129,257},{192,64},{193,... | collective-permute-start | bytes 442376 | tf_op jit(solution)/shard_map/ppermute | solution.py:34
  56.5 17.0 %collective-permute-start.6 = (bf16[4,2,24,384]{3,2,1,0:T(8,128)(2,1)S(1)}, bf16[4,2,24,384]{3,2,1,0:T(8,128)(2,1)S(1)}, u32[]{:S(2)}, u32[]{:S(2)}) collective-permute-start(bf16[4,2,24,384]{3,2,1,0:T(8,128)(2,1)S(1)} %slice.74), channel_id=1, source_target_pairs={{0,960},{64,0},{128,64},{192,128},{256,192},{320,256},{384,320},{4... | collective-permute-start | bytes 442376 | tf_op jit(solution)/shard_map/ppermute | solution.py:24
  60.6 13.0 %collective-permute-start.7 = (bf16[4,2,24,384]{3,2,1,0:T(8,128)(2,1)S(1)}, bf16[4,2,24,384]{3,2,1,0:T(8,128)(2,1)S(1)}, u32[]{:S(2)}, u32[]{:S(2)}) collective-permute-start(bf16[4,2,24,384]{3,2,1,0:T(8,128)(2,1)S(1)} %slice.74), channel_id=1, source_target_pairs={{0,64},{64,128},{128,192},{192,256},{256,320},{320,384},{384,448},... | collective-permute-start | bytes 442376 | tf_op jit(solution)/shard_map/ppermute | solution.py:24
  63.4 11.3 %all-to-all-start.1 = ((bf16[4,4,2,24,288]{4,3,2,1,0:T(8,128)(2,1)}), bf16[4,4,2,24,288]{4,3,2,1,0:T(8,128)(2,1)S(1)}, u32[]{:S(2)}, u32[]{:S(2)}) async-start(bf16[4,4,2,24,288]{4,3,2,1,0:T(8,128)(2,1)} %broadcast_in_dim.63), calls=%async_computation.1 | async-start | bytes 1179648 | tf_op jit(solution)/shard_map/all_to_all | solution.py:19
  69.6 27.2 %collective-permute-start.2 = (bf16[2,48,3200]{2,1,0:T(8,128)(2,1)}, bf16[2,48,3200]{2,1,0:T(8,128)(2,1)}, u32[]{:S(2)}, u32[]{:S(2)}) collective-permute-start(bf16[2,48,3200]{2,1,0:T(8,128)(2,1)} %maximum_select_fusion.2), channel_id=1, source_target_pairs={{0,2},{2,0},{4,6},{6,4},{1,3},{3,1},{5,7},{7,5},{8,10},{10,8},{12,... | collective-permute-start | bytes 1843208 | tf_op jit(solution)/shard_map/ppermute | solution.py:84
  74.7 1.8 %copy-start.3 = (bf16[4,4,2,24,288]{4,3,2,1,0:T(8,128)(2,1)}, bf16[4,4,2,24,288]{4,3,2,1,0:T(8,128)(2,1)S(1)}, u32[]{:S(2)}) copy-start(bf16[4,4,2,24,288]{4,3,2,1,0:T(8,128)(2,1)S(1)} %all-to-all-done.1) | copy-start | bytes 1327108
  76.5 31.1 %all-to-all-start.2 = ((bf16[4,4,4,2,24,384]{5,4,3,1,2,0:T(8,128)(2,1)}), bf16[4,4,4,2,24,384]{5,4,3,1,2,0:T(8,128)(2,1)S(1)}, u32[]{:S(2)}, u32[]{:S(2)}) async-start(bf16[4,4,4,2,24,384]{5,4,3,1,2,0:T(8,128)(2,1)} %broadcast_in_dim.67), calls=%async_computation.2 | async-start | bytes 4718592 | tf_op jit(solution)/shard_map/all_to_all | solution.py:19
  80.1 15.8 %copy-start.4 = (bf16[4,4,2,24,288]{4,3,2,1,0:T(8,128)(2,1)S(1)}, bf16[4,4,2,24,288]{4,3,2,1,0:T(8,128)(2,1)}, u32[]{:S(2)}) copy-start(bf16[4,4,2,24,288]{4,3,2,1,0:T(8,128)(2,1)} %copy-done.3) | copy-start | bytes 1327108
  80.1 25.6 %collective-permute-start.4 = (bf16[4,4,2,24,288]{4,3,2,1,0:T(8,128)(2,1)}, bf16[4,4,2,24,288]{4,3,2,1,0:T(8,128)(2,1)S(1)}, u32[]{:S(2)}, u32[]{:S(2)}) collective-permute-start(bf16[4,4,2,24,288]{4,3,2,1,0:T(8,128)(2,1)} %copy-done.3), channel_id=1, source_target_pairs={{0,64},{64,128},{128,192},{192,256},{256,320},{320,384},{384,448},... | collective-permute-start | bytes 1327112 | tf_op jit(solution)/shard_map/ppermute | solution.py:24
  82.9 23.8 %collective-permute-start.5 = (bf16[4,4,2,24,288]{4,3,2,1,0:T(8,128)(2,1)}, bf16[4,4,2,24,288]{4,3,2,1,0:T(8,128)(2,1)S(1)}, u32[]{:S(2)}, u32[]{:S(2)}) collective-permute-start(bf16[4,4,2,24,288]{4,3,2,1,0:T(8,128)(2,1)} %copy-done.3), channel_id=1, source_target_pairs={{0,960},{64,0},{128,64},{192,128},{256,192},{320,256},{384,320},{4... | collective-permute-start | bytes 1327112 | tf_op jit(solution)/shard_map/ppermute | solution.py:24
  87.0 25.8 %collective-permute-start.8 = (bf16[4,4,2,24,288]{4,3,2,1,0:T(8,128)(2,1)}, bf16[4,4,2,24,288]{4,3,2,1,0:T(8,128)(2,1)}, u32[]{:S(2)}, u32[]{:S(2)}) collective-permute-start(bf16[4,4,2,24,288]{4,3,2,1,0:T(8,128)(2,1)} %copy-done.3), channel_id=1, source_target_pairs={{0,896},{1,129},{64,960},{65,193},{128,0},{129,257},{192,64},{193,... | collective-permute-start | bytes 1327112 | tf_op jit(solution)/shard_map/ppermute | solution.py:34
  95.9 2.0 %copy-start.6 = (bf16[1,48,3200]{2,1,0:T(8,128)(2,1)S(1)}, bf16[1,48,3200]{2,1,0:T(8,128)(2,1)}, u32[]{:S(2)}) copy-start(bf16[1,48,3200]{2,1,0:T(8,128)(2,1)} %get-tuple-element.26) | copy-start | bytes 921604
  95.9 2.1 %copy-start.7 = (bf16[1,48,3200]{2,1,0:T(8,128)(2,1)S(1)}, bf16[1,48,3200]{2,1,0:T(8,128)(2,1)}, u32[]{:S(2)}) copy-start(bf16[1,48,3200]{2,1,0:T(8,128)(2,1)} %get-tuple-element.29) | copy-start | bytes 921604
  98.0 5.8 %copy-start.5 = (bf16[1,1,48,3200]{3,2,1,0:T(8,128)(2,1)S(1)}, bf16[1,1,48,3200]{3,2,1,0:T(8,128)(2,1)}, u32[]{:S(2)}) copy-start(bf16[1,1,48,3200]{3,2,1,0:T(8,128)(2,1)} %get-tuple-element.28) | copy-start | bytes 921604
  99.3 15.5 %collective-permute-start.3 = (bf16[4,48,3200]{2,1,0:T(8,128)(2,1)}, bf16[4,48,3200]{2,1,0:T(8,128)(2,1)}, u32[]{:S(2)}, u32[]{:S(2)}) collective-permute-start(bf16[4,48,3200]{2,1,0:T(8,128)(2,1)} %maximum_select_fusion.1), channel_id=1, source_target_pairs={{0,1},{1,0},{2,3},{3,2},{4,5},{5,4},{6,7},{7,6},{8,9},{9,8},{10,11... | collective-permute-start | bytes 3686408 | tf_op jit(solution)/shard_map/ppermute | solution.py:95
  107.6 7.2 %copy-start.1 = (bf16[4,2,48,3200]{3,2,1,0:T(8,128)(2,1)S(1)}, bf16[4,2,48,3200]{3,2,1,0:T(8,128)(2,1)}, u32[]{:S(2)}) copy-start(bf16[4,2,48,3200]{3,2,1,0:T(8,128)(2,1)} %pad_maximum_fusion) | copy-start | bytes 7372804
  114.8 3.2 %copy-start.8 = (bf16[384,672]{0,1:T(8,128)(2,1)S(1)}, bf16[384,672]{0,1:T(8,128)(2,1)}, u32[]{:S(2)}) copy-start(bf16[384,672]{0,1:T(8,128)(2,1)} %param.12) | copy-start | bytes 1548292
  116.3 1.5 copy-start.2
  118.0 6.4 %copy-start.9 = (bf16[384,672]{0,1:T(8,128)(2,1)S(1)}, bf16[384,672]{0,1:T(8,128)(2,1)}, u32[]{:S(2)}) copy-start(bf16[384,672]{0,1:T(8,128)(2,1)} %param.13) | copy-start | bytes 1548292
  130.3 9.7 %collective-permute-start.9 = (bf16[2,2,48,1536]{3,2,0,1:T(8,128)(2,1)}, bf16[2,2,48,1536]{3,2,0,1:T(8,128)(2,1)S(1)}, u32[]{:S(2)}, u32[]{:S(2)}) collective-permute-start(bf16[2,2,48,1536]{3,2,0,1:T(8,128)(2,1)} %bitcast.89), channel_id=1, source_target_pairs={{0,1},{1,0},{2,3},{3,2},{4,5},{5,4},{6,7},{7,6},{8,9},{9,8},{10,11... | collective-permute-start | bytes 1769480 | tf_op jit(solution)/shard_map/ppermute | solution.py:139
  138.0 4.1 %collective-permute-start.12 = (bf16[2,2,48,1536]{3,2,1,0:T(8,128)(2,1)S(1)}, bf16[2,2,48,1536]{3,2,1,0:T(8,128)(2,1)S(1)}, u32[]{:S(2)}, u32[]{:S(2)}) collective-permute-start(bf16[2,2,48,1536]{3,2,1,0:T(8,128)(2,1)S(1)} %dynamic-slice_bitcast_fusion), channel_id=1, source_target_pairs={{0,1},{1,0},{2,3},{3,2},{4,5},{5,4},{6,7},{7,6},{8,9},{9,8},{10,11... | collective-permute-start | bytes 1769480 | tf_op jit(solution)/shard_map/ppermute | solution.py:139
  140.1 10.0 %collective-permute-start.10 = (bf16[2,48,1536]{2,1,0:T(8,128)(2,1)S(1)}, bf16[2,48,1536]{2,1,0:T(8,128)(2,1)S(1)}, u32[]{:S(2)}, u32[]{:S(2)}) collective-permute-start(bf16[2,48,1536]{2,1,0:T(8,128)(2,1)S(1)} %dynamic-slice_bitcast_fusion.2), channel_id=1, source_target_pairs={{0,2},{2,0},{4,6},{6,4},{1,3},{3,1},{5,7},{7,5},{8,10},{10,8},{12,... | collective-permute-start | bytes 884744 | tf_op jit(solution)/shard_map/ppermute | solution.py:141
  142.3 15.3 %collective-permute-start.13 = (bf16[2,48,1536]{2,1,0:T(8,128)(2,1)S(1)}, bf16[2,48,1536]{2,1,0:T(8,128)(2,1)S(1)}, u32[]{:S(2)}, u32[]{:S(2)}) collective-permute-start(bf16[2,48,1536]{2,1,0:T(8,128)(2,1)S(1)} %dynamic-slice_bitcast_fusion.1), channel_id=1, source_target_pairs={{0,2},{2,0},{4,6},{6,4},{1,3},{3,1},{5,7},{7,5},{8,10},{10,8},{12,... | collective-permute-start | bytes 884744 | tf_op jit(solution)/shard_map/ppermute | solution.py:141
  150.2 10.6 %collective-permute-start.11 = (bf16[48,1536]{1,0:T(8,128)(2,1)S(1)}, bf16[48,1536]{1,0:T(8,128)(2,1)S(1)}, u32[]{:S(2)}, u32[]{:S(2)}) collective-permute-start(bf16[48,1536]{1,0:T(8,128)(2,1)S(1)} %dynamic-slice_bitcast_fusion.4), channel_id=1, source_target_pairs={{0,4},{2,6},{4,0},{6,2},{1,5},{3,7},{5,1},{7,3},{8,12},{10,14},{12... | collective-permute-start | bytes 442376 | tf_op jit(solution)/shard_map/ppermute | solution.py:143
  157.7 10.0 %collective-permute-start.14 = (bf16[48,1536]{1,0:T(8,128)(2,1)S(1)}, bf16[48,1536]{1,0:T(8,128)(2,1)S(1)}, u32[]{:S(2)}, u32[]{:S(2)}) collective-permute-start(bf16[48,1536]{1,0:T(8,128)(2,1)S(1)} %dynamic-slice_bitcast_fusion.3), channel_id=1, source_target_pairs={{0,4},{2,6},{4,0},{6,2},{1,5},{3,7},{5,1},{7,3},{8,12},{10,14},{12... | collective-permute-start | bytes 442376 | tf_op jit(solution)/shard_map/ppermute | solution.py:143

commit v7 on v6

--- a/solution.py
+++ b/solution.py
@@ -77,7 +77,7 @@
     opposite = lax.ppermute(sent, "yl", by_two)
 
     far = everyone(weight, ("za", "yh")).reshape(4, 2, depth, width)
-    far, opposite = lax.optimization_barrier((far, opposite))
+
     one, two = far[..., :cut], far[..., cut:]
     beside = (along_z(one, 1), along_z(one, -1), two_along_z(one))
     two_rows = in_order(sent, opposite, (yl + nothing(beside[2])) // 2)

time: 170 us -> 166 us (0.976)
  waiting for transfers between devices: 43.7 us -> 31.8 us
  starting transfers between devices: 82.7 us -> 88.4 us
    ppermute x1, waiting for transfers between devices: 21.5 us -> 0.01 us  [body(): opposite = lax.ppermute(sent, 'yl', by_two)]
    all_to_all x3, waiting for transfers between devices: 0.89 us -> 12.6 us  [everyone(): lax.all_to_all(jnp.broadcast_to(part[None], (count,) + part.shape), axes,...]
    ppermute x1, starting transfers between devices: 4.4 us -> 6.71 us  [body(): theirs = lax.ppermute(four_rows, 'core', [(0, 1), (1, 0)])]
    ppermute x4, starting transfers between devices: 12.9 us -> 15 us  [along_z(): return lax.ppermute(part, ('za', 'zb'), shifted(za, zb, by))]
  transfers between devices with their start and end apart: 18 -> 18, of which waited for: 7 -> 6; matrix products, arithmetic and copies ran while one was open for 13% -> 14% of each run, Pallas kernels for 0% -> 0%
where the time goes in v7:
time: 166 us; the launch traced here: 164 us
  starting transfers between devices  88.4 us (53%)
  waiting for transfers between devices  31.8 us (19%)
  local copies, waits for them, and re-layouts  22.5 us (14%)
  matrix products  13.5 us (8%)
  other arithmetic  6.1 us (4%)
  between operations  1.91 us (1%)
    all_to_all x3, starting transfers between devices, everyone(): lax.all_to_all(jnp.broadcast_to(part[None], (count,) + part.shape), axes,...  32.5 us
    ppermute x4, starting transfers between devices, along_z(): return lax.ppermute(part, ('za', 'zb'), shifted(za, zb, by))  15 us
    all_to_all x3, waiting for transfers between devices, everyone(): lax.all_to_all(jnp.broadcast_to(part[None], (count,) + part.shape), axes,...  12.6 us
    ppermute x2, starting transfers between devices, two_along_z(): return lax.ppermute(part, ('za', 'zb', 'core'), pairs)  11.6 us
    ppermute x2, waiting for transfers between devices, returned(): near = lax.ppermute(pick(pair, 1, 1 - yl % 2), 'yl', by_one)  9.91 us
    ppermute x2, starting transfers between devices, returned(): swapped = lax.ppermute(pick(part, 2, 1 - core), 'core', [(0, 1), (1, 0)])  8.24 us
    ppermute x2, waiting for transfers between devices, returned(): far = lax.ppermute(pick(four, 0, 1 - yl // 2), 'yl', by_two)  7.35 us
    ppermute x1, starting transfers between devices, body(): theirs = lax.ppermute(four_rows, 'core', [(0, 1), (1, 0)])  6.71 us
  transfers between devices with their start and end apart: 18, of which 6 were waited for; matrix products, arithmetic and copies ran while one was open for 14% of the time, Pallas kernels for 0%

profile of v7, /device:TPU:1, one launch (start us, length us, event | category | flops | bytes accessed | tf_op | source)
XLA Modules:
  0.0 164.2 jit_solution(7752070379607035212)
XLA Ops:
  0.6 1.6 broadcast_in_dim.59
  2.2 24.5 %all-to-all-start = ((bf16[8,24,672]{2,1,0:T(8,128)(2,1)}), bf16[8,24,672]{2,1,0:T(8,128)(2,1)S(1)}, u32[]{:S(2)}, u32[]{:S(2)}) async-start(bf16[8,24,672]{2,1,0:T(8,128)(2,1)} %broadcast_in_dim.59), calls=%async_computation | async-start | bytes 589824 | tf_op jit(solution)/shard_map/all_to_all | solution.py:19
  29.0 2.4 %collective-permute-start.1 = (bf16[48,3200]{1,0:T(8,128)(2,1)S(1)}, bf16[48,3200]{1,0:T(8,128)(2,1)S(1)}, u32[]{:S(2)}, u32[]{:S(2)}) collective-permute-start(bf16[48,3200]{1,0:T(8,128)(2,1)S(1)} %get-tuple-element.31), channel_id=1, source_target_pairs={{0,4},{2,6},{4,0},{6,2},{1,5},{3,7},{5,1},{7,3},{8,12},{10,14},{12... | collective-permute-start | bytes 921608 | tf_op jit(solution)/shard_map/ppermute | solution.py:77
  31.5 12.3 %all-to-all-done = bf16[8,24,672]{2,1,0:T(8,128)(2,1)S(1)} async-done(((bf16[8,24,672]{2,1,0:T(8,128)(2,1)}), bf16[8,24,672]{2,1,0:T(8,128)(2,1)S(1)}, u32[]{:S(2)}, u32[]{:S(2)}) %all-to-all-start) | async-done | bytes 258080 | tf_op jit(solution)/shard_map/all_to_all | solution.py:19
  44.5 9.7 %collective-permute-start = (bf16[4,2,24,384]{3,2,1,0:T(8,128)(2,1)}, bf16[4,2,24,384]{3,2,1,0:T(8,128)(2,1)S(1)}, u32[]{:S(2)}, u32[]{:S(2)}) collective-permute-start(bf16[4,2,24,384]{3,2,1,0:T(8,128)(2,1)} %slice.85), channel_id=1, source_target_pairs={{0,896},{1,129},{64,960},{65,193},{128,0},{129,257},{192,64},{193,... | collective-permute-start | bytes 442376 | tf_op jit(solution)/shard_map/ppermute | solution.py:34
  54.4 5.8 %collective-permute-start.6 = (bf16[4,2,24,384]{3,2,1,0:T(8,128)(2,1)}, bf16[4,2,24,384]{3,2,1,0:T(8,128)(2,1)S(1)}, u32[]{:S(2)}, u32[]{:S(2)}) collective-permute-start(bf16[4,2,24,384]{3,2,1,0:T(8,128)(2,1)} %slice.85), channel_id=1, source_target_pairs={{0,960},{64,0},{128,64},{192,128},{256,192},{320,256},{384,320},{4... | collective-permute-start | bytes 442376 | tf_op jit(solution)/shard_map/ppermute | solution.py:24
  60.1 1.9 %collective-permute-start.7 = (bf16[4,2,24,384]{3,2,1,0:T(8,128)(2,1)}, bf16[4,2,24,384]{3,2,1,0:T(8,128)(2,1)S(1)}, u32[]{:S(2)}, u32[]{:S(2)}) collective-permute-start(bf16[4,2,24,384]{3,2,1,0:T(8,128)(2,1)} %slice.85), channel_id=1, source_target_pairs={{0,64},{64,128},{128,192},{192,256},{256,320},{320,384},{384,448},... | collective-permute-start | bytes 442376 | tf_op jit(solution)/shard_map/ppermute | solution.py:24
  62.9 4.0 %all-to-all-start.1 = ((bf16[4,4,2,24,288]{4,3,2,1,0:T(8,128)(2,1)}), bf16[4,4,2,24,288]{4,3,2,1,0:T(8,128)(2,1)S(1)}, u32[]{:S(2)}, u32[]{:S(2)}) async-start(bf16[4,4,2,24,288]{4,3,2,1,0:T(8,128)(2,1)} %broadcast_in_dim.63), calls=%async_computation.1 | async-start | bytes 1179648 | tf_op jit(solution)/shard_map/all_to_all | solution.py:19
  69.1 2.5 %collective-permute-start.2 = (bf16[2,48,3200]{2,1,0:T(8,128)(2,1)}, bf16[2,48,3200]{2,1,0:T(8,128)(2,1)}, u32[]{:S(2)}, u32[]{:S(2)}) collective-permute-start(bf16[2,48,3200]{2,1,0:T(8,128)(2,1)} %maximum_select_fusion.2), channel_id=1, source_target_pairs={{0,2},{2,0},{4,6},{6,4},{1,3},{3,1},{5,7},{7,5},{8,10},{10,8},{12,... | collective-permute-start | bytes 1843208 | tf_op jit(solution)/shard_map/ppermute | solution.py:84
  71.7 2.0 %fusion.39 = (bf16[1,48,3200]{2,1,0:T(8,128)(2,1)}, bf16[1,1,48,3200]{3,2,1,0:T(8,128)(2,1)S(1)}, bf16[1,1,48,3200]{3,2,1,0:T(8,128)(2,1)}, bf16[1,48,3200]{2,1,0:T(8,128)(2,1)}) fusion(bf16[2,48,3200]{2,1,0:T(8,128)(2,1)} %maximum_select_fusion.2), kind=kLoop, calls=%fused_computation.81 | loop fusion | bytes 1843200 | tf_op jit(solution)/shard_map/slice | solution.py:92
  74.3 1.8 %broadcast_in_dim.67 = bf16[4,4,4,2,24,384]{5,4,3,1,2,0:T(8,128)(2,1)} broadcast(bf16[4,4,2,24,384]{4,3,2,0,1:T(8,128)(2,1)S(1)} %copy.34), dimensions={1,2,3,4,5} | broadcast | bytes 2949120 | tf_op jit(solution)/shard_map/broadcast_in_dim | solution.py:19
  76.0 4.0 %all-to-all-start.2 = ((bf16[4,4,4,2,24,384]{5,4,3,1,2,0:T(8,128)(2,1)}), bf16[4,4,4,2,24,384]{5,4,3,1,2,0:T(8,128)(2,1)S(1)}, u32[]{:S(2)}, u32[]{:S(2)}) async-start(bf16[4,4,4,2,24,384]{5,4,3,1,2,0:T(8,128)(2,1)} %broadcast_in_dim.67), calls=%async_computation.2 | async-start | bytes 4718592 | tf_op jit(solution)/shard_map/all_to_all | solution.py:19
  80.0 2.0 %collective-permute-start.4 = (bf16[4,4,2,24,288]{4,3,2,1,0:T(8,128)(2,1)}, bf16[4,4,2,24,288]{4,3,2,1,0:T(8,128)(2,1)S(1)}, u32[]{:S(2)}, u32[]{:S(2)}) collective-permute-start(bf16[4,4,2,24,288]{4,3,2,1,0:T(8,128)(2,1)} %copy-done.3), channel_id=1, source_target_pairs={{0,64},{64,128},{128,192},{192,256},{256,320},{320,384},{384,448},... | collective-permute-start | bytes 1327112 | tf_op jit(solution)/shard_map/ppermute | solution.py:24
  82.1 5.2 %collective-permute-start.5 = (bf16[4,4,2,24,288]{4,3,2,1,0:T(8,128)(2,1)}, bf16[4,4,2,24,288]{4,3,2,1,0:T(8,128)(2,1)S(1)}, u32[]{:S(2)}, u32[]{:S(2)}) collective-permute-start(bf16[4,4,2,24,288]{4,3,2,1,0:T(8,128)(2,1)} %copy-done.3), channel_id=1, source_target_pairs={{0,960},{64,0},{128,64},{192,128},{256,192},{320,256},{384,320},{4... | collective-permute-start | bytes 1327112 | tf_op jit(solution)/shard_map/ppermute | solution.py:24
  87.3 1.9 %collective-permute-start.8 = (bf16[4,4,2,24,288]{4,3,2,1,0:T(8,128)(2,1)}, bf16[4,4,2,24,288]{4,3,2,1,0:T(8,128)(2,1)}, u32[]{:S(2)}, u32[]{:S(2)}) collective-permute-start(bf16[4,4,2,24,288]{4,3,2,1,0:T(8,128)(2,1)} %copy-done.3), channel_id=1, source_target_pairs={{0,896},{1,129},{64,960},{65,193},{128,0},{129,257},{192,64},{193,... | collective-permute-start | bytes 1327112 | tf_op jit(solution)/shard_map/ppermute | solution.py:34
  89.3 2.7 %broadcast_in_dim.62 = bf16[4,4,2,4,24,672]{5,4,3,2,1,0:T(8,128)(2,1)} broadcast(bf16[]{:T(256)} %constant.175.clone.1), dimensions={} | broadcast | bytes 4128770 | tf_op jit(solution)/shard_map/broadcast_in_dim | solution.py:102
  95.4 6.7 %collective-permute-start.3 = (bf16[4,48,3200]{2,1,0:T(8,128)(2,1)}, bf16[4,48,3200]{2,1,0:T(8,128)(2,1)}, u32[]{:S(2)}, u32[]{:S(2)}) collective-permute-start(bf16[4,48,3200]{2,1,0:T(8,128)(2,1)} %maximum_select_fusion.1), channel_id=1, source_target_pairs={{0,1},{1,0},{2,3},{3,2},{4,5},{5,4},{6,7},{7,6},{8,9},{9,8},{10,11... | collective-permute-start | bytes 3686408 | tf_op jit(solution)/shard_map/ppermute | solution.py:95
  102.4 1.7 %pad_maximum_fusion = bf16[4,2,48,3200]{3,2,1,0:T(8,128)(2,1)} fusion(bf16[4,1,48,3200]{3,2,1,0:T(8,128)(2,1)S(1)} %maximum_select_fusion), kind=kLoop, calls=%fused_computation.3 | loop fusion | flops 1228800 | bytes 3686400 | tf_op jit(solution)/shard_map/stack | solution.py:96
  106.0 1.8 %copy_dynamic-update-slice_fusion = bf16[4,4,2,4,24,672]{5,4,3,2,1,0:T(8,128)(2,1)} fusion(bf16[4,4,2,4,24,672]{5,4,3,2,1,0:T(8,128)(2,1)} %copy_dynamic-update-slice_fusion.2, bf16[4,4,4,2,24,384]{5,4,3,1,2,0:T(8,128)(2,1)S(1)} %all-to-all-done.2), kind=kLoop, calls=%fused_computation.6 | loop fusion | bytes 4718592 | tf_op jit(solution)/shard_map/scatter | solution.py:113
  107.9 1.9 %collective-permute-done.8 = bf16[4,4,2,24,288]{4,3,2,1,0:T(8,128)(2,1)} collective-permute-done((bf16[4,4,2,24,288]{4,3,2,1,0:T(8,128)(2,1)}, bf16[4,4,2,24,288]{4,3,2,1,0:T(8,128)(2,1)}, u32[]{:S(2)}, u32[]{:S(2)}) %collective-permute-start.8) | collective-permute-done | bytes 442400 | tf_op jit(solution)/shard_map/ppermute | solution.py:34
  109.7 2.0 %copy_dynamic-update-slice_fusion.1 = bf16[4,4,2,4,24,672]{5,4,3,2,1,0:T(8,128)(2,1)} fusion(bf16[4,4,2,4,24,672]{5,4,3,2,1,0:T(8,128)(2,1)} %copy_dynamic-update-slice_fusion, s32[]{:T(128)S(6)} %select_n.246, bf16[4,4,2,24,288]{4,3,2,1,0:T(8,128)(2,1)} %collective-permute-done.8), kind=kLoop, calls=%fused_computation.32 | loop fusion | bytes 1179652 | tf_op jit(solution)/shard_map/dynamic_update_slice | solution.py:108
  114.9 6.4 %fusion.7 = (bf16[384,672]{0,1:T(8,128)(2,1)}, f32[384,672]{0,1:T(8,128)S(1)}) fusion(bf16[384,672]{0,1:T(8,128)(2,1)S(1)} %copy-done.8, f32[384]{0:T(512)S(1)} %convert_reduce_fusion, bf16[3072,672]{1,0:T(8,128)(2,1)} %bitcast.25, bf16[384,3200]{1,0:T(8,128)(2,1)} %bitcast.91), kind=kOutput, calls=%fused_computation.18 | convolution fusion | flops 1587511296 | bytes 9143808 | tf_op jit(solution)/shard_map/dot_general | solution.py:117
  121.3 4.7 %convolution_convert_fusion = bf16[384,3072]{1,0:T(8,128)(2,1)S(1)} fusion(bf16[3072,672]{1,0:T(8,128)(2,1)} %bitcast.25, bf16[384,672]{0,1:T(8,128)(2,1)S(1)} %copy-done.8, f32[384,672]{0,1:T(8,128)S(1)} %get-tuple-element.33, bf16[384,672]{0,1:T(8,128)(2,1)S(1)} %copy-done.9, pred[384]{0:T(512)(128)(4,1)S(1)} %compare_reduce_fusion), kind=kOutput, calls=%fused_computation | convolution fusion | flops 1589981184 | bytes 8552832 | tf_op jit(solution)/shard_map/dot_general | solution.py:135
  127.1 6.3 %collective-permute-start.9 = (bf16[2,2,48,1536]{3,2,0,1:T(8,128)(2,1)}, bf16[2,2,48,1536]{3,2,0,1:T(8,128)(2,1)S(1)}, u32[]{:S(2)}, u32[]{:S(2)}) collective-permute-start(bf16[2,2,48,1536]{3,2,0,1:T(8,128)(2,1)} %bitcast.89), channel_id=1, source_target_pairs={{0,1},{1,0},{2,3},{3,2},{4,5},{5,4},{6,7},{7,6},{8,9},{9,8},{10,11... | collective-permute-start | bytes 1769480 | tf_op jit(solution)/shard_map/ppermute | solution.py:139
  133.6 1.9 %collective-permute-start.12 = (bf16[2,2,48,1536]{3,2,1,0:T(8,128)(2,1)S(1)}, bf16[2,2,48,1536]{3,2,1,0:T(8,128)(2,1)S(1)}, u32[]{:S(2)}, u32[]{:S(2)}) collective-permute-start(bf16[2,2,48,1536]{3,2,1,0:T(8,128)(2,1)S(1)} %dynamic-slice_bitcast_fusion), channel_id=1, source_target_pairs={{0,1},{1,0},{2,3},{3,2},{4,5},{5,4},{6,7},{7,6},{8,9},{9,8},{10,11... | collective-permute-start | bytes 1769480 | tf_op jit(solution)/shard_map/ppermute | solution.py:139
  135.7 2.1 %collective-permute-start.10 = (bf16[2,48,1536]{2,1,0:T(8,128)(2,1)S(1)}, bf16[2,48,1536]{2,1,0:T(8,128)(2,1)S(1)}, u32[]{:S(2)}, u32[]{:S(2)}) collective-permute-start(bf16[2,48,1536]{2,1,0:T(8,128)(2,1)S(1)} %dynamic-slice_bitcast_fusion.2), channel_id=1, source_target_pairs={{0,2},{2,0},{4,6},{6,4},{1,3},{3,1},{5,7},{7,5},{8,10},{10,8},{12,... | collective-permute-start | bytes 884744 | tf_op jit(solution)/shard_map/ppermute | solution.py:141
  138.0 3.1 %collective-permute-start.13 = (bf16[2,48,1536]{2,1,0:T(8,128)(2,1)S(1)}, bf16[2,48,1536]{2,1,0:T(8,128)(2,1)S(1)}, u32[]{:S(2)}, u32[]{:S(2)}) collective-permute-start(bf16[2,48,1536]{2,1,0:T(8,128)(2,1)S(1)} %dynamic-slice_bitcast_fusion.1), channel_id=1, source_target_pairs={{0,2},{2,0},{4,6},{6,4},{1,3},{3,1},{5,7},{7,5},{8,10},{10,8},{12,... | collective-permute-start | bytes 884744 | tf_op jit(solution)/shard_map/ppermute | solution.py:141
  141.2 4.5 %collective-permute-done.10 = bf16[2,48,1536]{2,1,0:T(8,128)(2,1)S(1)} collective-permute-done((bf16[2,48,1536]{2,1,0:T(8,128)(2,1)S(1)}, bf16[2,48,1536]{2,1,0:T(8,128)(2,1)S(1)}, u32[]{:S(2)}, u32[]{:S(2)}) %collective-permute-start.10) | collective-permute-done | bytes 294944 | tf_op jit(solution)/shard_map/ppermute | solution.py:141
  145.8 2.2 %collective-permute-start.11 = (bf16[48,1536]{1,0:T(8,128)(2,1)S(1)}, bf16[48,1536]{1,0:T(8,128)(2,1)S(1)}, u32[]{:S(2)}, u32[]{:S(2)}) collective-permute-start(bf16[48,1536]{1,0:T(8,128)(2,1)S(1)} %dynamic-slice_bitcast_fusion.4), channel_id=1, source_target_pairs={{0,4},{2,6},{4,0},{6,2},{1,5},{3,7},{5,1},{7,3},{8,12},{10,14},{12... | collective-permute-start | bytes 442376 | tf_op jit(solution)/shard_map/ppermute | solution.py:143
  148.0 5.4 %collective-permute-done.13 = bf16[2,48,1536]{2,1,0:T(8,128)(2,1)S(1)} collective-permute-done((bf16[2,48,1536]{2,1,0:T(8,128)(2,1)S(1)}, bf16[2,48,1536]{2,1,0:T(8,128)(2,1)S(1)}, u32[]{:S(2)}, u32[]{:S(2)}) %collective-permute-start.13) | collective-permute-done | bytes 294944 | tf_op jit(solution)/shard_map/ppermute | solution.py:141
  153.6 1.9 %collective-permute-start.14 = (bf16[48,1536]{1,0:T(8,128)(2,1)S(1)}, bf16[48,1536]{1,0:T(8,128)(2,1)S(1)}, u32[]{:S(2)}, u32[]{:S(2)}) collective-permute-start(bf16[48,1536]{1,0:T(8,128)(2,1)S(1)} %dynamic-slice_bitcast_fusion.3), channel_id=1, source_target_pairs={{0,4},{2,6},{4,0},{6,2},{1,5},{3,7},{5,1},{7,3},{8,12},{10,14},{12... | collective-permute-start | bytes 442376 | tf_op jit(solution)/shard_map/ppermute | solution.py:143
  155.5 7.3 %collective-permute-done.14 = bf16[48,1536]{1,0:T(8,128)(2,1)S(1)} collective-permute-done((bf16[48,1536]{1,0:T(8,128)(2,1)S(1)}, bf16[48,1536]{1,0:T(8,128)(2,1)S(1)}, u32[]{:S(2)}, u32[]{:S(2)}) %collective-permute-start.14) | collective-permute-done | bytes 147488 | tf_op jit(solution)/shard_map/ppermute | solution.py:143
  (75 shorter events, 17.8 us)
Async XLA Ops:
  0.6 28.1 %copy-start = (bf16[128,3072]{1,0:T(8,128)(2,1)S(1)}, bf16[128,3072]{1,0:T(8,128)(2,1)}, u32[]{:S(2)}) copy-start(bf16[128,3072]{1,0:T(8,128)(2,1)} %param.8) | copy-start | bytes 2359300
  2.2 41.6 %all-to-all-start = ((bf16[8,24,672]{2,1,0:T(8,128)(2,1)}), bf16[8,24,672]{2,1,0:T(8,128)(2,1)S(1)}, u32[]{:S(2)}, u32[]{:S(2)}) async-start(bf16[8,24,672]{2,1,0:T(8,128)(2,1)} %broadcast_in_dim.59), calls=%async_computation | async-start | bytes 589824 | tf_op jit(solution)/shard_map/all_to_all | solution.py:19
  29.0 39.1 %collective-permute-start.1 = (bf16[48,3200]{1,0:T(8,128)(2,1)S(1)}, bf16[48,3200]{1,0:T(8,128)(2,1)S(1)}, u32[]{:S(2)}, u32[]{:S(2)}) collective-permute-start(bf16[48,3200]{1,0:T(8,128)(2,1)S(1)} %get-tuple-element.31), channel_id=1, source_target_pairs={{0,4},{2,6},{4,0},{6,2},{1,5},{3,7},{5,1},{7,3},{8,12},{10,14},{12... | collective-permute-start | bytes 921608 | tf_op jit(solution)/shard_map/ppermute | solution.py:77
  44.5 22.5 %collective-permute-start = (bf16[4,2,24,384]{3,2,1,0:T(8,128)(2,1)}, bf16[4,2,24,384]{3,2,1,0:T(8,128)(2,1)S(1)}, u32[]{:S(2)}, u32[]{:S(2)}) collective-permute-start(bf16[4,2,24,384]{3,2,1,0:T(8,128)(2,1)} %slice.85), channel_id=1, source_target_pairs={{0,896},{1,129},{64,960},{65,193},{128,0},{129,257},{192,64},{193,... | collective-permute-start | bytes 442376 | tf_op jit(solution)/shard_map/ppermute | solution.py:34
  54.4 19.3 %collective-permute-start.6 = (bf16[4,2,24,384]{3,2,1,0:T(8,128)(2,1)}, bf16[4,2,24,384]{3,2,1,0:T(8,128)(2,1)S(1)}, u32[]{:S(2)}, u32[]{:S(2)}) collective-permute-start(bf16[4,2,24,384]{3,2,1,0:T(8,128)(2,1)} %slice.85), channel_id=1, source_target_pairs={{0,960},{64,0},{128,64},{192,128},{256,192},{320,256},{384,320},{4... | collective-permute-start | bytes 442376 | tf_op jit(solution)/shard_map/ppermute | solution.py:24
  60.1 13.6 %collective-permute-start.7 = (bf16[4,2,24,384]{3,2,1,0:T(8,128)(2,1)}, bf16[4,2,24,384]{3,2,1,0:T(8,128)(2,1)S(1)}, u32[]{:S(2)}, u32[]{:S(2)}) collective-permute-start(bf16[4,2,24,384]{3,2,1,0:T(8,128)(2,1)} %slice.85), channel_id=1, source_target_pairs={{0,64},{64,128},{128,192},{192,256},{256,320},{320,384},{384,448},... | collective-permute-start | bytes 442376 | tf_op jit(solution)/shard_map/ppermute | solution.py:24
  62.9 11.3 %all-to-all-start.1 = ((bf16[4,4,2,24,288]{4,3,2,1,0:T(8,128)(2,1)}), bf16[4,4,2,24,288]{4,3,2,1,0:T(8,128)(2,1)S(1)}, u32[]{:S(2)}, u32[]{:S(2)}) async-start(bf16[4,4,2,24,288]{4,3,2,1,0:T(8,128)(2,1)} %broadcast_in_dim.63), calls=%async_computation.1 | async-start | bytes 1179648 | tf_op jit(solution)/shard_map/all_to_all | solution.py:19
  69.1 23.7 %collective-permute-start.2 = (bf16[2,48,3200]{2,1,0:T(8,128)(2,1)}, bf16[2,48,3200]{2,1,0:T(8,128)(2,1)}, u32[]{:S(2)}, u32[]{:S(2)}) collective-permute-start(bf16[2,48,3200]{2,1,0:T(8,128)(2,1)} %maximum_select_fusion.2), channel_id=1, source_target_pairs={{0,2},{2,0},{4,6},{6,4},{1,3},{3,1},{5,7},{7,5},{8,10},{10,8},{12,... | collective-permute-start | bytes 1843208 | tf_op jit(solution)/shard_map/ppermute | solution.py:84
  74.3 1.8 %copy-start.3 = (bf16[4,4,2,24,288]{4,3,2,1,0:T(8,128)(2,1)}, bf16[4,4,2,24,288]{4,3,2,1,0:T(8,128)(2,1)S(1)}, u32[]{:S(2)}) copy-start(bf16[4,4,2,24,288]{4,3,2,1,0:T(8,128)(2,1)S(1)} %all-to-all-done.1) | copy-start | bytes 1327108
  76.0 30.0 %all-to-all-start.2 = ((bf16[4,4,4,2,24,384]{5,4,3,1,2,0:T(8,128)(2,1)}), bf16[4,4,4,2,24,384]{5,4,3,1,2,0:T(8,128)(2,1)S(1)}, u32[]{:S(2)}, u32[]{:S(2)}) async-start(bf16[4,4,4,2,24,384]{5,4,3,1,2,0:T(8,128)(2,1)} %broadcast_in_dim.67), calls=%async_computation.2 | async-start | bytes 4718592 | tf_op jit(solution)/shard_map/all_to_all | solution.py:19
  80.0 11.9 %copy-start.4 = (bf16[4,4,2,24,288]{4,3,2,1,0:T(8,128)(2,1)S(1)}, bf16[4,4,2,24,288]{4,3,2,1,0:T(8,128)(2,1)}, u32[]{:S(2)}) copy-start(bf16[4,4,2,24,288]{4,3,2,1,0:T(8,128)(2,1)} %copy-done.3) | copy-start | bytes 1327108
  80.0 24.1 %collective-permute-start.4 = (bf16[4,4,2,24,288]{4,3,2,1,0:T(8,128)(2,1)}, bf16[4,4,2,24,288]{4,3,2,1,0:T(8,128)(2,1)S(1)}, u32[]{:S(2)}, u32[]{:S(2)}) collective-permute-start(bf16[4,4,2,24,288]{4,3,2,1,0:T(8,128)(2,1)} %copy-done.3), channel_id=1, source_target_pairs={{0,64},{64,128},{128,192},{192,256},{256,320},{320,384},{384,448},... | collective-permute-start | bytes 1327112 | tf_op jit(solution)/shard_map/ppermute | solution.py:24
  82.1 23.0 %collective-permute-start.5 = (bf16[4,4,2,24,288]{4,3,2,1,0:T(8,128)(2,1)}, bf16[4,4,2,24,288]{4,3,2,1,0:T(8,128)(2,1)S(1)}, u32[]{:S(2)}, u32[]{:S(2)}) collective-permute-start(bf16[4,4,2,24,288]{4,3,2,1,0:T(8,128)(2,1)} %copy-done.3), channel_id=1, source_target_pairs={{0,960},{64,0},{128,64},{192,128},{256,192},{320,256},{384,320},{4... | collective-permute-start | bytes 1327112 | tf_op jit(solution)/shard_map/ppermute | solution.py:24
  87.3 22.4 %collective-permute-start.8 = (bf16[4,4,2,24,288]{4,3,2,1,0:T(8,128)(2,1)}, bf16[4,4,2,24,288]{4,3,2,1,0:T(8,128)(2,1)}, u32[]{:S(2)}, u32[]{:S(2)}) collective-permute-start(bf16[4,4,2,24,288]{4,3,2,1,0:T(8,128)(2,1)} %copy-done.3), channel_id=1, source_target_pairs={{0,896},{1,129},{64,960},{65,193},{128,0},{129,257},{192,64},{193,... | collective-permute-start | bytes 1327112 | tf_op jit(solution)/shard_map/ppermute | solution.py:34
  91.9 2.1 %copy-start.6 = (bf16[1,48,3200]{2,1,0:T(8,128)(2,1)S(1)}, bf16[1,48,3200]{2,1,0:T(8,128)(2,1)}, u32[]{:S(2)}) copy-start(bf16[1,48,3200]{2,1,0:T(8,128)(2,1)} %get-tuple-element.22) | copy-start | bytes 921604
  91.9 2.1 %copy-start.7 = (bf16[1,48,3200]{2,1,0:T(8,128)(2,1)S(1)}, bf16[1,48,3200]{2,1,0:T(8,128)(2,1)}, u32[]{:S(2)}) copy-start(bf16[1,48,3200]{2,1,0:T(8,128)(2,1)} %get-tuple-element.25) | copy-start | bytes 921604
  94.0 8.1 %copy-start.5 = (bf16[1,1,48,3200]{3,2,1,0:T(8,128)(2,1)S(1)}, bf16[1,1,48,3200]{3,2,1,0:T(8,128)(2,1)}, u32[]{:S(2)}) copy-start(bf16[1,1,48,3200]{3,2,1,0:T(8,128)(2,1)} %get-tuple-element.24) | copy-start | bytes 921604
  95.4 16.3 %collective-permute-start.3 = (bf16[4,48,3200]{2,1,0:T(8,128)(2,1)}, bf16[4,48,3200]{2,1,0:T(8,128)(2,1)}, u32[]{:S(2)}, u32[]{:S(2)}) collective-permute-start(bf16[4,48,3200]{2,1,0:T(8,128)(2,1)} %maximum_select_fusion.1), channel_id=1, source_target_pairs={{0,1},{1,0},{2,3},{3,2},{4,5},{5,4},{6,7},{7,6},{8,9},{9,8},{10,11... | collective-permute-start | bytes 3686408 | tf_op jit(solution)/shard_map/ppermute | solution.py:95
  106.0 5.7 %copy-start.1 = (bf16[4,2,48,3200]{3,2,1,0:T(8,128)(2,1)S(1)}, bf16[4,2,48,3200]{3,2,1,0:T(8,128)(2,1)}, u32[]{:S(2)}) copy-start(bf16[4,2,48,3200]{3,2,1,0:T(8,128)(2,1)} %pad_maximum_fusion) | copy-start | bytes 7372804
  111.7 3.2 %copy-start.8 = (bf16[384,672]{0,1:T(8,128)(2,1)S(1)}, bf16[384,672]{0,1:T(8,128)(2,1)}, u32[]{:S(2)}) copy-start(bf16[384,672]{0,1:T(8,128)(2,1)} %param.12) | copy-start | bytes 1548292
  113.2 1.5 copy-start.2
  114.9 6.4 %copy-start.9 = (bf16[384,672]{0,1:T(8,128)(2,1)S(1)}, bf16[384,672]{0,1:T(8,128)(2,1)}, u32[]{:S(2)}) copy-start(bf16[384,672]{0,1:T(8,128)(2,1)} %param.13) | copy-start | bytes 1548292
  127.1 8.4 %collective-permute-start.9 = (bf16[2,2,48,1536]{3,2,0,1:T(8,128)(2,1)}, bf16[2,2,48,1536]{3,2,0,1:T(8,128)(2,1)S(1)}, u32[]{:S(2)}, u32[]{:S(2)}) collective-permute-start(bf16[2,2,48,1536]{3,2,0,1:T(8,128)(2,1)} %bitcast.89), channel_id=1, source_target_pairs={{0,1},{1,0},{2,3},{3,2},{4,5},{5,4},{6,7},{7,6},{8,9},{9,8},{10,11... | collective-permute-start | bytes 1769480 | tf_op jit(solution)/shard_map/ppermute | solution.py:139
  133.6 4.3 %collective-permute-start.12 = (bf16[2,2,48,1536]{3,2,1,0:T(8,128)(2,1)S(1)}, bf16[2,2,48,1536]{3,2,1,0:T(8,128)(2,1)S(1)}, u32[]{:S(2)}, u32[]{:S(2)}) collective-permute-start(bf16[2,2,48,1536]{3,2,1,0:T(8,128)(2,1)S(1)} %dynamic-slice_bitcast_fusion), channel_id=1, source_target_pairs={{0,1},{1,0},{2,3},{3,2},{4,5},{5,4},{6,7},{7,6},{8,9},{9,8},{10,11... | collective-permute-start | bytes 1769480 | tf_op jit(solution)/shard_map/ppermute | solution.py:139
  135.7 10.0 %collective-permute-start.10 = (bf16[2,48,1536]{2,1,0:T(8,128)(2,1)S(1)}, bf16[2,48,1536]{2,1,0:T(8,128)(2,1)S(1)}, u32[]{:S(2)}, u32[]{:S(2)}) collective-permute-start(bf16[2,48,1536]{2,1,0:T(8,128)(2,1)S(1)} %dynamic-slice_bitcast_fusion.2), channel_id=1, source_target_pairs={{0,2},{2,0},{4,6},{6,4},{1,3},{3,1},{5,7},{7,5},{8,10},{10,8},{12,... | collective-permute-start | bytes 884744 | tf_op jit(solution)/shard_map/ppermute | solution.py:141
  138.0 15.4 %collective-permute-start.13 = (bf16[2,48,1536]{2,1,0:T(8,128)(2,1)S(1)}, bf16[2,48,1536]{2,1,0:T(8,128)(2,1)S(1)}, u32[]{:S(2)}, u32[]{:S(2)}) collective-permute-start(bf16[2,48,1536]{2,1,0:T(8,128)(2,1)S(1)} %dynamic-slice_bitcast_fusion.1), channel_id=1, source_target_pairs={{0,2},{2,0},{4,6},{6,4},{1,3},{3,1},{5,7},{7,5},{8,10},{10,8},{12,... | collective-permute-start | bytes 884744 | tf_op jit(solution)/shard_map/ppermute | solution.py:141
  145.8 9.7 %collective-permute-start.11 = (bf16[48,1536]{1,0:T(8,128)(2,1)S(1)}, bf16[48,1536]{1,0:T(8,128)(2,1)S(1)}, u32[]{:S(2)}, u32[]{:S(2)}) collective-permute-start(bf16[48,1536]{1,0:T(8,128)(2,1)S(1)} %dynamic-slice_bitcast_fusion.4), channel_id=1, source_target_pairs={{0,4},{2,6},{4,0},{6,2},{1,5},{3,7},{5,1},{7,3},{8,12},{10,14},{12... | collective-permute-start | bytes 442376 | tf_op jit(solution)/shard_map/ppermute | solution.py:143
  153.6 9.3 %collective-permute-start.14 = (bf16[48,1536]{1,0:T(8,128)(2,1)S(1)}, bf16[48,1536]{1,0:T(8,128)(2,1)S(1)}, u32[]{:S(2)}, u32[]{:S(2)}) collective-permute-start(bf16[48,1536]{1,0:T(8,128)(2,1)S(1)} %dynamic-slice_bitcast_fusion.3), channel_id=1, source_target_pairs={{0,4},{2,6},{4,0},{6,2},{1,5},{3,7},{5,1},{7,3},{8,12},{10,14},{12... | collective-permute-start | bytes 442376 | tf_op jit(solution)/shard_map/ppermute | solution.py:143

commit v8 on v7

--- a/solution.py
+++ b/solution.py
@@ -93,7 +93,8 @@
 
     four_rows = jnp.where(yl % 2 == 0, between(two_rows, beyond), between(beyond, two_rows))
     theirs = lax.ppermute(four_rows, "core", [(0, 1), (1, 0)])
-    got = jnp.stack([four_rows, four_rows], 1)
+    got = jnp.zeros((n_yl, n_core) + four_rows.shape[1:], four_rows.dtype)
+    got = lax.dynamic_update_slice(got, four_rows[:, None], (0, core, 0, 0))
     got = lax.dynamic_update_slice(got, theirs[:, None], (0, 1 - core, 0, 0))
     got = got.reshape(n_yl * n_core * slot_count, model + 128)
     rows = got[:, :model]

time: 166 us -> 163 us (0.982)
  transfers between devices with their start and end apart: 18 -> 18, of which waited for: 6 -> 7; matrix products, arithmetic and copies ran while one was open for 14% -> 14% of each run, Pallas kernels for 0% -> 0%
where the time goes in v8:
time: 163 us; the launch traced here: 162 us
  starting transfers between devices  88.4 us (54%)
  waiting for transfers between devices  32.6 us (20%)
  local copies, waits for them, and re-layouts  21.7 us (13%)
  matrix products  12.8 us (8%)
  other arithmetic  4.6 us (3%)
  between operations  1.91 us (1%)
    all_to_all x3, starting transfers between devices, everyone(): lax.all_to_all(jnp.broadcast_to(part[None], (count,) + part.shape), axes,...  32.5 us
    ppermute x4, starting transfers between devices, along_z(): return lax.ppermute(part, ('za', 'zb'), shifted(za, zb, by))  15 us
    all_to_all x3, waiting for transfers between devices, everyone(): lax.all_to_all(jnp.broadcast_to(part[None], (count,) + part.shape), axes,...  12.9 us
    ppermute x2, starting transfers between devices, two_along_z(): return lax.ppermute(part, ('za', 'zb', 'core'), pairs)  11.6 us
    ppermute x2, waiting for transfers between devices, returned(): near = lax.ppermute(pick(pair, 1, 1 - yl % 2), 'yl', by_one)  9.91 us
    ppermute x2, starting transfers between devices, returned(): swapped = lax.ppermute(pick(part, 2, 1 - core), 'core', [(0, 1), (1, 0)])  8.24 us
    ppermute x2, waiting for transfers between devices, returned(): far = lax.ppermute(pick(four, 0, 1 - yl // 2), 'yl', by_two)  7.28 us
    ppermute x1, starting transfers between devices, body(): theirs = lax.ppermute(four_rows, 'core', [(0, 1), (1, 0)])  6.71 us
  transfers between devices with their start and end apart: 18, of which 7 were waited for; matrix products, arithmetic and copies ran while one was open for 14% of the time, Pallas kernels for 0%

profile of v8, /device:TPU:1, one launch (start us, length us, event | category | flops | bytes accessed | tf_op | source)
XLA Modules:
  0.0 162.0 jit_solution(14526703003367936652)
XLA Ops:
  0.6 1.6 broadcast_in_dim.64
  2.2 24.5 %all-to-all-start = ((bf16[8,24,672]{2,1,0:T(8,128)(2,1)}), bf16[8,24,672]{2,1,0:T(8,128)(2,1)S(1)}, u32[]{:S(2)}, u32[]{:S(2)}) async-start(bf16[8,24,672]{2,1,0:T(8,128)(2,1)} %broadcast_in_dim.64), calls=%async_computation | async-start | bytes 589824 | tf_op jit(solution)/shard_map/all_to_all | solution.py:19
  29.0 2.4 %collective-permute-start.1 = (bf16[48,3200]{1,0:T(8,128)(2,1)S(1)}, bf16[48,3200]{1,0:T(8,128)(2,1)S(1)}, u32[]{:S(2)}, u32[]{:S(2)}) collective-permute-start(bf16[48,3200]{1,0:T(8,128)(2,1)S(1)} %get-tuple-element.31), channel_id=1, source_target_pairs={{0,4},{2,6},{4,0},{6,2},{1,5},{3,7},{5,1},{7,3},{8,12},{10,14},{12... | collective-permute-start | bytes 921608 | tf_op jit(solution)/shard_map/ppermute | solution.py:77
  31.5 12.3 %all-to-all-done = bf16[8,24,672]{2,1,0:T(8,128)(2,1)S(1)} async-done(((bf16[8,24,672]{2,1,0:T(8,128)(2,1)}), bf16[8,24,672]{2,1,0:T(8,128)(2,1)S(1)}, u32[]{:S(2)}, u32[]{:S(2)}) %all-to-all-start) | async-done | bytes 258080 | tf_op jit(solution)/shard_map/all_to_all | solution.py:19
  44.5 9.7 %collective-permute-start = (bf16[4,2,24,384]{3,2,1,0:T(8,128)(2,1)}, bf16[4,2,24,384]{3,2,1,0:T(8,128)(2,1)S(1)}, u32[]{:S(2)}, u32[]{:S(2)}) collective-permute-start(bf16[4,2,24,384]{3,2,1,0:T(8,128)(2,1)} %slice.85), channel_id=1, source_target_pairs={{0,896},{1,129},{64,960},{65,193},{128,0},{129,257},{192,64},{193,... | collective-permute-start | bytes 442376 | tf_op jit(solution)/shard_map/ppermute | solution.py:34
  54.4 5.8 %collective-permute-start.6 = (bf16[4,2,24,384]{3,2,1,0:T(8,128)(2,1)}, bf16[4,2,24,384]{3,2,1,0:T(8,128)(2,1)S(1)}, u32[]{:S(2)}, u32[]{:S(2)}) collective-permute-start(bf16[4,2,24,384]{3,2,1,0:T(8,128)(2,1)} %slice.85), channel_id=1, source_target_pairs={{0,960},{64,0},{128,64},{192,128},{256,192},{320,256},{384,320},{4... | collective-permute-start | bytes 442376 | tf_op jit(solution)/shard_map/ppermute | solution.py:24
  60.1 1.9 %collective-permute-start.7 = (bf16[4,2,24,384]{3,2,1,0:T(8,128)(2,1)}, bf16[4,2,24,384]{3,2,1,0:T(8,128)(2,1)S(1)}, u32[]{:S(2)}, u32[]{:S(2)}) collective-permute-start(bf16[4,2,24,384]{3,2,1,0:T(8,128)(2,1)} %slice.85), channel_id=1, source_target_pairs={{0,64},{64,128},{128,192},{192,256},{256,320},{320,384},{384,448},... | collective-permute-start | bytes 442376 | tf_op jit(solution)/shard_map/ppermute | solution.py:24
  62.9 4.0 %all-to-all-start.1 = ((bf16[4,4,2,24,288]{4,3,2,1,0:T(8,128)(2,1)}), bf16[4,4,2,24,288]{4,3,2,1,0:T(8,128)(2,1)S(1)}, u32[]{:S(2)}, u32[]{:S(2)}) async-start(bf16[4,4,2,24,288]{4,3,2,1,0:T(8,128)(2,1)} %broadcast_in_dim.68), calls=%async_computation.1 | async-start | bytes 1179648 | tf_op jit(solution)/shard_map/all_to_all | solution.py:19
  69.1 2.5 %collective-permute-start.2 = (bf16[2,48,3200]{2,1,0:T(8,128)(2,1)}, bf16[2,48,3200]{2,1,0:T(8,128)(2,1)}, u32[]{:S(2)}, u32[]{:S(2)}) collective-permute-start(bf16[2,48,3200]{2,1,0:T(8,128)(2,1)} %maximum_select_fusion.2), channel_id=1, source_target_pairs={{0,2},{2,0},{4,6},{6,4},{1,3},{3,1},{5,7},{7,5},{8,10},{10,8},{12,... | collective-permute-start | bytes 1843208 | tf_op jit(solution)/shard_map/ppermute | solution.py:84
  71.7 2.0 %fusion.41 = (bf16[1,48,3200]{2,1,0:T(8,128)(2,1)}, bf16[1,1,48,3200]{3,2,1,0:T(8,128)(2,1)S(1)}, bf16[1,1,48,3200]{3,2,1,0:T(8,128)(2,1)}, bf16[1,48,3200]{2,1,0:T(8,128)(2,1)}) fusion(bf16[2,48,3200]{2,1,0:T(8,128)(2,1)} %maximum_select_fusion.2), kind=kLoop, calls=%fused_computation.82 | loop fusion | bytes 1843200 | tf_op jit(solution)/shard_map/slice | solution.py:92
  74.3 1.8 %broadcast_in_dim.72 = bf16[4,4,4,2,24,384]{5,4,3,1,2,0:T(8,128)(2,1)} broadcast(bf16[4,4,2,24,384]{4,3,2,0,1:T(8,128)(2,1)S(1)} %copy.32), dimensions={1,2,3,4,5} | broadcast | bytes 2949120 | tf_op jit(solution)/shard_map/broadcast_in_dim | solution.py:19
  76.0 4.0 %all-to-all-start.2 = ((bf16[4,4,4,2,24,384]{5,4,3,1,2,0:T(8,128)(2,1)}), bf16[4,4,4,2,24,384]{5,4,3,1,2,0:T(8,128)(2,1)S(1)}, u32[]{:S(2)}, u32[]{:S(2)}) async-start(bf16[4,4,4,2,24,384]{5,4,3,1,2,0:T(8,128)(2,1)} %broadcast_in_dim.72), calls=%async_computation.2 | async-start | bytes 4718592 | tf_op jit(solution)/shard_map/all_to_all | solution.py:19
  80.0 2.0 %collective-permute-start.4 = (bf16[4,4,2,24,288]{4,3,2,1,0:T(8,128)(2,1)}, bf16[4,4,2,24,288]{4,3,2,1,0:T(8,128)(2,1)S(1)}, u32[]{:S(2)}, u32[]{:S(2)}) collective-permute-start(bf16[4,4,2,24,288]{4,3,2,1,0:T(8,128)(2,1)} %copy-done.3), channel_id=1, source_target_pairs={{0,64},{64,128},{128,192},{192,256},{256,320},{320,384},{384,448},... | collective-permute-start | bytes 1327112 | tf_op jit(solution)/shard_map/ppermute | solution.py:24
  82.1 5.2 %collective-permute-start.5 = (bf16[4,4,2,24,288]{4,3,2,1,0:T(8,128)(2,1)}, bf16[4,4,2,24,288]{4,3,2,1,0:T(8,128)(2,1)S(1)}, u32[]{:S(2)}, u32[]{:S(2)}) collective-permute-start(bf16[4,4,2,24,288]{4,3,2,1,0:T(8,128)(2,1)} %copy-done.3), channel_id=1, source_target_pairs={{0,960},{64,0},{128,64},{192,128},{256,192},{320,256},{384,320},{4... | collective-permute-start | bytes 1327112 | tf_op jit(solution)/shard_map/ppermute | solution.py:24
  87.3 1.9 %collective-permute-start.8 = (bf16[4,4,2,24,288]{4,3,2,1,0:T(8,128)(2,1)}, bf16[4,4,2,24,288]{4,3,2,1,0:T(8,128)(2,1)}, u32[]{:S(2)}, u32[]{:S(2)}) collective-permute-start(bf16[4,4,2,24,288]{4,3,2,1,0:T(8,128)(2,1)} %copy-done.3), channel_id=1, source_target_pairs={{0,896},{1,129},{64,960},{65,193},{128,0},{129,257},{192,64},{193,... | collective-permute-start | bytes 1327112 | tf_op jit(solution)/shard_map/ppermute | solution.py:34
  89.3 2.7 %broadcast_in_dim.67 = bf16[4,4,2,4,24,672]{5,4,3,2,1,0:T(8,128)(2,1)} broadcast(bf16[]{:T(256)} %constant.167.clone.1), dimensions={} | broadcast | bytes 4128770 | tf_op jit(solution)/shard_map/broadcast_in_dim | solution.py:103
  95.4 6.7 %collective-permute-start.3 = (bf16[4,48,3200]{2,1,0:T(8,128)(2,1)}, bf16[4,48,3200]{2,1,0:T(8,128)(2,1)}, u32[]{:S(2)}, u32[]{:S(2)}) collective-permute-start(bf16[4,48,3200]{2,1,0:T(8,128)(2,1)} %maximum_select_fusion.1), channel_id=1, source_target_pairs={{0,1},{1,0},{2,3},{3,2},{4,5},{5,4},{6,7},{7,6},{8,9},{9,8},{10,11... | collective-permute-start | bytes 3686408 | tf_op jit(solution)/shard_map/ppermute | solution.py:95
  105.5 1.8 %copy_dynamic-update-slice_fusion = bf16[4,4,2,4,24,672]{5,4,3,2,1,0:T(8,128)(2,1)} fusion(bf16[4,4,2,4,24,672]{5,4,3,2,1,0:T(8,128)(2,1)} %copy_dynamic-update-slice_fusion.2, bf16[4,4,4,2,24,384]{5,4,3,1,2,0:T(8,128)(2,1)S(1)} %all-to-all-done.2), kind=kLoop, calls=%fused_computation.5 | loop fusion | bytes 4718592 | tf_op jit(solution)/shard_map/scatter | solution.py:114
  107.3 2.5 %collective-permute-done.8 = bf16[4,4,2,24,288]{4,3,2,1,0:T(8,128)(2,1)} collective-permute-done((bf16[4,4,2,24,288]{4,3,2,1,0:T(8,128)(2,1)}, bf16[4,4,2,24,288]{4,3,2,1,0:T(8,128)(2,1)}, u32[]{:S(2)}, u32[]{:S(2)}) %collective-permute-start.8) | collective-permute-done | bytes 442400 | tf_op jit(solution)/shard_map/ppermute | solution.py:34
  109.7 2.0 %copy_dynamic-update-slice_fusion.1 = bf16[4,4,2,4,24,672]{5,4,3,2,1,0:T(8,128)(2,1)} fusion(bf16[4,4,2,4,24,672]{5,4,3,2,1,0:T(8,128)(2,1)} %copy_dynamic-update-slice_fusion, s32[]{:T(128)S(6)} %select_n.248, bf16[4,4,2,24,288]{4,3,2,1,0:T(8,128)(2,1)} %collective-permute-done.8), kind=kLoop, calls=%fused_computation.32 | loop fusion | bytes 1179652 | tf_op jit(solution)/shard_map/dynamic_update_slice | solution.py:109
  111.7 1.4 bitcast_dynamic-update-slice_fusion
  113.4 5.7 %fusion.8 = (bf16[384,672]{0,1:T(8,128)(2,1)}, f32[384,672]{0,1:T(8,128)S(1)}) fusion(bf16[384,672]{0,1:T(8,128)(2,1)S(1)} %copy-done.8, f32[384]{0:T(512)S(1)} %convert_reduce_fusion, bf16[3072,672]{1,0:T(8,128)(2,1)} %bitcast.25, bf16[384,3200]{1,0:T(8,128)(2,1)S(1)} %bitcast.92), kind=kOutput, calls=%fused_computation.18 | convolution fusion | flops 1587511296 | bytes 8554496 | tf_op jit(solution)/shard_map/dot_general | solution.py:118
  119.2 4.7 %convolution_convert_fusion = bf16[384,3072]{1,0:T(8,128)(2,1)S(1)} fusion(bf16[3072,672]{1,0:T(8,128)(2,1)} %bitcast.25, bf16[384,672]{0,1:T(8,128)(2,1)S(1)} %copy-done.8, f32[384,672]{0,1:T(8,128)S(1)} %get-tuple-element.33, bf16[384,672]{0,1:T(8,128)(2,1)S(1)} %copy-done.9, pred[384]{0:T(512)(128)(4,1)S(1)} %fusion.24), kind=kOutput, calls=%fused_computation | convolution fusion | flops 1589981184 | bytes 8552832 | tf_op jit(solution)/shard_map/dot_general | solution.py:136
  125.0 6.3 %collective-permute-start.9 = (bf16[2,2,48,1536]{3,2,0,1:T(8,128)(2,1)}, bf16[2,2,48,1536]{3,2,0,1:T(8,128)(2,1)S(1)}, u32[]{:S(2)}, u32[]{:S(2)}) collective-permute-start(bf16[2,2,48,1536]{3,2,0,1:T(8,128)(2,1)} %bitcast.89), channel_id=1, source_target_pairs={{0,1},{1,0},{2,3},{3,2},{4,5},{5,4},{6,7},{7,6},{8,9},{9,8},{10,11... | collective-permute-start | bytes 1769480 | tf_op jit(solution)/shard_map/ppermute | solution.py:140
  131.4 1.9 %collective-permute-start.12 = (bf16[2,2,48,1536]{3,2,1,0:T(8,128)(2,1)S(1)}, bf16[2,2,48,1536]{3,2,1,0:T(8,128)(2,1)S(1)}, u32[]{:S(2)}, u32[]{:S(2)}) collective-permute-start(bf16[2,2,48,1536]{3,2,1,0:T(8,128)(2,1)S(1)} %dynamic-slice_bitcast_fusion), channel_id=1, source_target_pairs={{0,1},{1,0},{2,3},{3,2},{4,5},{5,4},{6,7},{7,6},{8,9},{9,8},{10,11... | collective-permute-start | bytes 1769480 | tf_op jit(solution)/shard_map/ppermute | solution.py:140
  133.6 2.2 %collective-permute-start.10 = (bf16[2,48,1536]{2,1,0:T(8,128)(2,1)S(1)}, bf16[2,48,1536]{2,1,0:T(8,128)(2,1)S(1)}, u32[]{:S(2)}, u32[]{:S(2)}) collective-permute-start(bf16[2,48,1536]{2,1,0:T(8,128)(2,1)S(1)} %dynamic-slice_bitcast_fusion.2), channel_id=1, source_target_pairs={{0,2},{2,0},{4,6},{6,4},{1,3},{3,1},{5,7},{7,5},{8,10},{10,8},{12,... | collective-permute-start | bytes 884744 | tf_op jit(solution)/shard_map/ppermute | solution.py:142
  136.0 3.1 %collective-permute-start.13 = (bf16[2,48,1536]{2,1,0:T(8,128)(2,1)S(1)}, bf16[2,48,1536]{2,1,0:T(8,128)(2,1)S(1)}, u32[]{:S(2)}, u32[]{:S(2)}) collective-permute-start(bf16[2,48,1536]{2,1,0:T(8,128)(2,1)S(1)} %dynamic-slice_bitcast_fusion.1), channel_id=1, source_target_pairs={{0,2},{2,0},{4,6},{6,4},{1,3},{3,1},{5,7},{7,5},{8,10},{10,8},{12,... | collective-permute-start | bytes 884744 | tf_op jit(solution)/shard_map/ppermute | solution.py:142
  139.1 4.5 %collective-permute-done.10 = bf16[2,48,1536]{2,1,0:T(8,128)(2,1)S(1)} collective-permute-done((bf16[2,48,1536]{2,1,0:T(8,128)(2,1)S(1)}, bf16[2,48,1536]{2,1,0:T(8,128)(2,1)S(1)}, u32[]{:S(2)}, u32[]{:S(2)}) %collective-permute-start.10) | collective-permute-done | bytes 294944 | tf_op jit(solution)/shard_map/ppermute | solution.py:142
  143.6 2.2 %collective-permute-start.11 = (bf16[48,1536]{1,0:T(8,128)(2,1)S(1)}, bf16[48,1536]{1,0:T(8,128)(2,1)S(1)}, u32[]{:S(2)}, u32[]{:S(2)}) collective-permute-start(bf16[48,1536]{1,0:T(8,128)(2,1)S(1)} %dynamic-slice_bitcast_fusion.4), channel_id=1, source_target_pairs={{0,4},{2,6},{4,0},{6,2},{1,5},{3,7},{5,1},{7,3},{8,12},{10,14},{12... | collective-permute-start | bytes 442376 | tf_op jit(solution)/shard_map/ppermute | solution.py:144
  145.9 5.4 %collective-permute-done.13 = bf16[2,48,1536]{2,1,0:T(8,128)(2,1)S(1)} collective-permute-done((bf16[2,48,1536]{2,1,0:T(8,128)(2,1)S(1)}, bf16[2,48,1536]{2,1,0:T(8,128)(2,1)S(1)}, u32[]{:S(2)}, u32[]{:S(2)}) %collective-permute-start.13) | collective-permute-done | bytes 294944 | tf_op jit(solution)/shard_map/ppermute | solution.py:142
  151.4 1.9 %collective-permute-start.14 = (bf16[48,1536]{1,0:T(8,128)(2,1)S(1)}, bf16[48,1536]{1,0:T(8,128)(2,1)S(1)}, u32[]{:S(2)}, u32[]{:S(2)}) collective-permute-start(bf16[48,1536]{1,0:T(8,128)(2,1)S(1)} %dynamic-slice_bitcast_fusion.3), channel_id=1, source_target_pairs={{0,4},{2,6},{4,0},{6,2},{1,5},{3,7},{5,1},{7,3},{8,12},{10,14},{12... | collective-permute-start | bytes 442376 | tf_op jit(solution)/shard_map/ppermute | solution.py:144
  153.4 7.3 %collective-permute-done.14 = bf16[48,1536]{1,0:T(8,128)(2,1)S(1)} collective-permute-done((bf16[48,1536]{1,0:T(8,128)(2,1)S(1)}, bf16[48,1536]{1,0:T(8,128)(2,1)S(1)}, u32[]{:S(2)}, u32[]{:S(2)}) %collective-permute-start.14) | collective-permute-done | bytes 147488 | tf_op jit(solution)/shard_map/ppermute | solution.py:144
  (73 shorter events, 16.0 us)
Async XLA Ops:
  0.6 28.1 %copy-start = (bf16[128,3072]{1,0:T(8,128)(2,1)S(1)}, bf16[128,3072]{1,0:T(8,128)(2,1)}, u32[]{:S(2)}) copy-start(bf16[128,3072]{1,0:T(8,128)(2,1)} %param.8) | copy-start | bytes 2359300
  2.2 41.6 %all-to-all-start = ((bf16[8,24,672]{2,1,0:T(8,128)(2,1)}), bf16[8,24,672]{2,1,0:T(8,128)(2,1)S(1)}, u32[]{:S(2)}, u32[]{:S(2)}) async-start(bf16[8,24,672]{2,1,0:T(8,128)(2,1)} %broadcast_in_dim.64), calls=%async_computation | async-start | bytes 589824 | tf_op jit(solution)/shard_map/all_to_all | solution.py:19
  29.0 39.1 %collective-permute-start.1 = (bf16[48,3200]{1,0:T(8,128)(2,1)S(1)}, bf16[48,3200]{1,0:T(8,128)(2,1)S(1)}, u32[]{:S(2)}, u32[]{:S(2)}) collective-permute-start(bf16[48,3200]{1,0:T(8,128)(2,1)S(1)} %get-tuple-element.31), channel_id=1, source_target_pairs={{0,4},{2,6},{4,0},{6,2},{1,5},{3,7},{5,1},{7,3},{8,12},{10,14},{12... | collective-permute-start | bytes 921608 | tf_op jit(solution)/shard_map/ppermute | solution.py:77
  44.5 22.5 %collective-permute-start = (bf16[4,2,24,384]{3,2,1,0:T(8,128)(2,1)}, bf16[4,2,24,384]{3,2,1,0:T(8,128)(2,1)S(1)}, u32[]{:S(2)}, u32[]{:S(2)}) collective-permute-start(bf16[4,2,24,384]{3,2,1,0:T(8,128)(2,1)} %slice.85), channel_id=1, source_target_pairs={{0,896},{1,129},{64,960},{65,193},{128,0},{129,257},{192,64},{193,... | collective-permute-start | bytes 442376 | tf_op jit(solution)/shard_map/ppermute | solution.py:34
  54.4 19.3 %collective-permute-start.6 = (bf16[4,2,24,384]{3,2,1,0:T(8,128)(2,1)}, bf16[4,2,24,384]{3,2,1,0:T(8,128)(2,1)S(1)}, u32[]{:S(2)}, u32[]{:S(2)}) collective-permute-start(bf16[4,2,24,384]{3,2,1,0:T(8,128)(2,1)} %slice.85), channel_id=1, source_target_pairs={{0,960},{64,0},{128,64},{192,128},{256,192},{320,256},{384,320},{4... | collective-permute-start | bytes 442376 | tf_op jit(solution)/shard_map/ppermute | solution.py:24
  60.1 13.6 %collective-permute-start.7 = (bf16[4,2,24,384]{3,2,1,0:T(8,128)(2,1)}, bf16[4,2,24,384]{3,2,1,0:T(8,128)(2,1)S(1)}, u32[]{:S(2)}, u32[]{:S(2)}) collective-permute-start(bf16[4,2,24,384]{3,2,1,0:T(8,128)(2,1)} %slice.85), channel_id=1, source_target_pairs={{0,64},{64,128},{128,192},{192,256},{256,320},{320,384},{384,448},... | collective-permute-start | bytes 442376 | tf_op jit(solution)/shard_map/ppermute | solution.py:24
  62.9 11.3 %all-to-all-start.1 = ((bf16[4,4,2,24,288]{4,3,2,1,0:T(8,128)(2,1)}), bf16[4,4,2,24,288]{4,3,2,1,0:T(8,128)(2,1)S(1)}, u32[]{:S(2)}, u32[]{:S(2)}) async-start(bf16[4,4,2,24,288]{4,3,2,1,0:T(8,128)(2,1)} %broadcast_in_dim.68), calls=%async_computation.1 | async-start | bytes 1179648 | tf_op jit(solution)/shard_map/all_to_all | solution.py:19
  69.1 23.7 %collective-permute-start.2 = (bf16[2,48,3200]{2,1,0:T(8,128)(2,1)}, bf16[2,48,3200]{2,1,0:T(8,128)(2,1)}, u32[]{:S(2)}, u32[]{:S(2)}) collective-permute-start(bf16[2,48,3200]{2,1,0:T(8,128)(2,1)} %maximum_select_fusion.2), channel_id=1, source_target_pairs={{0,2},{2,0},{4,6},{6,4},{1,3},{3,1},{5,7},{7,5},{8,10},{10,8},{12,... | collective-permute-start | bytes 1843208 | tf_op jit(solution)/shard_map/ppermute | solution.py:84
  74.3 1.8 %copy-start.3 = (bf16[4,4,2,24,288]{4,3,2,1,0:T(8,128)(2,1)}, bf16[4,4,2,24,288]{4,3,2,1,0:T(8,128)(2,1)S(1)}, u32[]{:S(2)}) copy-start(bf16[4,4,2,24,288]{4,3,2,1,0:T(8,128)(2,1)S(1)} %all-to-all-done.1) | copy-start | bytes 1327108
  76.0 29.4 %all-to-all-start.2 = ((bf16[4,4,4,2,24,384]{5,4,3,1,2,0:T(8,128)(2,1)}), bf16[4,4,4,2,24,384]{5,4,3,1,2,0:T(8,128)(2,1)S(1)}, u32[]{:S(2)}, u32[]{:S(2)}) async-start(bf16[4,4,4,2,24,384]{5,4,3,1,2,0:T(8,128)(2,1)} %broadcast_in_dim.72), calls=%async_computation.2 | async-start | bytes 4718592 | tf_op jit(solution)/shard_map/all_to_all | solution.py:19
  80.0 11.9 %copy-start.4 = (bf16[4,4,2,24,288]{4,3,2,1,0:T(8,128)(2,1)S(1)}, bf16[4,4,2,24,288]{4,3,2,1,0:T(8,128)(2,1)}, u32[]{:S(2)}) copy-start(bf16[4,4,2,24,288]{4,3,2,1,0:T(8,128)(2,1)} %copy-done.3) | copy-start | bytes 1327108
  80.0 22.6 %collective-permute-start.4 = (bf16[4,4,2,24,288]{4,3,2,1,0:T(8,128)(2,1)}, bf16[4,4,2,24,288]{4,3,2,1,0:T(8,128)(2,1)S(1)}, u32[]{:S(2)}, u32[]{:S(2)}) collective-permute-start(bf16[4,4,2,24,288]{4,3,2,1,0:T(8,128)(2,1)} %copy-done.3), channel_id=1, source_target_pairs={{0,64},{64,128},{128,192},{192,256},{256,320},{320,384},{384,448},... | collective-permute-start | bytes 1327112 | tf_op jit(solution)/shard_map/ppermute | solution.py:24
  82.1 21.6 %collective-permute-start.5 = (bf16[4,4,2,24,288]{4,3,2,1,0:T(8,128)(2,1)}, bf16[4,4,2,24,288]{4,3,2,1,0:T(8,128)(2,1)S(1)}, u32[]{:S(2)}, u32[]{:S(2)}) collective-permute-start(bf16[4,4,2,24,288]{4,3,2,1,0:T(8,128)(2,1)} %copy-done.3), channel_id=1, source_target_pairs={{0,960},{64,0},{128,64},{192,128},{256,192},{320,256},{384,320},{4... | collective-permute-start | bytes 1327112 | tf_op jit(solution)/shard_map/ppermute | solution.py:24
  87.3 22.4 %collective-permute-start.8 = (bf16[4,4,2,24,288]{4,3,2,1,0:T(8,128)(2,1)}, bf16[4,4,2,24,288]{4,3,2,1,0:T(8,128)(2,1)}, u32[]{:S(2)}, u32[]{:S(2)}) collective-permute-start(bf16[4,4,2,24,288]{4,3,2,1,0:T(8,128)(2,1)} %copy-done.3), channel_id=1, source_target_pairs={{0,896},{1,129},{64,960},{65,193},{128,0},{129,257},{192,64},{193,... | collective-permute-start | bytes 1327112 | tf_op jit(solution)/shard_map/ppermute | solution.py:34
  91.9 2.1 %copy-start.6 = (bf16[1,48,3200]{2,1,0:T(8,128)(2,1)S(1)}, bf16[1,48,3200]{2,1,0:T(8,128)(2,1)}, u32[]{:S(2)}) copy-start(bf16[1,48,3200]{2,1,0:T(8,128)(2,1)} %get-tuple-element.22) | copy-start | bytes 921604
  91.9 2.1 %copy-start.7 = (bf16[1,48,3200]{2,1,0:T(8,128)(2,1)S(1)}, bf16[1,48,3200]{2,1,0:T(8,128)(2,1)}, u32[]{:S(2)}) copy-start(bf16[1,48,3200]{2,1,0:T(8,128)(2,1)} %get-tuple-element.25) | copy-start | bytes 921604
  94.0 8.3 %copy-start.5 = (bf16[1,1,48,3200]{3,2,1,0:T(8,128)(2,1)S(1)}, bf16[1,1,48,3200]{3,2,1,0:T(8,128)(2,1)}, u32[]{:S(2)}) copy-start(bf16[1,1,48,3200]{3,2,1,0:T(8,128)(2,1)} %get-tuple-element.24) | copy-start | bytes 921604
  95.4 16.3 %collective-permute-start.3 = (bf16[4,48,3200]{2,1,0:T(8,128)(2,1)}, bf16[4,48,3200]{2,1,0:T(8,128)(2,1)}, u32[]{:S(2)}, u32[]{:S(2)}) collective-permute-start(bf16[4,48,3200]{2,1,0:T(8,128)(2,1)} %maximum_select_fusion.1), channel_id=1, source_target_pairs={{0,1},{1,0},{2,3},{3,2},{4,5},{5,4},{6,7},{7,6},{8,9},{9,8},{10,11... | collective-permute-start | bytes 3686408 | tf_op jit(solution)/shard_map/ppermute | solution.py:95
  102.6 1.6 %copy-start.1 = (bf16[4,2,48,3200]{3,2,1,0:T(8,128)(2,1)}, bf16[4,2,48,3200]{3,2,1,0:T(8,128)(2,1)S(1)}, u32[]{:S(2)}) copy-start(bf16[4,2,48,3200]{3,2,1,0:T(8,128)(2,1)S(1)} %fusion.5) | copy-start | bytes 7372804
  105.5 6.2 %copy-start.2 = (bf16[4,2,48,3200]{3,2,1,0:T(8,128)(2,1)S(1)}, bf16[4,2,48,3200]{3,2,1,0:T(8,128)(2,1)}, u32[]{:S(2)}) copy-start(bf16[4,2,48,3200]{3,2,1,0:T(8,128)(2,1)} %copy-done.1) | copy-start | bytes 7372804
  107.3 6.1 %copy-start.8 = (bf16[384,672]{0,1:T(8,128)(2,1)S(1)}, bf16[384,672]{0,1:T(8,128)(2,1)}, u32[]{:S(2)}) copy-start(bf16[384,672]{0,1:T(8,128)(2,1)} %param.12) | copy-start | bytes 1548292
  113.4 5.7 %copy-start.9 = (bf16[384,672]{0,1:T(8,128)(2,1)S(1)}, bf16[384,672]{0,1:T(8,128)(2,1)}, u32[]{:S(2)}) copy-start(bf16[384,672]{0,1:T(8,128)(2,1)} %param.13) | copy-start | bytes 1548292
  125.0 8.3 %collective-permute-start.9 = (bf16[2,2,48,1536]{3,2,0,1:T(8,128)(2,1)}, bf16[2,2,48,1536]{3,2,0,1:T(8,128)(2,1)S(1)}, u32[]{:S(2)}, u32[]{:S(2)}) collective-permute-start(bf16[2,2,48,1536]{3,2,0,1:T(8,128)(2,1)} %bitcast.89), channel_id=1, source_target_pairs={{0,1},{1,0},{2,3},{3,2},{4,5},{5,4},{6,7},{7,6},{8,9},{9,8},{10,11... | collective-permute-start | bytes 1769480 | tf_op jit(solution)/shard_map/ppermute | solution.py:140
  131.4 4.3 %collective-permute-start.12 = (bf16[2,2,48,1536]{3,2,1,0:T(8,128)(2,1)S(1)}, bf16[2,2,48,1536]{3,2,1,0:T(8,128)(2,1)S(1)}, u32[]{:S(2)}, u32[]{:S(2)}) collective-permute-start(bf16[2,2,48,1536]{3,2,1,0:T(8,128)(2,1)S(1)} %dynamic-slice_bitcast_fusion), channel_id=1, source_target_pairs={{0,1},{1,0},{2,3},{3,2},{4,5},{5,4},{6,7},{7,6},{8,9},{9,8},{10,11... | collective-permute-start | bytes 1769480 | tf_op jit(solution)/shard_map/ppermute | solution.py:140
  133.6 10.0 %collective-permute-start.10 = (bf16[2,48,1536]{2,1,0:T(8,128)(2,1)S(1)}, bf16[2,48,1536]{2,1,0:T(8,128)(2,1)S(1)}, u32[]{:S(2)}, u32[]{:S(2)}) collective-permute-start(bf16[2,48,1536]{2,1,0:T(8,128)(2,1)S(1)} %dynamic-slice_bitcast_fusion.2), channel_id=1, source_target_pairs={{0,2},{2,0},{4,6},{6,4},{1,3},{3,1},{5,7},{7,5},{8,10},{10,8},{12,... | collective-permute-start | bytes 884744 | tf_op jit(solution)/shard_map/ppermute | solution.py:142
  136.0 15.4 %collective-permute-start.13 = (bf16[2,48,1536]{2,1,0:T(8,128)(2,1)S(1)}, bf16[2,48,1536]{2,1,0:T(8,128)(2,1)S(1)}, u32[]{:S(2)}, u32[]{:S(2)}) collective-permute-start(bf16[2,48,1536]{2,1,0:T(8,128)(2,1)S(1)} %dynamic-slice_bitcast_fusion.1), channel_id=1, source_target_pairs={{0,2},{2,0},{4,6},{6,4},{1,3},{3,1},{5,7},{7,5},{8,10},{10,8},{12,... | collective-permute-start | bytes 884744 | tf_op jit(solution)/shard_map/ppermute | solution.py:142
  143.6 9.7 %collective-permute-start.11 = (bf16[48,1536]{1,0:T(8,128)(2,1)S(1)}, bf16[48,1536]{1,0:T(8,128)(2,1)S(1)}, u32[]{:S(2)}, u32[]{:S(2)}) collective-permute-start(bf16[48,1536]{1,0:T(8,128)(2,1)S(1)} %dynamic-slice_bitcast_fusion.4), channel_id=1, source_target_pairs={{0,4},{2,6},{4,0},{6,2},{1,5},{3,7},{5,1},{7,3},{8,12},{10,14},{12... | collective-permute-start | bytes 442376 | tf_op jit(solution)/shard_map/ppermute | solution.py:144
  151.4 9.3 %collective-permute-start.14 = (bf16[48,1536]{1,0:T(8,128)(2,1)S(1)}, bf16[48,1536]{1,0:T(8,128)(2,1)S(1)}, u32[]{:S(2)}, u32[]{:S(2)}) collective-permute-start(bf16[48,1536]{1,0:T(8,128)(2,1)S(1)} %dynamic-slice_bitcast_fusion.3), channel_id=1, source_target_pairs={{0,4},{2,6},{4,0},{6,2},{1,5},{3,7},{5,1},{7,3},{8,12},{10,14},{12... | collective-permute-start | bytes 442376 | tf_op jit(solution)/shard_map/ppermute | solution.py:144
